TPU v7x, 1024 devices: a whole 8x8x8 slice. The times are simulated.
1024 devices in a mesh: dom: 128 (over z, y, core), rep: 8 (over x).
Axes of the slice: x: 8, y: 8, z: 8, core: 2. Of those that a mesh axis runs over, the one named last changes fastest.
Arguments:
- features: bfloat16 [262144, 256], P(('dom', 'rep')), may hold values from -6 to 6
- weight: bfloat16 [256, 172], replicated, may hold values from -0.375 to 0.375
- tiles: bfloat16 [65536, 128, 128], P(('dom', 'rep')), may hold values from -0.09375 to 0.09375
- tile_rows: int32 [65536], P(('dom', 'rep')), may hold values from 0 to 1
- tile_cols: int32 [65536], P(('dom', 'rep')), may hold values from 0 to 23
- send_lists: int32 [2048, 64], P(('dom', 'rep')), may hold values from 0 to 255
- counts: int32 [2048], P(('dom', 'rep')), may hold values from 1 to 64, as said below
- labels: int32 [262144], P(('dom', 'rep')), may hold values from 0 to 171
Outputs:
- grad_features: bfloat16 [262144, 256], P(('dom', 'rep'))
- grad_weight: float32 [256, 172], replicated
- loss: float32 [], replicated
Inputs may be any that keep to these rules, and one draw needn't show every extreme that they name: `counts`: at most 64, and a list of 64 live slots occurs in every draw.
All inputs are finite; a program needn't handle non-finite values.
Results may differ from a plain program's by a relative error of at most 0.0055.
Values may be sent and summed in bfloat16 or wider, within the bound.
No kernel may reach another device: no remote copies, remote signals or barrier semaphores. Data moves between devices by JAX's collectives and lax.ppermute only.
A program may use at most 32 MiB of HBM per device.

v0:
```python
import jax
import jax.numpy as jnp
from jax import lax
from jax.sharding import PartitionSpec as P


def extended_2(block, sides, width):
    for axis, dim in sides:
        count = lax.axis_size(axis)
        forward = [(i, i + 1) for i in range(count - 1)]
        backward = [(target, source) for source, target in forward]
        low = lax.ppermute(
            lax.slice_in_dim(block, block.shape[dim] - width, None, axis=dim), axis, forward
        )
        high = lax.ppermute(lax.slice_in_dim(block, 0, width, axis=dim), axis, backward)
        block = jnp.concatenate([low, block, high], axis=dim)
    return block


def per_device(features, weight, tiles, tile_rows, tile_cols, send_lists, counts, labels):
    rows_here = features.shape[0]
    send = send_lists.shape[1]
    width = weight.shape[1]
    tile = tiles.shape[1]
    reps = lax.axis_size("rep")
    block = rows_here + 2 * send
    projected = jnp.dot(features, weight, preferred_element_type=jnp.float32).astype(jnp.bfloat16)
    live = jnp.arange(send, dtype=jnp.int32)[None, :] < counts[:, None]
    picks = (
        jnp.arange(rows_here, dtype=jnp.int32)[None, None, :] == send_lists[:, :, None]
    ) & live[:, :, None]
    picked = jnp.einsum(
        "ksn,nc->ksc", picks.astype(jnp.bfloat16), projected, preferred_element_type=jnp.float32
    )
    outgoing = picked.astype(jnp.bfloat16).reshape(2 * send, width)
    gathered_rows, gathered_sends = (
        lax.all_gather(projected, "rep", axis=0, tiled=True),
        lax.all_gather(outgoing, "rep", axis=0, tiled=True),
    )
    ordered = (
        gathered_sends.reshape(reps, 2, send, width)
        .transpose(1, 0, 2, 3)
        .reshape(2 * reps * send, width)
    )
    padded = extended_2(ordered, (("dom", 0),), reps * send)
    from_left = padded[: reps * send].reshape(reps, send, width)
    from_right = padded[-reps * send :].reshape(reps, send, width)
    extended = jnp.concatenate(
        [gathered_rows.reshape(reps, rows_here, width), from_left, from_right], axis=1
    )
    extended = extended.reshape(reps * block, width)
    col_count = reps * block // tile
    row_count = rows_here // tile
    chosen = extended.reshape(col_count, tile, width)[tile_cols]
    products = jnp.einsum("tij,tjc->tic", tiles, chosen, preferred_element_type=jnp.float32)
    logits = (
        jnp.zeros((row_count, tile, width), jnp.float32)
        .at[tile_rows]
        .add(products)
        .reshape(rows_here, width)
    )
    peak = jnp.max(logits, axis=1, keepdims=True)
    shifted = logits - peak
    logp = shifted - jnp.log(jnp.sum(jnp.exp(shifted), axis=1, keepdims=True))
    onehot = labels[:, None] == jnp.arange(width, dtype=jnp.int32)[None, :]
    total = -jnp.sum(jnp.where(onehot, logp, jnp.float32(0.0)))
    grad_logits = (jnp.exp(logp) - onehot.astype(jnp.float32)).astype(jnp.bfloat16)
    grad_tiles = grad_logits.reshape(row_count, tile, width)[tile_rows]
    parts = jnp.einsum("tji,tjc->tic", tiles, grad_tiles, preferred_element_type=jnp.float32)
    count = reps * block
    span = count // tile
    local = tile_cols - 0 // tile
    target = jnp.where((local >= 0) & (local < span), local, span)
    columns = (
        jnp.zeros((span, tile, width), jnp.float32)
        .at[target]
        .add(parts, mode="drop")
        .reshape(count, width)
    )
    summed = lax.psum_scatter(columns, "rep", scatter_dimension=0, tiled=True)
    returned = extended_2(summed[rows_here:], (("dom", 0),), send)
    own_rows = summed[:rows_here]
    back_first = returned[:send]
    back_second = returned[-send:]
    returned_rows = jnp.stack([back_first, back_second], axis=0)
    grad_sum = own_rows + jnp.einsum(
        "ksn,ksc->nc", picks.astype(jnp.float32), returned_rows, precision=lax.Precision.HIGHEST
    )
    grad_rows = grad_sum.astype(jnp.bfloat16)
    grad_features = jnp.dot(grad_rows, weight.T, preferred_element_type=jnp.float32).astype(
        jnp.bfloat16
    )
    local_weight = jnp.dot(features.T, grad_rows, preferred_element_type=jnp.float32)
    weight_total, loss_total = lax.psum((local_weight, total), ("dom", "rep"))
    node_count = lax.axis_size("dom") * reps * rows_here
    return (grad_features, weight_total / node_count, loss_total / node_count)


def solution(mesh):
    placed = (
        P(("dom", "rep"), None),
        P(),
        P(("dom", "rep"), None, None),
        P(("dom", "rep")),
        P(("dom", "rep")),
        P(("dom", "rep"), None),
        P(("dom", "rep")),
        P(("dom", "rep")),
    )
    return jax.shard_map(
        per_device,
        mesh=mesh,
        in_specs=placed,
        out_specs=(P(("dom", "rep"), None), P(), P()),
        check_vma=False,
    )
```

profile of v0, /device:TPU:1, one launch (start us, length us, event | category | flops | bytes accessed | tf_op | source)
XLA Modules:
  0.0 598.2 jit_solution(11418974097780111663)
XLA Ops:
  7.2 0.0 copy-start
  7.2 0.0 reduce-scatter.2.cloned.1.call-start
  7.2 0.9 iota_compare_fusion.2
  8.1 0.0 copy-start.5
  8.1 0.0 copy-start.6
  8.1 1.2 convolution_convert_fusion.1
  9.3 0.9 convolution_convert_fusion.2
  10.2 21.3 %all_gather.7 = bf16[1024,172]{1,0:T(8,128)(2,1)S(1)} all-gather(bf16[128,172]{1,0:T(8,128)(2,1)S(1)} %bitcast.56), channel_id=1, replica_groups=mesh['dom'=128,'rep'=8] {'rep'}, dimensions={0}, use_global_device_ids=true | all-gather | bytes 396288 | tf_op jit(solution)/shard_map/all_gather | solution.py:38
  31.5 9.8 %collective-permute-start = (bf16[512,172]{1,0:T(8,128)(2,1)S(1)}, bf16[512,172]{1,0:T(8,128)(2,1)S(1)}, u32[]{:S(2)}, u32[]{:S(2)}) collective-permute-start(bf16[512,172]{1,0:T(8,128)(2,1)S(1)} %bitcast.53), channel_id=1, source_target_pairs={{0,8},{8,16},{16,24},{24,32},{32,40},{40,48},{48,56},{56,64},{64,7... | collective-permute-start | bytes 528392 | tf_op jit(solution)/shard_map/ppermute | solution.py:12
  41.3 11.6 %collective-permute-start.1 = (bf16[512,172]{1,0:T(8,128)(2,1)S(1)}, bf16[512,172]{1,0:T(8,128)(2,1)S(1)}, u32[]{:S(2)}, u32[]{:S(2)}) collective-permute-start(bf16[512,172]{1,0:T(8,128)(2,1)S(1)} %bitcast.52), channel_id=1, source_target_pairs={{8,0},{16,8},{24,16},{32,24},{40,32},{48,40},{56,48},{64,56},{72,6... | collective-permute-start | bytes 528392 | tf_op jit(solution)/shard_map/ppermute | solution.py:15
  52.8 20.5 %all_gather.6 = bf16[2048,172]{0,1:T(8,128)(2,1)S(1)} all-gather(bf16[256,172]{0,1:T(8,128)(2,1)S(1)} %convolution_convert_fusion.1), channel_id=1, replica_groups=mesh['dom'=128,'rep'=8] {'rep'}, dimensions={0}, use_global_device_ids=true | all-gather | bytes 792576 | tf_op jit(solution)/shard_map/all_gather | solution.py:37
  73.3 0.2 copy.26
  73.5 0.9 slice_bitcast_fusion
  74.4 0.0 copy-done.5
  74.4 0.0 copy-done.6
  74.5 0.0 collective-permute-done
  74.5 0.3 copy.19
  74.8 0.0 collective-permute-done.1
  74.8 1.0 copy.20
  75.8 1.4 pad_maximum_fusion
  77.2 1.3 reshape_reshape.3
  78.6 1.4 copy.21
  79.9 2.5 gather_fusion
  82.4 0.0 copy-done
  82.4 6.0 convolution_bitcast_fusion.1
  88.4 0.0 copy-start.4
  88.4 10.1 %scatter_fusion = f32[2,128,172]{1,2,0:T(8,128)S(1)} fusion(f32[2,128,172]{1,2,0:T(8,128)S(1)} %broadcast_in_dim.15, s32[64]{0:T(128)S(1)} %compare_select_fusion.1, f32[64,128,172]{1,2,0:T(8,128)} %convolution_bitcast_fusion.1), kind=kCustom, calls=%fused_computation.2 | custom fusion | flops 1409024 | bytes 16908544 | tf_op jit(solution)/shard_map/scatter-add | solution.py:59
  98.5 0.1 fusion.2
  98.7 0.0 copy-done.4
  98.7 0.7 select_reduce_fusion
  99.4 2.5 gather_fusion.1
  101.9 5.9 convolution_bitcast_fusion
  107.8 1.5 broadcast_in_dim.12
  109.3 15.5 %scatter_fusion.1 = f32[24,128,172]{1,2,0:T(8,128)} fusion(f32[24,128,172]{1,2,0:T(8,128)} %broadcast_in_dim.12, s32[64]{0:T(128)S(1)} %get-tuple-element.10, f32[64,128,172]{1,2,0:T(8,128)} %convolution_bitcast_fusion), kind=kCustom, calls=%fused_computation.3 | custom fusion | flops 1409024 | bytes 16908544 | tf_op jit(solution)/shard_map/scatter-add | solution.py:77
  124.7 3.4 copy.22
  128.1 0.0 copy-start.3
  128.1 0.0 copy-start.1
  128.1 0.0 copy-start.2
  128.1 0.0 reduce-scatter.2.cloned.1.call-update
  128.2 0.0 all-reduce.2.cloned.1.call-start
  128.2 56.8 %reduce-scatter.2.cloned.1.call-done = f32[384,172]{1,0:T(8,128)} async-done(((f32[3072,172]{1,0:T(8,128)}), f32[384,172]{1,0:T(8,128)}) %reduce-scatter.2.cloned.1.call-update) | async-done | bytes 264208 | tf_op jit(solution)/shard_map/reduce_scatter | solution.py:80
  185.0 0.9 fusion.21
  185.9 6.2 %collective-permute-start.2 = (f32[64,172]{1,0:T(8,128)S(1)}, f32[64,172]{1,0:T(8,128)S(1)}, u32[]{:S(2)}, u32[]{:S(2)}) collective-permute-start(f32[64,172]{1,0:T(8,128)S(1)} %get-tuple-element.5), channel_id=1, source_target_pairs={{0,8},{8,16},{16,24},{24,32},{32,40},{40,48},{48,56},{56,64},{64,7... | collective-permute-start | bytes 132104 | tf_op jit(solution)/shard_map/ppermute | solution.py:12
  192.1 1.9 collective-permute-start.3
  194.7 115.3 %psum.15 = f32[]{:T(128)} all-reduce(f32[]{:T(128)S(6)} %neg.3), channel_id=1, replica_groups=mesh['dom'=128,'rep'=8] {'dom','rep'}, use_global_device_ids=true, to_apply=%region_7.8 | all-reduce | flops 1 | bytes 8 | tf_op jit(solution)/shard_map/psum | solution.py:94
  310.6 0.0 collective-permute-done.2
  310.6 0.0 collective-permute-done.3
  310.7 0.0 copy-done.3
  310.7 1.3 fusion.4
  312.0 0.0 copy-done.1
  312.0 0.9 convolution_bitcast_fusion.3
  312.9 0.0 all-reduce.2.cloned.1.call-update
  312.9 0.0 copy-done.2
  312.9 0.8 convolution_convert_fusion
  313.8 274.8 %all-reduce.2.cloned.1.call-done = f32[256,172]{0,1:T(8,128)} async-done(((f32[256,172]{0,1:T(8,128)}), f32[256,172]{0,1:T(8,128)}) %all-reduce.2.cloned.1.call-update) | async-done | bytes 176144 | tf_op jit(solution)/shard_map/psum | solution.py:94
  588.6 1.6 broadcast_multiply_fusion
  (6 shorter events, 0.1 us)
Async XLA Ops:
  7.2 75.3 %copy-start = (bf16[64,128,128]{2,1,0:T(8,128)(2,1)S(1)}, bf16[64,128,128]{2,1,0:T(8,128)(2,1)}, u32[]{:S(2)}) copy-start(bf16[64,128,128]{2,1,0:T(8,128)(2,1)} %param.10) | copy-start | bytes 6291460
  7.2 177.8 %reduce-scatter.2.cloned.1.call-start = ((), (), s32[]{:S(2)}) async-start(), calls=%async_computation.1 | async-start | bytes 3538944 | tf_op jit(solution)/shard_map/reduce_scatter | solution.py:80
  8.1 66.3 %copy-start.5 = (s32[64]{0:T(128)S(1)}, s32[64]{0:T(128)}, u32[]{:S(2)}) copy-start(s32[64]{0:T(128)} %param.12) | copy-start | bytes 772
  8.1 66.3 %copy-start.6 = (s32[64]{0:T(128)S(1)}, s32[64]{0:T(128)}, u32[]{:S(2)}) copy-start(s32[64]{0:T(128)} %param.11) | copy-start | bytes 772
  31.5 43.0 %collective-permute-start = (bf16[512,172]{1,0:T(8,128)(2,1)S(1)}, bf16[512,172]{1,0:T(8,128)(2,1)S(1)}, u32[]{:S(2)}, u32[]{:S(2)}) collective-permute-start(bf16[512,172]{1,0:T(8,128)(2,1)S(1)} %bitcast.53), channel_id=1, source_target_pairs={{0,8},{8,16},{16,24},{24,32},{32,40},{40,48},{48,56},{56,64},{64,7... | collective-permute-start | bytes 528392 | tf_op jit(solution)/shard_map/ppermute | solution.py:12
  41.3 33.5 %collective-permute-start.1 = (bf16[512,172]{1,0:T(8,128)(2,1)S(1)}, bf16[512,172]{1,0:T(8,128)(2,1)S(1)}, u32[]{:S(2)}, u32[]{:S(2)}) collective-permute-start(bf16[512,172]{1,0:T(8,128)(2,1)S(1)} %bitcast.52), channel_id=1, source_target_pairs={{8,0},{16,8},{24,16},{32,24},{40,32},{48,40},{56,48},{64,56},{72,6... | collective-permute-start | bytes 528392 | tf_op jit(solution)/shard_map/ppermute | solution.py:15
  88.4 10.3 %copy-start.4 = (s32[256]{0:T(256)S(1)}, s32[256]{0:T(256)}, u32[]{:S(2)}) copy-start(s32[256]{0:T(256)} %param.15) | copy-start | bytes 3076
  128.1 182.5 %copy-start.3 = (s32[2,64]{1,0:T(2,128)S(1)}, s32[2,64]{1,0:T(2,128)}, u32[]{:S(2)}) copy-start(s32[2,64]{1,0:T(2,128)} %param.13) | copy-start | bytes 1540
  128.1 183.9 %copy-start.1 = (bf16[256,256]{1,0:T(8,128)(2,1)S(1)}, bf16[256,256]{1,0:T(8,128)(2,1)}, u32[]{:S(2)}) copy-start(bf16[256,256]{1,0:T(8,128)(2,1)} %param.8) | copy-start | bytes 393220
  128.1 184.8 %copy-start.2 = (bf16[256,172]{0,1:T(8,128)(2,1)S(1)}, bf16[256,172]{0,1:T(8,128)(2,1)}, u32[]{:S(2)}) copy-start(bf16[256,172]{0,1:T(8,128)(2,1)} %param.9) | copy-start | bytes 264196
  128.2 460.4 %all-reduce.2.cloned.1.call-start = ((), (), s32[]{:S(2)}) async-start(), calls=%async_computation.2 | async-start | bytes 360448 | tf_op jit(solution)/shard_map/psum | solution.py:94
  185.9 124.8 %collective-permute-start.2 = (f32[64,172]{1,0:T(8,128)S(1)}, f32[64,172]{1,0:T(8,128)S(1)}, u32[]{:S(2)}, u32[]{:S(2)}) collective-permute-start(f32[64,172]{1,0:T(8,128)S(1)} %get-tuple-element.5), channel_id=1, source_target_pairs={{0,8},{8,16},{16,24},{24,32},{32,40},{40,48},{48,56},{56,64},{64,7... | collective-permute-start | bytes 132104 | tf_op jit(solution)/shard_map/ppermute | solution.py:12
  192.1 118.5 %collective-permute-start.3 = (f32[64,172]{1,0:T(8,128)S(1)}, f32[64,172]{1,0:T(8,128)S(1)}, u32[]{:S(2)}, u32[]{:S(2)}) collective-permute-start(f32[64,172]{1,0:T(8,128)S(1)} %get-tuple-element.6), channel_id=1, source_target_pairs={{8,0},{16,8},{24,16},{32,24},{40,32},{48,40},{56,48},{64,56},{72,6... | collective-permute-start | bytes 132104 | tf_op jit(solution)/shard_map/ppermute | solution.py:15
Sparse Core Ops, SparseCore 0:
  128.3 56.6 reduce-scatter.1
  313.1 275.4 all-reduce.1
where the time goes:
time: 599 us; the launch traced here: 598 us
  waiting for transfers between devices  332 us (55%)
  blocking collectives  157 us (26%)
  other arithmetic  30.3 us (5%)
  starting transfers between devices  29.5 us (5%)
  matrix products  17 us (3%)
  between operations  16.7 us (3%)
  local copies, waits for them, and re-layouts  15.9 us (3%)
    psum x1, waiting for transfers between devices, per_device(): weight_total, loss_total = lax.psum((local_weight, total), ('dom', 'rep'))  275 us
    psum x1, blocking collectives, per_device(): weight_total, loss_total = lax.psum((local_weight, total), ('dom', 'rep'))  115 us
    reduce_scatter x1, waiting for transfers between devices, per_device(): summed = lax.psum_scatter(columns, 'rep', scatter_dimension=0, tiled=True)  56.8 us
    all_gather x1, blocking collectives, per_device(): lax.all_gather(outgoing, 'rep', axis=0, tiled=True)  21.3 us
    all_gather x1, blocking collectives, per_device(): lax.all_gather(projected, 'rep', axis=0, tiled=True)  20.5 us
    ppermute x2, starting transfers between devices, extended_2(): lax.ppermute(lax.slice_in_dim(block, block.shape[dim] - width, None, axis...  16 us
    scatter-add x1, other arithmetic, per_device(): columns = jnp.zeros((span, tile, width), jnp.float32).at[target].add(part...  15.5 us
    ppermute x2, starting transfers between devices, extended_2(): lax.ppermute(lax.slice_in_dim(block, 0, width, axis=dim), axis, backward)  13.5 us
  transfers between devices with their start and end apart: 6, of which 2 were waited for; matrix products, arithmetic and copies ran while one was open for 0% of the time, Pallas kernels for 0%

commit v1 on v0

v1 whole, which is shorter than its diff:
```python
import jax
import jax.numpy as jnp
from jax import lax
from jax.experimental import pallas as pl
from jax.experimental.pallas import tpu as pltpu
from jax.sharding import Mesh, PartitionSpec as P

F32 = jnp.float32
BF16 = jnp.bfloat16
LANES = 128
SHAPE = (8, 8, 2, 8)
LAST = (((1,), (1,)), ((), ()))
FIRST = (((0,), (0,)), ((), ()))
PLAIN = (((1,), (0,)), ((), ()))


def round_up(value, unit):
    return -(-value // unit) * unit


def dot(a, b, dims=PLAIN):
    return lax.dot_general(a, b, dims, preferred_element_type=F32)


def vmem():
    return pl.BlockSpec(memory_space=pltpu.VMEM)


def smem():
    return pl.BlockSpec(memory_space=pltpu.SMEM)


def params(mib):
    return pltpu.CompilerParams(vmem_limit_bytes=mib * 2**20)


def pick_kernel(lists, features, picked):
    rows, slots = features.shape[0], lists.shape[1]
    chosen = lax.broadcasted_iota(jnp.int32, (rows, slots), 0) == lists[...]
    onehot = jnp.where(chosen, 1.0, 0.0).astype(BF16)
    picked[...] = dot(onehot, features[...], FIRST).astype(BF16)


def layer_kernel(rows, cols, tiles, columns, weight, labels, out, sums, grads):
    count, tile = tiles.shape[0], tiles.shape[1]
    classes, hidden = weight.shape
    padded = grads.shape[1]
    nodes = labels.shape[1]
    group = 4

    def masked(t):
        block = tiles[t]
        none = jnp.zeros_like(block)
        first = rows[t] == 0
        return jnp.where(first, block, none), jnp.where(first, none, block)

    sums[...] = jnp.zeros_like(sums)
    for start in range(0, count, group):
        picks = [masked(t) for t in range(start, start + group)]
        left = jnp.concatenate(
            [jnp.concatenate([p[i] for p in picks], axis=1) for i in range(2)], axis=0
        )
        right = jnp.concatenate([columns[cols[t]] for t in range(start, start + group)], axis=0)
        sums[...] += dot(left, right)

    total = sums[...]
    high = total.astype(BF16)
    low = (total - high.astype(F32)).astype(BF16)
    wide = jnp.concatenate(
        [weight[...].astype(F32), jnp.zeros((padded - classes, hidden), F32)], axis=0
    ).astype(BF16)
    logits = dot(wide, high, LAST) + dot(wide, low, LAST)
    kind = lax.broadcasted_iota(jnp.int32, (padded, nodes), 0)
    real = kind < classes
    logits = jnp.where(real, logits, -jnp.inf)
    shifted = logits - jnp.max(logits, axis=0, keepdims=True)
    logp = shifted - jnp.log(jnp.sum(jnp.exp(shifted), axis=0, keepdims=True))
    onehot = kind == labels[...]
    losses = -jnp.sum(jnp.where(onehot, logp, 0.0), axis=0, keepdims=True)
    grad = (jnp.exp(logp) - onehot.astype(F32)).astype(BF16)

    weight_grad = dot(grad, high) + dot(grad, low)
    weight_grad = jnp.where(kind == classes, losses, weight_grad)
    quarter = out.shape[1] - 3 * padded
    weight_grad = jnp.concatenate(
        [weight_grad, jnp.zeros((4 * quarter - padded, hidden), F32)], axis=0
    ).astype(BF16)
    for r in range(8):
        h, q = r // 4, r % 4
        out[r, 3 * padded :, :] = weight_grad[
            q * quarter : (q + 1) * quarter, h * LANES : (h + 1) * LANES
        ]

    grads[...] = jnp.zeros_like(grads)
    for start in range(0, count, 2):
        a, b = masked(start), masked(start + 1)
        right = jnp.concatenate(
            [jnp.concatenate([a[i], b[i]], axis=1) for i in range(2)], axis=0
        )
        both = dot(grad, right)
        grads[cols[start]] += both[:, :tile]
        grads[cols[start + 1]] += both[:, tile:]
    for r in range(8):
        for j in range(3):
            out[r, j * padded : (j + 1) * padded, :] = grads[3 * r + j].astype(BF16)


def fold_kernel(parts, own, halo, chunk):
    padded = halo.shape[0]
    summed = parts[0].astype(F32)
    for k in range(1, parts.shape[0]):
        summed += parts[k].astype(F32)
    own[...] = summed[: 2 * padded]
    halo[...] = summed[2 * padded : 3 * padded].astype(BF16)
    chunk[...] = jnp.broadcast_to(summed[3 * padded :][None], chunk.shape)


def sum_kernel(parts, out):
    summed = parts[0]
    for k in range(1, parts.shape[0]):
        summed += parts[k]
    out[...] = jnp.broadcast_to(summed[None], out.shape)


def pair_kernel(a, b, out):
    out[...] = jnp.broadcast_to((a[...] + b[...])[None], out.shape)


def rows_kernel(own, before, after, lists, weight, out):
    padded = before.shape[0]
    classes, hidden = weight.shape
    nodes, slots = out.shape[0], lists.shape[1]
    send = slots // 2
    chosen = lax.broadcasted_iota(jnp.int32, (nodes, slots), 0) == lists[...]
    onehot = jnp.where(chosen, 1.0, 0.0).astype(BF16)
    low = lax.broadcasted_iota(jnp.int32, (padded, slots), 1)
    back = jnp.where(low < send, pltpu.roll(before[...].astype(F32), send, 1), pltpu.roll(after[...].astype(F32), send, 1))
    total = jnp.concatenate([own[:padded], own[padded:]], axis=1)
    total += dot(back.astype(BF16), onehot, LAST)
    grad = total[:classes].astype(BF16)
    out[...] = dot(grad, weight[...], FIRST).astype(BF16)


def last_kernel(parts, weight_grad, loss, scale):
    classes = weight_grad.shape[0]
    gathered = jnp.concatenate(
        [jnp.concatenate([parts[4 * h + q] for q in range(4)], axis=0) for h in range(2)], axis=1
    )
    weight_grad[...] = gathered[:classes] * scale
    loss[...] = jnp.sum(gathered[classes : classes + 1], axis=1, keepdims=True) * scale


def per_device(features, weight, tiles, tile_rows, tile_cols, send_lists, counts, labels):
    nodes, hidden = features.shape
    classes = weight.shape[1]
    send = send_lists.shape[1]
    slots = 2 * send
    tile = tiles.shape[1]
    reps = lax.axis_size("x")
    domains = lax.axis_size("z") * lax.axis_size("y") * lax.axis_size("c")
    padded = round_up(classes + 1, 16)
    quarter = round_up(-(-padded // 4), 16)
    height = 3 * padded + quarter
    dom = ("z", "y", "c")
    up = [(i, i + 1) for i in range(domains - 1)]
    down = [(i + 1, i) for i in range(domains - 1)]
    shape = jax.ShapeDtypeStruct
    weight = weight.T

    live = jnp.arange(send, dtype=jnp.int32)[None, :] < counts[:, None]
    lists = jnp.where(live, send_lists, -1).reshape(1, slots)
    picked = pl.pallas_call(
        pick_kernel,
        out_shape=shape((slots, hidden), BF16),
        in_specs=[vmem()] * 2,
        out_specs=vmem(),
    )(lists, features)
    from_before = lax.ppermute(picked[send:], dom, up)
    from_after = lax.ppermute(picked[:send], dom, down)
    block = jnp.concatenate([features, from_before, from_after], axis=0)
    extended = lax.all_gather(block, "x", axis=0, tiled=True)

    payload = pl.pallas_call(
        layer_kernel,
        out_shape=shape((reps, height, LANES), BF16),
        in_specs=[smem(), smem(), vmem(), vmem(), vmem(), vmem()],
        out_specs=vmem(),
        scratch_shapes=[
            pltpu.VMEM((nodes, hidden), F32),
            pltpu.VMEM((3 * reps, padded, tile), F32),
        ],
        compiler_params=params(40),
    )(
        tile_rows,
        tile_cols,
        tiles,
        extended.reshape(-1, tile, hidden),
        weight,
        labels.reshape(1, nodes),
    )
    parts = lax.all_to_all(payload, "x", 0, 0, tiled=True)
    own, halo, chunk = pl.pallas_call(
        fold_kernel,
        out_shape=(
            shape((2 * padded, LANES), F32),
            shape((padded, LANES), BF16),
            shape((lax.axis_size("y"), quarter, LANES), F32),
        ),
        in_specs=[vmem()],
        out_specs=(vmem(),) * 3,
    )(parts)
    before = lax.ppermute(halo, dom, up)
    after = lax.ppermute(halo, dom, down)

    def fold(x, axis, copies):
        return pl.pallas_call(
            sum_kernel,
            out_shape=shape((copies, *x.shape[1:]), F32),
            in_specs=[vmem()],
            out_specs=vmem(),
        )(lax.all_to_all(x, axis, 0, 0, tiled=True))

    chunk = fold(fold(chunk, "y", lax.axis_size("z")), "z", 1)[0]
    other = lax.ppermute(chunk, "c", [(0, 1), (1, 0)])
    chunk = pl.pallas_call(
        pair_kernel,
        out_shape=shape((reps, quarter, LANES), F32),
        in_specs=[vmem()] * 2,
        out_specs=vmem(),
    )(chunk, other)
    chunks = lax.all_to_all(chunk, "x", 0, 0, tiled=True)
    scale = 1.0 / (domains * reps * nodes)
    weight_grad, loss = pl.pallas_call(
        lambda a, b, c: last_kernel(a, b, c, scale),
        out_shape=(shape((classes, hidden), F32), shape((1, 1), F32)),
        in_specs=[vmem()],
        out_specs=(vmem(),) * 2,
    )(chunks)

    grad_features = pl.pallas_call(
        rows_kernel,
        out_shape=shape((nodes, hidden), BF16),
        in_specs=[vmem()] * 5,
        out_specs=vmem(),
    )(own, before, after, lists, weight)
    return grad_features, weight_grad.T, loss.reshape(())


def solution(mesh):
    split = Mesh(mesh.devices.reshape(SHAPE), ("z", "y", "c", "x"))
    both = ("z", "y", "c", "x")
    placed = (
        P(both, None),
        P(),
        P(both, None, None),
        P(both),
        P(both),
        P(both, None),
        P(both),
        P(both),
    )
    return jax.shard_map(
        per_device,
        mesh=split,
        in_specs=placed,
        out_specs=(P(both, None), P(), P()),
        check_vma=False,
    )
```

time: 599 us -> 191 us (0.32)
  waiting for transfers between devices: 332 us -> 47.7 us
  blocking collectives: 157 us -> 61.5 us
  other arithmetic: 30.3 us -> 2.34 us
  Pallas kernels: 0 us -> 17.2 us
  matrix products: 17 us -> 0 us
  starting transfers between devices: 29.5 us -> 37.8 us
  local copies, waits for them, and re-layouts: 15.9 us -> 9.14 us
    psum x1 -> x0, waiting for transfers between devices: 275 us -> none  [per_device(): weight_total, loss_total = lax.psum((local_weight, total), ('dom', 'rep'))]
    psum x1 -> x0, blocking collectives: 115 us -> none  [per_device(): weight_total, loss_total = lax.psum((local_weight, total), ('dom', 'rep'))]
    all_to_all x0 -> x3, blocking collectives: none -> 61.5 us  [the longest x2 32 us: fold(): lax.all_to_all(x, axis, 0, 0, tiled=True)]
    reduce_scatter x1 -> x0, waiting for transfers between devices: 56.8 us -> none  [per_device(): summed = lax.psum_scatter(columns, 'rep', scatter_dimension=0, tiled=True)]
    all_gather x0 -> x1, waiting for transfers between devices: none -> 43.7 us  [per_device(): extended = lax.all_gather(block, 'x', axis=0, tiled=True)]
    all_gather x2 -> x0, blocking collectives: 41.8 us -> none  [the longest x1 21.3 us: per_device(): lax.all_gather(outgoing, 'rep', axis=0, tiled=True)]
    scatter-add x2 -> x0, other arithmetic: 25.6 us -> none  [the longest x1 15.5 us: per_device(): columns = jnp.zeros((span, tile, width), jnp.float32).at[target].add(part...]
    pallas_call x0 -> x8, Pallas kernels: none -> 17.2 us  [the longest x1 4.96 us: per_device(): pl.pallas_call(layer_kernel, out_shape=shape((reps, height, LANES), BF16)...]
  transfers between devices with their start and end apart: 6 -> 7, of which waited for: 2 -> 6; matrix products, arithmetic and copies ran while one was open for 0% -> 0% of each run, Pallas kernels for 0% -> 1%
where the time goes in v1:
time: 191 us; the launch traced here: 190 us
  blocking collectives  61.5 us (32%)
  waiting for transfers between devices  47.7 us (25%)
  starting transfers between devices  37.8 us (20%)
  Pallas kernels  17.2 us (9%)
  between operations  14.1 us (7%)
  local copies, waits for them, and re-layouts  9.14 us (5%)
  other arithmetic  2.34 us (1%)
    all_gather x1, waiting for transfers between devices, per_device(): extended = lax.all_gather(block, 'x', axis=0, tiled=True)  43.7 us
    all_to_all x2, blocking collectives, fold(): lax.all_to_all(x, axis, 0, 0, tiled=True)  32 us
    all_to_all x1, blocking collectives, per_device(): parts = lax.all_to_all(payload, 'x', 0, 0, tiled=True)  29.5 us
    ppermute x1, starting transfers between devices, per_device(): from_after = lax.ppermute(picked[:send], dom, down)  12.6 us
    ppermute x1, starting transfers between devices, per_device(): other = lax.ppermute(chunk, 'c', [(0, 1), (1, 0)])  11.5 us
    unnamed x22, local copies, waits for them, and re-layouts  7.77 us
    pallas_call x1, Pallas kernels, per_device(): pl.pallas_call(layer_kernel, out_shape=shape((reps, height, LANES), BF16)...  4.96 us
    ppermute x1, starting transfers between devices, per_device(): from_before = lax.ppermute(picked[send:], dom, up)  4.7 us
  transfers between devices with their start and end apart: 7, of which 6 were waited for; matrix products, arithmetic and copies ran while one was open for 0% of the time, Pallas kernels for 1%

profile of v1, /device:TPU:1, one launch (start us, length us, event | category | flops | bytes accessed | tf_op | source)
XLA Modules:
  0.0 189.8 jit_solution(13723410158605862291)
XLA Ops:
  7.2 0.0 all-gather.2.cloned.1.call-start
  7.2 0.8 compare_select_fusion
  8.0 0.6 reshape.19.lists
  8.6 1.8 shard_map.103
  10.3 0.8 fusion
  11.1 4.7 %collective-permute-start = (bf16[64,256]{1,0:T(8,128)(2,1)S(1)}, bf16[64,256]{1,0:T(8,128)(2,1)S(1)}, u32[]{:S(2)}, u32[]{:S(2)}) collective-permute-start(bf16[64,256]{1,0:T(8,128)(2,1)S(1)} %get-tuple-element.13), channel_id=1, source_target_pairs={{0,8},{8,16},{16,24},{24,32},{32,40},{40,48},{48,56},{56,64},{64,7... | collective-permute-start | bytes 98312 | tf_op jit(solution)/shard_map/ppermute | solution.py:178
  15.8 12.6 %collective-permute-start.1 = (bf16[64,256]{1,0:T(8,128)(2,1)S(1)}, bf16[64,256]{1,0:T(8,128)(2,1)S(1)}, u32[]{:S(2)}, u32[]{:S(2)}) collective-permute-start(bf16[64,256]{1,0:T(8,128)(2,1)S(1)} %get-tuple-element.14), channel_id=1, source_target_pairs={{8,0},{16,8},{24,16},{32,24},{40,32},{48,40},{56,48},{64,56},{72,6... | collective-permute-start | bytes 98312 | tf_op jit(solution)/shard_map/ppermute | solution.py:179
  28.4 0.0 collective-permute-done
  28.5 0.8 collective-permute-done.1
  29.3 1.6 pad_maximum_fusion
  30.9 0.0 all-gather.2.cloned.1.call-update
  30.9 43.7 %all-gather.2.cloned.1.call-done = bf16[3072,256]{1,0:T(8,128)(2,1)} async-done(((bf16[384,256]{1,0:T(8,128)(2,1)}), bf16[3072,256]{1,0:T(8,128)(2,1)}) %all-gather.2.cloned.1.call-update) | async-done | bytes 1572880 | tf_op jit(solution)/shard_map/all_gather | solution.py:181
  74.6 0.0 copy-start
  74.6 1.6 copy-done
  76.2 0.0 copy-start.1
  76.2 1.4 copy-done.1
  77.6 0.0 copy-start.2
  77.6 0.9 copy-done.2
  78.5 0.0 copy-start.3
  78.5 0.7 copy-done.3
  79.2 0.0 copy-start.4
  79.2 0.7 copy-done.4
  79.9 0.0 copy-start.5
  79.9 0.7 copy-done.5
  80.5 5.0 %shard_map.104 = bf16[8,576,128]{2,1,0:T(8,128)(2,1)S(1)} custom-call(s32[64]{0:T(128)S(1)} %copy-done.4, s32[64]{0:T(128)S(1)} %copy-done.5, bf16[64,128,128]{2,1,0:T(8,128)(2,1)S(1)} %copy-done, bf16[24,128,256]{2,1,0:T(8,128)(2,1)S(1)} %bitcast.6, bf16[172,256]{1,0:T(8,128)(2,1)S(1)} %bitcast.8, s32[1,256]{1,0:T(1,128)S(1)} %bitcast.9), custom_call_target="tpu_custom_call" | custom-call | tf_op jit(solution)/shard_map/pallas_call | solution.py:183
  85.5 29.5 %all_to_all.20.parts = bf16[8,576,128]{2,1,0:T(8,128)(2,1)} all-to-all(bf16[8,576,128]{2,1,0:T(8,128)(2,1)S(1)} %shard_map.104), channel_id=1, replica_groups=mesh['z'=8,'y'=8,'c'=2,'x'=8] {'x'}, dimensions={0} | all-to-all | bytes 2359296 | tf_op jit(solution)/shard_map/all_to_all | solution.py:201
  115.0 2.1 %shard_map.105 = (f32[352,128]{1,0:T(8,128)}, bf16[176,128]{1,0:T(8,128)(2,1)}, f32[8,48,128]{2,1,0:T(8,128)}) custom-call(bf16[8,576,128]{2,1,0:T(8,128)(2,1)} %all_to_all.20.parts), custom_call_target="tpu_custom_call" | custom-call | tf_op jit(solution)/shard_map/pallas_call | solution.py:202
  117.1 0.0 copy-start.10
  117.1 15.4 %all_to_all.21.parts = f32[8,48,128]{2,1,0:T(8,128)} all-to-all(f32[8,48,128]{2,1,0:T(8,128)} %get-tuple-element.10), channel_id=1, replica_groups=mesh['z'=8,'y'=8,'c'=2,'x'=8] {'y'}, dimensions={0} | all-to-all | bytes 393216 | tf_op jit(solution)/shard_map/all_to_all | solution.py:221
  132.6 1.6 shard_map.107
  134.2 16.6 %all_to_all.22.parts = f32[8,48,128]{2,1,0:T(8,128)} all-to-all(f32[8,48,128]{2,1,0:T(8,128)} %shard_map.107), channel_id=1, replica_groups=mesh['z'=8,'y'=8,'c'=2,'x'=8] {'z'}, dimensions={0} | all-to-all | bytes 393216 | tf_op jit(solution)/shard_map/all_to_all | solution.py:221
  150.7 1.5 shard_map.108
  152.3 11.5 %collective-permute-start.4 = (f32[48,128]{1,0:T(8,128)}, f32[48,128]{1,0:T(8,128)S(1)}, u32[]{:S(2)}, u32[]{:S(2)}) collective-permute-start(f32[48,128]{1,0:T(8,128)} %bitcast.10), channel_id=1, source_target_pairs={{0,8},{8,0},{1,9},{9,1},{2,10},{10,2},{3,11},{11,3},{4,12},{12,4},... | collective-permute-start | bytes 73736 | tf_op jit(solution)/shard_map/ppermute | solution.py:224
  163.8 1.0 collective-permute-done.4.b
  164.8 0.0 copy-start.9
  164.8 0.6 copy-done.9
  165.4 1.4 shard_map.109
  166.8 3.4 %all-to-all-start.3 = ((f32[8,48,128]{2,1,0:T(8,128)}), f32[8,48,128]{2,1,0:T(8,128)S(1)}, u32[]{:S(2)}, u32[]{:S(2)}) async-start(f32[8,48,128]{2,1,0:T(8,128)} %shard_map.109), calls=%async_computation.3 | async-start | bytes 393216 | tf_op jit(solution)/shard_map/all_to_all | solution.py:231
  170.2 0.0 copy-done.10
  170.2 2.3 %collective-permute-start.3 = (bf16[176,128]{1,0:T(8,128)(2,1)S(1)}, bf16[176,128]{1,0:T(8,128)(2,1)S(1)}, u32[]{:S(2)}, u32[]{:S(2)}) collective-permute-start(bf16[176,128]{1,0:T(8,128)(2,1)S(1)} %copy-done.10), channel_id=1, source_target_pairs={{8,0},{16,8},{24,16},{32,24},{40,32},{48,40},{56,48},{64,56},{72,6... | collective-permute-start | bytes 135176 | tf_op jit(solution)/shard_map/ppermute | solution.py:213
  172.5 3.3 %collective-permute-start.2 = (bf16[176,128]{1,0:T(8,128)(2,1)S(1)}, bf16[176,128]{1,0:T(8,128)(2,1)S(1)}, u32[]{:S(2)}, u32[]{:S(2)}) collective-permute-start(bf16[176,128]{1,0:T(8,128)(2,1)S(1)} %copy-done.10), channel_id=1, source_target_pairs={{0,8},{8,16},{16,24},{24,32},{32,40},{40,48},{48,56},{56,64},{64,7... | collective-permute-start | bytes 135176 | tf_op jit(solution)/shard_map/ppermute | solution.py:212
  175.8 0.1 collective-permute-done.3.after
  175.9 0.0 copy-start.7
  175.9 1.0 collective-permute-done.2.before
  176.9 0.0 copy-start.8
  176.9 0.0 copy-done.7
  176.9 0.6 copy-done.8
  177.6 2.2 %shard_map.106 = bf16[256,256]{1,0:T(8,128)(2,1)} custom-call(f32[352,128]{1,0:T(8,128)} %get-tuple-element.8.own, bf16[176,128]{1,0:T(8,128)(2,1)} %copy-done.8, bf16[176,128]{1,0:T(8,128)(2,1)} %copy-done.7, s32[1,128]{1,0:T(1,128)} %reshape.19.lists, bf16[172,256]{1,0:T(8,128)(2,1)} %bitcast.7), custom_call_target="tpu_custom_call" | custom-call | tf_op jit(solution)/shard_map/pallas_call | solution.py:240
  179.7 0.9 all-to-all-done.3.a
  180.7 0.0 copy-start.6
  180.7 0.7 copy-done.6
  181.3 1.6 shard_map.110
Async XLA Ops:
  7.2 67.5 %all-gather.2.cloned.1.call-start = ((), (), s32[]{:S(2)}) async-start(), calls=%async_computation.4 | async-start | bytes 1769472 | tf_op jit(solution)/shard_map/all_gather | solution.py:181
  11.1 17.4 %collective-permute-start = (bf16[64,256]{1,0:T(8,128)(2,1)S(1)}, bf16[64,256]{1,0:T(8,128)(2,1)S(1)}, u32[]{:S(2)}, u32[]{:S(2)}) collective-permute-start(bf16[64,256]{1,0:T(8,128)(2,1)S(1)} %get-tuple-element.13), channel_id=1, source_target_pairs={{0,8},{8,16},{16,24},{24,32},{32,40},{40,48},{48,56},{56,64},{64,7... | collective-permute-start | bytes 98312 | tf_op jit(solution)/shard_map/ppermute | solution.py:178
  15.8 13.5 %collective-permute-start.1 = (bf16[64,256]{1,0:T(8,128)(2,1)S(1)}, bf16[64,256]{1,0:T(8,128)(2,1)S(1)}, u32[]{:S(2)}, u32[]{:S(2)}) collective-permute-start(bf16[64,256]{1,0:T(8,128)(2,1)S(1)} %get-tuple-element.14), channel_id=1, source_target_pairs={{8,0},{16,8},{24,16},{32,24},{40,32},{48,40},{56,48},{64,56},{72,6... | collective-permute-start | bytes 98312 | tf_op jit(solution)/shard_map/ppermute | solution.py:179
  74.6 1.6 copy-start
  76.2 1.4 copy-start.1
  77.6 0.9 copy-start.2
  78.5 0.7 copy-start.3
  79.2 0.7 copy-start.4
  79.9 0.7 copy-start.5
  117.1 53.1 %copy-start.10 = (bf16[176,128]{1,0:T(8,128)(2,1)S(1)}, bf16[176,128]{1,0:T(8,128)(2,1)}, u32[]{:S(2)}) copy-start(bf16[176,128]{1,0:T(8,128)(2,1)} %get-tuple-element.9) | copy-start | bytes 135172
  152.3 12.5 %collective-permute-start.4 = (f32[48,128]{1,0:T(8,128)}, f32[48,128]{1,0:T(8,128)S(1)}, u32[]{:S(2)}, u32[]{:S(2)}) collective-permute-start(f32[48,128]{1,0:T(8,128)} %bitcast.10), channel_id=1, source_target_pairs={{0,8},{8,0},{1,9},{9,1},{2,10},{10,2},{3,11},{11,3},{4,12},{12,4},... | collective-permute-start | bytes 73736 | tf_op jit(solution)/shard_map/ppermute | solution.py:224
  164.8 0.6 copy-start.9
  166.8 13.8 %all-to-all-start.3 = ((f32[8,48,128]{2,1,0:T(8,128)}), f32[8,48,128]{2,1,0:T(8,128)S(1)}, u32[]{:S(2)}, u32[]{:S(2)}) async-start(f32[8,48,128]{2,1,0:T(8,128)} %shard_map.109), calls=%async_computation.3 | async-start | bytes 393216 | tf_op jit(solution)/shard_map/all_to_all | solution.py:231
  170.2 5.7 %collective-permute-start.3 = (bf16[176,128]{1,0:T(8,128)(2,1)S(1)}, bf16[176,128]{1,0:T(8,128)(2,1)S(1)}, u32[]{:S(2)}, u32[]{:S(2)}) collective-permute-start(bf16[176,128]{1,0:T(8,128)(2,1)S(1)} %copy-done.10), channel_id=1, source_target_pairs={{8,0},{16,8},{24,16},{32,24},{40,32},{48,40},{56,48},{64,56},{72,6... | collective-permute-start | bytes 135176 | tf_op jit(solution)/shard_map/ppermute | solution.py:213
  172.5 4.4 %collective-permute-start.2 = (bf16[176,128]{1,0:T(8,128)(2,1)S(1)}, bf16[176,128]{1,0:T(8,128)(2,1)S(1)}, u32[]{:S(2)}, u32[]{:S(2)}) collective-permute-start(bf16[176,128]{1,0:T(8,128)(2,1)S(1)} %copy-done.10), channel_id=1, source_target_pairs={{0,8},{8,16},{16,24},{24,32},{32,40},{40,48},{48,56},{56,64},{64,7... | collective-permute-start | bytes 135176 | tf_op jit(solution)/shard_map/ppermute | solution.py:212
  175.9 1.0 copy-start.7
  176.9 0.6 copy-start.8
  180.7 0.7 copy-start.6
Sparse Core Ops, SparseCore 0:
  31.0 43.5 all-gather.1

commit v2 on v1

v2 whole, which is shorter than its diff:
```python
import jax
import jax.numpy as jnp
from jax import lax
from jax.experimental import pallas as pl
from jax.experimental.pallas import tpu as pltpu
from jax.sharding import Mesh, PartitionSpec as P

F32 = jnp.float32
BF16 = jnp.bfloat16
LANES = 128
SHAPE = (8, 8, 2, 8)
LAST = (((1,), (1,)), ((), ()))
FIRST = (((0,), (0,)), ((), ()))
PLAIN = (((1,), (0,)), ((), ()))


def round_up(value, unit):
    return -(-value // unit) * unit


def dot(a, b, dims=PLAIN):
    return lax.dot_general(a, b, dims, preferred_element_type=F32)


def vmem():
    return pl.BlockSpec(memory_space=pltpu.VMEM)


def smem():
    return pl.BlockSpec(memory_space=pltpu.SMEM)


def hbm():
    return pl.BlockSpec(memory_space=pl.ANY)


def params(mib):
    return pltpu.CompilerParams(vmem_limit_bytes=mib * 2**20)


def slots_onehot(counts, send_lists, rows):
    send = send_lists.shape[1]
    row = lax.broadcasted_iota(jnp.int32, (rows, send), 0)
    slot = lax.broadcasted_iota(jnp.int32, (rows, send), 1)
    sides = [
        jnp.where((row == send_lists[i : i + 1, :]) & (slot < counts[i]), 1.0, 0.0)
        for i in range(2)
    ]
    return [side.astype(BF16) for side in sides]


def pick_kernel(counts, send_lists, features, first, second):
    sides = slots_onehot(counts, send_lists, features.shape[0])
    for onehot, out in zip(sides, (first, second), strict=True):
        out[...] = dot(onehot, features[...], FIRST).astype(BF16)


def layer_kernel(
    rows, cols, tiles_hbm, own_hbm, halo_hbm, weight, labels,
    weight_out, grads,
    tiles, columns, sums, sems,
):
    count, tile = tiles.shape[0], tiles.shape[1]
    classes, hidden = weight.shape
    padded = grads.shape[1]
    nodes = labels.shape[1]
    group = 4
    copies = [
        pltpu.make_async_copy(own_hbm, columns.at[:, 0:2], sems.at[0]),
        pltpu.make_async_copy(halo_hbm, columns.at[:, 2:3], sems.at[1]),
        pltpu.make_async_copy(tiles_hbm, tiles, sems.at[2]),
    ]
    for copy in copies:
        copy.start()

    def masked(t):
        block = tiles[t]
        none = jnp.zeros_like(block)
        first = rows[t] == 0
        return jnp.where(first, block, none), jnp.where(first, none, block)

    def column(t):
        member = cols[t] // 3
        return columns[member, cols[t] - 3 * member]

    sums[...] = jnp.zeros_like(sums)
    grads[...] = jnp.zeros_like(grads)
    for copy in copies:
        copy.wait()
    for start in range(0, count, group):
        picks = [masked(t) for t in range(start, start + group)]
        left = jnp.concatenate(
            [jnp.concatenate([p[i] for p in picks], axis=1) for i in range(2)], axis=0
        )
        right = jnp.concatenate([column(t) for t in range(start, start + group)], axis=0)
        sums[...] += dot(left, right)

    total = sums[...]
    high = total.astype(BF16)
    low = (total - high.astype(F32)).astype(BF16)
    wide = jnp.concatenate(
        [weight[...].astype(F32), jnp.zeros((padded - classes, hidden), F32)], axis=0
    ).astype(BF16)
    logits = dot(wide, high, LAST) + dot(wide, low, LAST)
    kind = lax.broadcasted_iota(jnp.int32, (padded, nodes), 0)
    logits = jnp.where(kind < classes, logits, -jnp.inf)
    shifted = logits - jnp.max(logits, axis=0, keepdims=True)
    logp = shifted - jnp.log(jnp.sum(jnp.exp(shifted), axis=0, keepdims=True))
    onehot = kind == labels[...]
    losses = -jnp.sum(jnp.where(onehot, logp, 0.0), axis=0, keepdims=True)
    grad = (jnp.exp(logp) - onehot.astype(F32)).astype(BF16)

    weight_grad = dot(grad, high) + dot(grad, low)
    weight_grad = jnp.where(kind == classes, losses, weight_grad)
    pieces, height = weight_out.shape[0] // 2, weight_out.shape[1]
    weight_grad = jnp.concatenate(
        [weight_grad, jnp.zeros((pieces * height - padded, hidden), F32)], axis=0
    )
    for half in range(2):
        for q in range(pieces):
            weight_out[pieces * half + q] = weight_grad[
                q * height : (q + 1) * height, half * LANES : (half + 1) * LANES
            ]

    for start in range(0, count, 2):
        a, b = masked(start), masked(start + 1)
        right = jnp.concatenate([jnp.concatenate([a[i], b[i]], axis=1) for i in range(2)], axis=0)
        both = dot(grad, right)
        grads[cols[start]] += both[:, :tile]
        grads[cols[start + 1]] += both[:, tile:]

def sum_kernel(parts, out):
    summed = parts[0]
    for k in range(1, parts.shape[0]):
        summed += parts[k]
    out[...] = jnp.broadcast_to(summed[None], out.shape)


def rows_kernel(counts, send_lists, own, before, after, weight, out):
    padded = before.shape[0]
    classes = weight.shape[0]
    first, second = slots_onehot(counts, send_lists, out.shape[0])
    send = send_lists.shape[1]
    total = jnp.concatenate([own[0], own[1]], axis=1)
    total += dot(before[:, send:], first, LAST)
    total += dot(after[:, :send], second, LAST)
    grad = total[:classes].astype(BF16)
    out[...] = dot(grad, weight[...], FIRST).astype(BF16)


def last_kernel(scale, parts, weight_grad, loss):
    classes = weight_grad.shape[0]
    pieces = parts.shape[0] // 2
    gathered = jnp.concatenate(
        [
            jnp.concatenate([parts[pieces * h + q] for q in range(pieces)], axis=0)
            for h in range(2)
        ],
        axis=1,
    )
    weight_grad[...] = gathered[:classes] * scale
    loss[...] = jnp.sum(gathered[classes : classes + 1], axis=1, keepdims=True) * scale


def per_device(features, weight, tiles, tile_rows, tile_cols, send_lists, counts, labels):
    nodes, hidden = features.shape
    classes = weight.shape[1]
    send = send_lists.shape[1]
    count, tile = tiles.shape[0], tiles.shape[1]
    reps = lax.axis_size("x")
    dom = ("z", "y", "c")
    domains = lax.axis_size(dom)
    near = ("y", "c")
    pieces = lax.axis_size(near)
    padded = round_up(classes + 1, 16)
    height = round_up(-(-padded // (pieces // 2)), 8)
    up = [(i, i + 1) for i in range(domains - 1)]
    down = [(i + 1, i) for i in range(domains - 1)]
    shape = jax.ShapeDtypeStruct
    weight = weight.T

    first, second = pl.pallas_call(
        pick_kernel,
        out_shape=(shape((send, hidden), BF16),) * 2,
        in_specs=[smem(), vmem(), vmem()],
        out_specs=(vmem(),) * 2,
    )(counts, send_lists, features)
    from_before = lax.ppermute(second, dom, up)
    from_after = lax.ppermute(first, dom, down)
    own_rows = lax.all_gather(features, "x", axis=0, tiled=True)
    halo_rows = lax.all_gather(
        jnp.concatenate([from_before, from_after], axis=0), "x", axis=0, tiled=True
    )

    weight_parts, parts = pl.pallas_call(
        layer_kernel,
        out_shape=(
            shape((pieces, height, LANES), F32),
            shape((3 * reps, padded, tile), F32),
        ),
        in_specs=[smem(), smem(), hbm(), hbm(), hbm(), vmem(), vmem()],
        out_specs=(vmem(),) * 2,
        scratch_shapes=[
            pltpu.VMEM((count, tile, tile), BF16),
            pltpu.VMEM((reps, 3, tile, hidden), BF16),
            pltpu.VMEM((nodes, hidden), F32),
            pltpu.SemaphoreType.DMA((3,)),
        ],
        compiler_params=params(56),
    )(
        tile_rows,
        tile_cols,
        tiles,
        own_rows.reshape(reps, 2, tile, hidden),
        halo_rows.reshape(reps, 1, tile, hidden),
        weight,
        labels.reshape(1, nodes),
    )

    def fold(parts, copies):
        return pl.pallas_call(
            sum_kernel,
            out_shape=shape((copies, *parts.shape[1:]), F32),
            in_specs=[vmem()],
            out_specs=vmem(),
        )(parts)

    weight_parts = lax.all_to_all(weight_parts, near, 0, 0, tiled=True)
    own = lax.psum_scatter(parts, "x", scatter_dimension=0, tiled=True)
    for axis, following in (("z", "z"), ("x", "x"), (near, near)):
        weight_parts = fold(weight_parts, lax.axis_size(axis))
        weight_parts = lax.all_to_all(weight_parts, following, 0, 0, tiled=True)

    halo = own[2].astype(BF16)
    before = lax.ppermute(halo, dom, up)
    after = lax.ppermute(halo, dom, down)
    grad_features = pl.pallas_call(
        rows_kernel,
        out_shape=shape((nodes, hidden), BF16),
        in_specs=[smem()] + [vmem()] * 5,
        out_specs=vmem(),
    )(counts, send_lists, own, before, after, weight)

    scale = 1.0 / (domains * reps * nodes)
    weight_grad, loss = pl.pallas_call(
        lambda *refs: last_kernel(scale, *refs),
        out_shape=(shape((classes, hidden), F32), shape((1, 1), F32)),
        in_specs=[vmem()],
        out_specs=(vmem(),) * 2,
    )(weight_parts)
    return grad_features, weight_grad.T, loss.reshape(())


def solution(mesh):
    split = Mesh(mesh.devices.reshape(SHAPE), ("z", "y", "c", "x"))
    both = ("z", "y", "c", "x")
    placed = (
        P(both, None),
        P(),
        P(both, None, None),
        P(both),
        P(both),
        P(both, None),
        P(both),
        P(both),
    )
    return jax.shard_map(
        per_device,
        mesh=split,
        in_specs=placed,
        out_specs=(P(both, None), P(), P()),
        check_vma=False,
    )
```

time: 191 us -> 156 us (0.82)
  waiting for transfers between devices: 47.7 us -> 19.2 us
  blocking collectives: 61.5 us -> 70.9 us
  starting transfers between devices: 37.8 us -> 28.6 us
  local copies, waits for them, and re-layouts: 9.14 us -> 3.68 us
  other arithmetic: 2.34 us -> 0.01 us
    all_gather x1, waiting for transfers between devices: 43.7 us -> 13.6 us  [per_device(): own_rows = lax.all_gather(features, 'x', axis=0, tiled=True)]
    all_gather x0 -> x1, blocking collectives: none -> 22.3 us  [per_device(): lax.all_gather(jnp.concatenate([from_before, from_after], axis=0), 'x', a...]
    all_to_all x3, blocking collectives: 61.5 us -> 48.6 us  [the longest x2 28.3 us: per_device(): weight_parts = lax.all_to_all(weight_parts, following, 0, 0, tiled=True)]
    ppermute x3 -> x2, starting transfers between devices: 28.8 us -> 17.3 us  [the longest x1 12.6 us: per_device(): from_after = lax.ppermute(first, dom, down)]
    unnamed x22 -> x8, local copies, waits for them, and re-layouts: 7.77 us -> 2.78 us
    all_to_all x1, waiting for transfers between devices: 0.94 us -> 3.89 us  [per_device(): weight_parts = lax.all_to_all(weight_parts, following, 0, 0, tiled=True)]
    all_to_all x1, starting transfers between devices: 3.39 us -> 5.61 us  [per_device(): weight_parts = lax.all_to_all(weight_parts, following, 0, 0, tiled=True)]
    pallas_call x7 -> x6, Pallas kernels: 15.1 us -> 16.7 us  [the longest x1 8.56 us: per_device(): pl.pallas_call(layer_kernel, out_shape=(shape((pieces, height, LANES), F3...]
  transfers between devices with their start and end apart: 7 -> 7, of which waited for: 6 -> 3; matrix products, arithmetic and copies ran while one was open for 0% -> 1% of each run, Pallas kernels for 1% -> 5%
where the time goes in v2:
time: 156 us; the launch traced here: 155 us
  blocking collectives  70.9 us (45%)
  starting transfers between devices  28.6 us (18%)
  waiting for transfers between devices  19.2 us (12%)
  Pallas kernels  18.9 us (12%)
  between operations  14.1 us (9%)
  local copies, waits for them, and re-layouts  3.68 us (2%)
    all_to_all x2, blocking collectives, per_device(): weight_parts = lax.all_to_all(weight_parts, following, 0, 0, tiled=True)  28.3 us
    all_gather x1, blocking collectives, per_device(): lax.all_gather(jnp.concatenate([from_before, from_after], axis=0), 'x', a...  22.3 us
    all_to_all x1, blocking collectives, per_device(): weight_parts = lax.all_to_all(weight_parts, near, 0, 0, tiled=True)  20.3 us
    all_gather x1, waiting for transfers between devices, per_device(): own_rows = lax.all_gather(features, 'x', axis=0, tiled=True)  13.6 us
    ppermute x1, starting transfers between devices, per_device(): from_after = lax.ppermute(first, dom, down)  12.6 us
    pallas_call x1, Pallas kernels, per_device(): pl.pallas_call(layer_kernel, out_shape=(shape((pieces, height, LANES), F3...  8.56 us
    all_to_all x1, starting transfers between devices, per_device(): weight_parts = lax.all_to_all(weight_parts, following, 0, 0, tiled=True)  5.61 us
    pallas_call x3, Pallas kernels, fold(): pl.pallas_call(sum_kernel, out_shape=shape((copies, *parts.shape[1:]), F3...  4.73 us
  transfers between devices with their start and end apart: 7, of which 3 were waited for; matrix products, arithmetic and copies ran while one was open for 1% of the time, Pallas kernels for 5%

profile of v2, /device:TPU:1, one launch (start us, length us, event | category | flops | bytes accessed | tf_op | source)
XLA Modules:
  0.0 155.4 jit_solution(12292604988833471031)
XLA Ops:
  7.2 0.0 all-gather.2.cloned.1.call-start
  7.2 0.7 all-gather.2.cloned.1.call-update
  7.9 0.0 reduce-scatter.2.cloned.1.call-start
  7.9 1.8 %shard_map.103 = (bf16[64,256]{1,0:T(8,128)(2,1)}, bf16[64,256]{1,0:T(8,128)(2,1)}) custom-call(s32[2]{0:T(128)} %counts.3, s32[2,64]{1,0:T(2,128)} %send_lists.3, bf16[256,256]{1,0:T(8,128)(2,1)} %features.1), custom_call_target="tpu_custom_call" | custom-call | tf_op jit(solution)/shard_map/pallas_call | solution.py:182
  9.7 4.7 %collective-permute-start = (bf16[64,256]{1,0:T(8,128)(2,1)}, bf16[64,256]{1,0:T(8,128)(2,1)S(1)}, u32[]{:S(2)}, u32[]{:S(2)}) collective-permute-start(bf16[64,256]{1,0:T(8,128)(2,1)} %get-tuple-element.9), channel_id=1, source_target_pairs={{0,8},{8,16},{16,24},{24,32},{32,40},{40,48},{48,56},{56,64},{64,7... | collective-permute-start | bytes 98312 | tf_op jit(solution)/shard_map/ppermute | solution.py:188
  14.4 12.6 %collective-permute-start.1 = (bf16[64,256]{1,0:T(8,128)(2,1)}, bf16[64,256]{1,0:T(8,128)(2,1)S(1)}, u32[]{:S(2)}, u32[]{:S(2)}) collective-permute-start(bf16[64,256]{1,0:T(8,128)(2,1)} %get-tuple-element.10), channel_id=1, source_target_pairs={{8,0},{16,8},{24,16},{32,24},{40,32},{48,40},{56,48},{64,56},{72,6... | collective-permute-start | bytes 98312 | tf_op jit(solution)/shard_map/ppermute | solution.py:189
  27.1 0.0 collective-permute-done
  27.1 1.0 collective-permute-done.1
  28.1 22.3 %all_gather.7 = bf16[1024,256]{1,0:T(8,128)(2,1)} all-gather(bf16[128,256]{1,0:T(8,128)(2,1)S(1)} %pad_maximum_fusion), channel_id=1, replica_groups=mesh['z'=8,'y'=8,'c'=2,'x'=8] {'x'}, dimensions={0}, use_global_device_ids=true | all-gather | bytes 589824 | tf_op jit(solution)/shard_map/all_gather | solution.py:191
  50.4 13.6 %all-gather.2.cloned.1.call-done = bf16[2048,256]{1,0:T(8,128)(2,1)} async-done(((bf16[256,256]{1,0:T(8,128)(2,1)}), bf16[2048,256]{1,0:T(8,128)(2,1)}) %all-gather.2.cloned.1.call-update) | async-done | bytes 1048592 | tf_op jit(solution)/shard_map/all_gather | solution.py:190
  64.0 8.6 %shard_map.104 = (f32[16,24,128]{2,1,0:T(8,128)}, f32[24,176,128]{2,1,0:T(8,128)}) custom-call(s32[64]{0:T(128)} %rows.1, s32[64]{0:T(128)} %cols.1, bf16[64,128,128]{2,1,0:T(8,128)(2,1)} %tiles_hbm.1, bf16[8,2,128,256]{3,2,1,0:T(8,128)(2,1)} %bitcast.9, bf16[8,1,128,256]{3,2,1,0:T(8,128)(2,1)} %bitcast.8, bf16[172,256]{1,0:T(8,128)(2,1)} %bitcast.10, ...), custom_call_target="tpu_custom_call" | custom-call | tf_op jit(solution)/shard_map/pallas_call | solution.py:195
  72.6 0.0 copy-start.1
  72.6 0.0 reduce-scatter.2.cloned.1.call-update
  72.6 0.9 copy-done.1
  73.5 20.3 %all_to_all.20.parts = f32[16,24,128]{2,1,0:T(8,128)} all-to-all(f32[16,24,128]{2,1,0:T(8,128)S(1)} %copy-done.1), channel_id=1, replica_groups=mesh['z'=8,'y'=8,'c'=2,'x'=8] {'y','c'}, dimensions={0} | all-to-all | bytes 393216 | tf_op jit(solution)/shard_map/all_to_all | solution.py:228
  93.8 1.6 %shard_map.106 = f32[8,24,128]{2,1,0:T(8,128)} custom-call(f32[16,24,128]{2,1,0:T(8,128)} %all_to_all.20.parts), custom_call_target="tpu_custom_call" | custom-call | tf_op jit(solution)/shard_map/pallas_call | solution.py:221
  95.4 16.2 %all_to_all.21.parts = f32[8,24,128]{2,1,0:T(8,128)} all-to-all(f32[8,24,128]{2,1,0:T(8,128)} %shard_map.106), channel_id=1, replica_groups=mesh['z'=8,'y'=8,'c'=2,'x'=8] {'z'}, dimensions={0} | all-to-all | bytes 196608 | tf_op jit(solution)/shard_map/all_to_all | solution.py:232
  111.7 1.5 shard_map.107
  113.2 12.1 %all_to_all.22.parts = f32[8,24,128]{2,1,0:T(8,128)} all-to-all(f32[8,24,128]{2,1,0:T(8,128)} %shard_map.107), channel_id=1, replica_groups=mesh['z'=8,'y'=8,'c'=2,'x'=8] {'x'}, dimensions={0} | all-to-all | bytes 196608 | tf_op jit(solution)/shard_map/all_to_all | solution.py:232
  125.3 1.6 %shard_map.108 = f32[16,24,128]{2,1,0:T(8,128)} custom-call(f32[8,24,128]{2,1,0:T(8,128)} %all_to_all.22.parts), custom_call_target="tpu_custom_call" | custom-call | tf_op jit(solution)/shard_map/pallas_call | solution.py:221
  126.9 5.6 %all-to-all-start.3 = ((f32[16,24,128]{2,1,0:T(8,128)}), f32[16,24,128]{2,1,0:T(8,128)S(1)}, u32[]{:S(2)}, u32[]{:S(2)}) async-start(f32[16,24,128]{2,1,0:T(8,128)} %shard_map.108), calls=%async_computation.4 | async-start | bytes 393216 | tf_op jit(solution)/shard_map/all_to_all | solution.py:232
  132.5 0.0 reduce-scatter.2.cloned.1.call-done.own
  132.5 0.9 fusion
  133.4 2.1 %collective-permute-start.3 = (bf16[176,128]{1,0:T(8,128)(2,1)S(1)}, bf16[176,128]{1,0:T(8,128)(2,1)S(1)}, u32[]{:S(2)}, u32[]{:S(2)}) collective-permute-start(bf16[176,128]{1,0:T(8,128)(2,1)S(1)} %fusion), channel_id=1, source_target_pairs={{8,0},{16,8},{24,16},{32,24},{40,32},{48,40},{56,48},{64,56},{72,6... | collective-permute-start | bytes 135176 | tf_op jit(solution)/shard_map/ppermute | solution.py:236
  135.5 3.4 %collective-permute-start.2 = (bf16[176,128]{1,0:T(8,128)(2,1)S(1)}, bf16[176,128]{1,0:T(8,128)(2,1)S(1)}, u32[]{:S(2)}, u32[]{:S(2)}) collective-permute-start(bf16[176,128]{1,0:T(8,128)(2,1)S(1)} %fusion), channel_id=1, source_target_pairs={{0,8},{8,16},{16,24},{24,32},{32,40},{40,48},{48,56},{56,64},{64,7... | collective-permute-start | bytes 135176 | tf_op jit(solution)/shard_map/ppermute | solution.py:235
  139.0 3.9 %all-to-all-done.3.refs_0_ = f32[16,24,128]{2,1,0:T(8,128)S(1)} async-done(((f32[16,24,128]{2,1,0:T(8,128)}), f32[16,24,128]{2,1,0:T(8,128)S(1)}, u32[]{:S(2)}, u32[]{:S(2)}) %all-to-all-start.3) | async-done | bytes 196640 | tf_op jit(solution)/shard_map/all_to_all | solution.py:232
  142.9 0.0 copy-start
  142.9 0.7 copy-done
  143.5 1.6 %shard_map.109 = (f32[172,256]{1,0:T(8,128)}, f32[1,1]{1,0:T(1,128)}) custom-call(f32[16,24,128]{2,1,0:T(8,128)} %copy-done), custom_call_target="tpu_custom_call" | custom-call | tf_op jit(solution)/shard_map/pallas_call | solution.py:245
  145.1 0.0 collective-permute-done.3.after
  145.2 0.0 copy-start.2
  145.2 0.0 collective-permute-done.2.before
  145.2 0.6 copy-done.2
  145.8 0.0 copy-start.3
  145.8 0.6 copy-done.3
  146.4 2.2 %shard_map.105 = bf16[256,256]{1,0:T(8,128)(2,1)} custom-call(s32[2]{0:T(128)} %counts.3, s32[2,64]{1,0:T(2,128)} %send_lists.3, f32[3,176,128]{2,1,0:T(8,128)} %reduce-scatter.2.cloned.1.call-done.own, bf16[176,128]{1,0:T(8,128)(2,1)} %copy-done.3, bf16[176,128]{1,0:T(8,128)(2,1)} %copy-done.2, bf16[172,256]{1,0:T(8,128)(2,1)} %bitcast.11), custom_call_target="tpu_custom_call" | custom-call | tf_op jit(solution)/shard_map/pallas_call | solution.py:237
  (1 shorter events, 0.0 us)
Async XLA Ops:
  7.2 56.8 %all-gather.2.cloned.1.call-start = ((), (), s32[]{:S(2)}) async-start(), calls=%async_computation.5 | async-start | bytes 1179648 | tf_op jit(solution)/shard_map/all_gather | solution.py:190
  7.9 124.6 %reduce-scatter.2.cloned.1.call-start = ((), (), s32[]{:S(2)}) async-start(), calls=%async_computation.6 | async-start | bytes 2433024 | tf_op jit(solution)/shard_map/reduce_scatter | solution.py:229
  9.7 17.4 %collective-permute-start = (bf16[64,256]{1,0:T(8,128)(2,1)}, bf16[64,256]{1,0:T(8,128)(2,1)S(1)}, u32[]{:S(2)}, u32[]{:S(2)}) collective-permute-start(bf16[64,256]{1,0:T(8,128)(2,1)} %get-tuple-element.9), channel_id=1, source_target_pairs={{0,8},{8,16},{16,24},{24,32},{32,40},{40,48},{48,56},{56,64},{64,7... | collective-permute-start | bytes 98312 | tf_op jit(solution)/shard_map/ppermute | solution.py:188
  14.4 13.7 %collective-permute-start.1 = (bf16[64,256]{1,0:T(8,128)(2,1)}, bf16[64,256]{1,0:T(8,128)(2,1)S(1)}, u32[]{:S(2)}, u32[]{:S(2)}) collective-permute-start(bf16[64,256]{1,0:T(8,128)(2,1)} %get-tuple-element.10), channel_id=1, source_target_pairs={{8,0},{16,8},{24,16},{32,24},{40,32},{48,40},{56,48},{64,56},{72,6... | collective-permute-start | bytes 98312 | tf_op jit(solution)/shard_map/ppermute | solution.py:189
  72.6 0.9 copy-start.1
  126.9 16.0 %all-to-all-start.3 = ((f32[16,24,128]{2,1,0:T(8,128)}), f32[16,24,128]{2,1,0:T(8,128)S(1)}, u32[]{:S(2)}, u32[]{:S(2)}) async-start(f32[16,24,128]{2,1,0:T(8,128)} %shard_map.108), calls=%async_computation.4 | async-start | bytes 393216 | tf_op jit(solution)/shard_map/all_to_all | solution.py:232
  133.4 11.8 %collective-permute-start.3 = (bf16[176,128]{1,0:T(8,128)(2,1)S(1)}, bf16[176,128]{1,0:T(8,128)(2,1)S(1)}, u32[]{:S(2)}, u32[]{:S(2)}) collective-permute-start(bf16[176,128]{1,0:T(8,128)(2,1)S(1)} %fusion), channel_id=1, source_target_pairs={{8,0},{16,8},{24,16},{32,24},{40,32},{48,40},{56,48},{64,56},{72,6... | collective-permute-start | bytes 135176 | tf_op jit(solution)/shard_map/ppermute | solution.py:236
  135.5 9.6 %collective-permute-start.2 = (bf16[176,128]{1,0:T(8,128)(2,1)S(1)}, bf16[176,128]{1,0:T(8,128)(2,1)S(1)}, u32[]{:S(2)}, u32[]{:S(2)}) collective-permute-start(bf16[176,128]{1,0:T(8,128)(2,1)S(1)} %fusion), channel_id=1, source_target_pairs={{0,8},{8,16},{16,24},{24,32},{32,40},{40,48},{48,56},{56,64},{64,7... | collective-permute-start | bytes 135176 | tf_op jit(solution)/shard_map/ppermute | solution.py:235
  142.9 0.7 copy-start
  145.2 0.6 copy-start.2
  145.8 0.6 copy-start.3
Sparse Core Ops, SparseCore 0:
  10.7 53.2 all-gather.1
  72.7 45.8 reduce-scatter.1

commit v3 on v2

--- a/solution.py
+++ b/solution.py
@@ -8,7 +8,9 @@
 F32 = jnp.float32
 BF16 = jnp.bfloat16
 LANES = 128
-SHAPE = (8, 8, 2, 8)
+PIECE = 16
+SHAPE = (4, 2, 8, 2, 8)
+AXES = ("zh", "zl", "y", "c", "x")
 LAST = (((1,), (1,)), ((), ()))
 FIRST = (((0,), (0,)), ((), ()))
 PLAIN = (((1,), (0,)), ((), ()))
@@ -112,15 +114,12 @@
 
     weight_grad = dot(grad, high) + dot(grad, low)
     weight_grad = jnp.where(kind == classes, losses, weight_grad)
-    pieces, height = weight_out.shape[0] // 2, weight_out.shape[1]
-    weight_grad = jnp.concatenate(
-        [weight_grad, jnp.zeros((pieces * height - padded, hidden), F32)], axis=0
-    )
-    for half in range(2):
-        for q in range(pieces):
-            weight_out[pieces * half + q] = weight_grad[
-                q * height : (q + 1) * height, half * LANES : (half + 1) * LANES
-            ]
+    weight_grad = weight_grad.astype(BF16)
+    pieces = padded // PIECE
+    weight_out[2 * pieces :] = jnp.zeros_like(weight_out[2 * pieces :])
+    for i in range(2 * pieces):
+        row, lane = i % pieces * PIECE, i // pieces * LANES
+        weight_out[i] = weight_grad[row : row + PIECE, lane : lane + LANES]
 
     for start in range(0, count, 2):
         a, b = masked(start), masked(start + 1)
@@ -130,10 +129,8 @@
         grads[cols[start + 1]] += both[:, tile:]
 
 def sum_kernel(parts, out):
-    summed = parts[0]
-    for k in range(1, parts.shape[0]):
-        summed += parts[k]
-    out[...] = jnp.broadcast_to(summed[None], out.shape)
+    summed = jnp.sum(parts[...].astype(F32), axis=0, keepdims=True)
+    out[...] = jnp.broadcast_to(summed.astype(out.dtype), out.shape)
 
 
 def rows_kernel(counts, send_lists, own, before, after, weight, out):
@@ -150,10 +147,10 @@
 
 def last_kernel(scale, parts, weight_grad, loss):
     classes = weight_grad.shape[0]
-    pieces = parts.shape[0] // 2
+    pieces = round_up(classes + 1, PIECE) // PIECE
     gathered = jnp.concatenate(
         [
-            jnp.concatenate([parts[pieces * h + q] for q in range(pieces)], axis=0)
+            jnp.concatenate([parts[pieces * h + q].astype(F32) for q in range(pieces)], axis=0)
             for h in range(2)
         ],
         axis=1,
@@ -168,12 +165,11 @@
     send = send_lists.shape[1]
     count, tile = tiles.shape[0], tiles.shape[1]
     reps = lax.axis_size("x")
-    dom = ("z", "y", "c")
+    dom = AXES[:-1]
     domains = lax.axis_size(dom)
-    near = ("y", "c")
-    pieces = lax.axis_size(near)
-    padded = round_up(classes + 1, 16)
-    height = round_up(-(-padded // (pieces // 2)), 8)
+    near = ("zl", "y", "c")
+    far = ("zh", "x")
+    padded = round_up(classes + 1, PIECE)
     up = [(i, i + 1) for i in range(domains - 1)]
     down = [(i + 1, i) for i in range(domains - 1)]
     shape = jax.ShapeDtypeStruct
@@ -195,7 +191,7 @@
     weight_parts, parts = pl.pallas_call(
         layer_kernel,
         out_shape=(
-            shape((pieces, height, LANES), F32),
+            shape((lax.axis_size(near), PIECE, LANES), BF16),
             shape((3 * reps, padded, tile), F32),
         ),
         in_specs=[smem(), smem(), hbm(), hbm(), hbm(), vmem(), vmem()],
@@ -220,16 +216,18 @@
     def fold(parts, copies):
         return pl.pallas_call(
             sum_kernel,
-            out_shape=shape((copies, *parts.shape[1:]), F32),
+            out_shape=shape((copies, *parts.shape[1:]), BF16),
             in_specs=[vmem()],
             out_specs=vmem(),
+            compiler_params=params(4),
         )(parts)
 
+    own = lax.psum_scatter(parts, "x", scatter_dimension=0, tiled=True)
     weight_parts = lax.all_to_all(weight_parts, near, 0, 0, tiled=True)
-    own = lax.psum_scatter(parts, "x", scatter_dimension=0, tiled=True)
-    for axis, following in (("z", "z"), ("x", "x"), (near, near)):
-        weight_parts = fold(weight_parts, lax.axis_size(axis))
-        weight_parts = lax.all_to_all(weight_parts, following, 0, 0, tiled=True)
+    weight_parts = fold(weight_parts, lax.axis_size(far))
+    weight_parts = lax.all_to_all(weight_parts, far, 0, 0, tiled=True)
+    weight_parts = fold(weight_parts, lax.axis_size(near))
+    weight_parts = lax.all_to_all(weight_parts, near, 0, 0, tiled=True)
 
     halo = own[2].astype(BF16)
     before = lax.ppermute(halo, dom, up)
@@ -239,6 +237,7 @@
         out_shape=shape((nodes, hidden), BF16),
         in_specs=[smem()] + [vmem()] * 5,
         out_specs=vmem(),
+        compiler_params=params(4),
     )(counts, send_lists, own, before, after, weight)
 
     scale = 1.0 / (domains * reps * nodes)
@@ -247,13 +246,14 @@
         out_shape=(shape((classes, hidden), F32), shape((1, 1), F32)),
         in_specs=[vmem()],
         out_specs=(vmem(),) * 2,
+        compiler_params=params(4),
     )(weight_parts)
     return grad_features, weight_grad.T, loss.reshape(())
 
 
 def solution(mesh):
-    split = Mesh(mesh.devices.reshape(SHAPE), ("z", "y", "c", "x"))
-    both = ("z", "y", "c", "x")
+    split = Mesh(mesh.devices.reshape(SHAPE), AXES)
+    both = AXES
     placed = (
         P(both, None),
         P(),

time: 156 us -> 144 us (0.923)
  blocking collectives: 70.9 us -> 65.1 us
  Pallas kernels: 18.9 us -> 13.5 us
    all_to_all x2 -> x1, blocking collectives: 28.3 us -> 22.7 us  [per_device(): weight_parts = lax.all_to_all(weight_parts, far, 0, 0, tiled=True)]
    pallas_call x4 -> x3, Pallas kernels: 13.3 us -> 9.3 us  [the longest x1 8.56 us: per_device(): pl.pallas_call(layer_kernel, out_shape=(shape((lax.axis_size(near), PIECE...]
  transfers between devices with their start and end apart: 7 -> 7, of which waited for: 3 -> 3; matrix products, arithmetic and copies ran while one was open for 1% -> 1% of each run, Pallas kernels for 5% -> 2%
where the time goes in v3:
time: 144 us; the launch traced here: 143 us
  blocking collectives  65.1 us (45%)
  starting transfers between devices  30 us (21%)
  waiting for transfers between devices  17.8 us (12%)
  between operations  14.2 us (10%)
  Pallas kernels  13.5 us (9%)
  local copies, waits for them, and re-layouts  2.7 us (2%)
    all_to_all x1, blocking collectives, per_device(): weight_parts = lax.all_to_all(weight_parts, far, 0, 0, tiled=True)  22.7 us
    all_gather x1, blocking collectives, per_device(): lax.all_gather(jnp.concatenate([from_before, from_after], axis=0), 'x', a...  22.3 us
    all_to_all x1, blocking collectives, per_device(): weight_parts = lax.all_to_all(weight_parts, near, 0, 0, tiled=True)  20.1 us
    all_gather x1, waiting for transfers between devices, per_device(): own_rows = lax.all_gather(features, 'x', axis=0, tiled=True)  13.6 us
    ppermute x1, starting transfers between devices, per_device(): from_after = lax.ppermute(first, dom, down)  12.6 us
    pallas_call x1, Pallas kernels, per_device(): pl.pallas_call(layer_kernel, out_shape=(shape((lax.axis_size(near), PIECE...  8.56 us
    all_to_all x1, starting transfers between devices, per_device(): weight_parts = lax.all_to_all(weight_parts, near, 0, 0, tiled=True)  6.79 us
    ppermute x1, starting transfers between devices, per_device(): from_before = lax.ppermute(second, dom, up)  4.7 us
  transfers between devices with their start and end apart: 7, of which 3 were waited for; matrix products, arithmetic and copies ran while one was open for 1% of the time, Pallas kernels for 2%

profile of v3, /device:TPU:1, one launch (start us, length us, event | category | flops | bytes accessed | tf_op | source)
XLA Modules:
  0.0 143.2 jit_solution(16501721282456121447)
XLA Ops:
  7.2 0.0 all-gather.2.cloned.1.call-start
  7.2 0.7 all-gather.2.cloned.1.call-update
  7.9 0.0 reduce-scatter.2.cloned.1.call-start
  7.9 1.8 %shard_map.103 = (bf16[64,256]{1,0:T(8,128)(2,1)}, bf16[64,256]{1,0:T(8,128)(2,1)}) custom-call(s32[2]{0:T(128)} %counts.3, s32[2,64]{1,0:T(2,128)} %send_lists.3, bf16[256,256]{1,0:T(8,128)(2,1)} %features.1), custom_call_target="tpu_custom_call" | custom-call | tf_op jit(solution)/shard_map/pallas_call | solution.py:178
  9.7 4.7 %collective-permute-start = (bf16[64,256]{1,0:T(8,128)(2,1)}, bf16[64,256]{1,0:T(8,128)(2,1)S(1)}, u32[]{:S(2)}, u32[]{:S(2)}) collective-permute-start(bf16[64,256]{1,0:T(8,128)(2,1)} %get-tuple-element.9), channel_id=1, source_target_pairs={{0,8},{8,16},{16,24},{24,32},{32,40},{40,48},{48,56},{56,64},{64,7... | collective-permute-start | bytes 98312 | tf_op jit(solution)/shard_map/ppermute | solution.py:184
  14.4 12.6 %collective-permute-start.1 = (bf16[64,256]{1,0:T(8,128)(2,1)}, bf16[64,256]{1,0:T(8,128)(2,1)S(1)}, u32[]{:S(2)}, u32[]{:S(2)}) collective-permute-start(bf16[64,256]{1,0:T(8,128)(2,1)} %get-tuple-element.10), channel_id=1, source_target_pairs={{8,0},{16,8},{24,16},{32,24},{40,32},{48,40},{56,48},{64,56},{72,6... | collective-permute-start | bytes 98312 | tf_op jit(solution)/shard_map/ppermute | solution.py:185
  27.1 0.0 collective-permute-done
  27.1 1.0 collective-permute-done.1
  28.1 22.3 %all_gather.7 = bf16[1024,256]{1,0:T(8,128)(2,1)} all-gather(bf16[128,256]{1,0:T(8,128)(2,1)S(1)} %pad_maximum_fusion), channel_id=1, replica_groups=mesh['zh'=4,'zl'=2,'y'=8,'c'=2,'x'=8] {'x'}, dimensions={0}, use_global_device_ids=true | all-gather | bytes 589824 | tf_op jit(solution)/shard_map/all_gather | solution.py:187
  50.4 13.6 %all-gather.2.cloned.1.call-done = bf16[2048,256]{1,0:T(8,128)(2,1)} async-done(((bf16[256,256]{1,0:T(8,128)(2,1)}), bf16[2048,256]{1,0:T(8,128)(2,1)}) %all-gather.2.cloned.1.call-update) | async-done | bytes 1048592 | tf_op jit(solution)/shard_map/all_gather | solution.py:186
  64.0 8.6 %shard_map.104 = (bf16[32,16,128]{2,1,0:T(8,128)(2,1)}, f32[24,176,128]{2,1,0:T(8,128)}) custom-call(s32[64]{0:T(128)} %rows.1, s32[64]{0:T(128)} %cols.1, bf16[64,128,128]{2,1,0:T(8,128)(2,1)} %tiles_hbm.1, bf16[8,2,128,256]{3,2,1,0:T(8,128)(2,1)} %bitcast.11, bf16[8,1,128,256]{3,2,1,0:T(8,128)(2,1)} %bitcast.10, bf16[172,256]{1,0:T(8,128)(2,1)} %bitcast.8, ...), custom_call_target="tpu_custom_call" | custom-call | tf_op jit(solution)/shard_map/pallas_call | solution.py:191
  72.6 0.0 copy-start.4
  72.6 0.0 copy-start.1
  72.6 0.0 copy-start.2
  72.6 0.0 copy-start.3
  72.6 0.0 reduce-scatter.2.cloned.1.call-update
  72.6 0.8 copy-done.4
  73.5 20.1 %all_to_all.15.parts = bf16[32,16,128]{2,1,0:T(8,128)(2,1)S(1)} all-to-all(bf16[32,16,128]{2,1,0:T(8,128)(2,1)S(1)} %copy-done.4), channel_id=1, replica_groups=mesh['zh'=4,'zl'=2,'y'=8,'c'=2,'x'=8] {'zl','y','c'}, dimensions={0} | all-to-all | bytes 262144 | tf_op jit(solution)/shard_map/all_to_all | solution.py:226
  93.6 22.7 %all_to_all.16.parts = bf16[32,16,128]{2,1,0:T(8,128)(2,1)S(1)} all-to-all(bf16[32,16,128]{2,1,0:T(8,128)(2,1)S(1)} %shard_map.106), channel_id=1, replica_groups=mesh['zh'=4,'zl'=2,'y'=8,'c'=2,'x'=8] {'zh','x'}, dimensions={0} | all-to-all | bytes 262144 | tf_op jit(solution)/shard_map/all_to_all | solution.py:228
  116.3 0.7 shard_map.107
  117.0 6.8 %all-to-all-start.2 = ((bf16[32,16,128]{2,1,0:T(8,128)(2,1)}), bf16[32,16,128]{2,1,0:T(8,128)(2,1)S(1)}, u32[]{:S(2)}, u32[]{:S(2)}) async-start(bf16[32,16,128]{2,1,0:T(8,128)(2,1)} %shard_map.107), calls=%async_computation.3 | async-start | bytes 262144 | tf_op jit(solution)/shard_map/all_to_all | solution.py:230
  123.8 0.0 reduce-scatter.2.cloned.1.call-done.own
  123.8 0.9 fusion
  124.7 3.2 %collective-permute-start.3 = (bf16[176,128]{1,0:T(8,128)(2,1)S(1)}, bf16[176,128]{1,0:T(8,128)(2,1)S(1)}, u32[]{:S(2)}, u32[]{:S(2)}) collective-permute-start(bf16[176,128]{1,0:T(8,128)(2,1)S(1)} %fusion), channel_id=1, source_target_pairs={{8,0},{16,8},{24,16},{32,24},{40,32},{48,40},{56,48},{64,56},{72,6... | collective-permute-start | bytes 135176 | tf_op jit(solution)/shard_map/ppermute | solution.py:234
  128.0 2.6 %collective-permute-start.2 = (bf16[176,128]{1,0:T(8,128)(2,1)S(1)}, bf16[176,128]{1,0:T(8,128)(2,1)S(1)}, u32[]{:S(2)}, u32[]{:S(2)}) collective-permute-start(bf16[176,128]{1,0:T(8,128)(2,1)S(1)} %fusion), channel_id=1, source_target_pairs={{0,8},{8,16},{16,24},{24,32},{32,40},{40,48},{48,56},{56,64},{64,7... | collective-permute-start | bytes 135176 | tf_op jit(solution)/shard_map/ppermute | solution.py:233
  130.5 2.4 %all-to-all-done.2.refs_0_ = bf16[32,16,128]{2,1,0:T(8,128)(2,1)S(1)} async-done(((bf16[32,16,128]{2,1,0:T(8,128)(2,1)}), bf16[32,16,128]{2,1,0:T(8,128)(2,1)S(1)}, u32[]{:S(2)}, u32[]{:S(2)}) %all-to-all-start.2) | async-done | bytes 131104 | tf_op jit(solution)/shard_map/all_to_all | solution.py:230
  133.0 0.7 shard_map.108
  133.7 0.0 collective-permute-done.3.after
  133.7 0.0 collective-permute-done.2.before
  133.7 0.0 copy-done.1
  133.7 0.0 copy-done.2
  133.7 0.0 copy-done.3
  133.7 0.0 copy-start
  133.7 0.9 copy-done
  134.6 1.7 %shard_map.105 = bf16[256,256]{1,0:T(8,128)(2,1)} custom-call(s32[2]{0:T(128)S(1)} %copy-done.3, s32[2,64]{1,0:T(2,128)S(1)} %copy-done.2, f32[3,176,128]{2,1,0:T(8,128)S(1)} %copy-done, bf16[176,128]{1,0:T(8,128)(2,1)S(1)} %collective-permute-done.2.before, bf16[176,128]{1,0:T(8,128)(2,1)S(1)} %collective-permute-done.3.after, bf16[172,256]{1,0:T(8,128)(2,1)S(1)} %bitcast.9), custom_call_target="tpu_custom_call" | custom-call | tf_op jit(solution)/shard_map/pallas_call | solution.py:235
  (2 shorter events, 0.0 us)
Async XLA Ops:
  7.2 56.8 %all-gather.2.cloned.1.call-start = ((), (), s32[]{:S(2)}) async-start(), calls=%async_computation.4 | async-start | bytes 1179648 | tf_op jit(solution)/shard_map/all_gather | solution.py:186
  7.9 115.9 %reduce-scatter.2.cloned.1.call-start = ((), (), s32[]{:S(2)}) async-start(), calls=%async_computation.5 | async-start | bytes 2433024 | tf_op jit(solution)/shard_map/reduce_scatter | solution.py:225
  9.7 17.4 %collective-permute-start = (bf16[64,256]{1,0:T(8,128)(2,1)}, bf16[64,256]{1,0:T(8,128)(2,1)S(1)}, u32[]{:S(2)}, u32[]{:S(2)}) collective-permute-start(bf16[64,256]{1,0:T(8,128)(2,1)} %get-tuple-element.9), channel_id=1, source_target_pairs={{0,8},{8,16},{16,24},{24,32},{32,40},{40,48},{48,56},{56,64},{64,7... | collective-permute-start | bytes 98312 | tf_op jit(solution)/shard_map/ppermute | solution.py:184
  14.4 13.7 %collective-permute-start.1 = (bf16[64,256]{1,0:T(8,128)(2,1)}, bf16[64,256]{1,0:T(8,128)(2,1)S(1)}, u32[]{:S(2)}, u32[]{:S(2)}) collective-permute-start(bf16[64,256]{1,0:T(8,128)(2,1)} %get-tuple-element.10), channel_id=1, source_target_pairs={{8,0},{16,8},{24,16},{32,24},{40,32},{48,40},{56,48},{64,56},{72,6... | collective-permute-start | bytes 98312 | tf_op jit(solution)/shard_map/ppermute | solution.py:185
  72.6 0.9 copy-start.4
  72.6 61.1 %copy-start.1 = (bf16[256,172]{0,1:T(8,128)(2,1)S(1)}, bf16[256,172]{0,1:T(8,128)(2,1)}, u32[]{:S(2)}) copy-start(bf16[256,172]{0,1:T(8,128)(2,1)} %param.9) | copy-start | bytes 264196
  72.6 61.1 %copy-start.2 = (s32[2,64]{1,0:T(2,128)S(1)}, s32[2,64]{1,0:T(2,128)}, u32[]{:S(2)}) copy-start(s32[2,64]{1,0:T(2,128)} %send_lists.3) | copy-start | bytes 1540
  72.6 61.1 %copy-start.3 = (s32[2]{0:T(128)S(1)}, s32[2]{0:T(128)}, u32[]{:S(2)}) copy-start(s32[2]{0:T(128)} %counts.3) | copy-start | bytes 28
  117.0 16.0 %all-to-all-start.2 = ((bf16[32,16,128]{2,1,0:T(8,128)(2,1)}), bf16[32,16,128]{2,1,0:T(8,128)(2,1)S(1)}, u32[]{:S(2)}, u32[]{:S(2)}) async-start(bf16[32,16,128]{2,1,0:T(8,128)(2,1)} %shard_map.107), calls=%async_computation.3 | async-start | bytes 262144 | tf_op jit(solution)/shard_map/all_to_all | solution.py:230
  124.7 8.9 %collective-permute-start.3 = (bf16[176,128]{1,0:T(8,128)(2,1)S(1)}, bf16[176,128]{1,0:T(8,128)(2,1)S(1)}, u32[]{:S(2)}, u32[]{:S(2)}) collective-permute-start(bf16[176,128]{1,0:T(8,128)(2,1)S(1)} %fusion), channel_id=1, source_target_pairs={{8,0},{16,8},{24,16},{32,24},{40,32},{48,40},{56,48},{64,56},{72,6... | collective-permute-start | bytes 135176 | tf_op jit(solution)/shard_map/ppermute | solution.py:234
  128.0 5.7 %collective-permute-start.2 = (bf16[176,128]{1,0:T(8,128)(2,1)S(1)}, bf16[176,128]{1,0:T(8,128)(2,1)S(1)}, u32[]{:S(2)}, u32[]{:S(2)}) collective-permute-start(bf16[176,128]{1,0:T(8,128)(2,1)S(1)} %fusion), channel_id=1, source_target_pairs={{0,8},{8,16},{16,24},{24,32},{32,40},{40,48},{48,56},{56,64},{64,7... | collective-permute-start | bytes 135176 | tf_op jit(solution)/shard_map/ppermute | solution.py:233
  133.7 1.0 copy-start
Sparse Core Ops, SparseCore 0:
  10.7 53.2 all-gather.1
  72.8 47.6 reduce-scatter.1

commit v4 on v3

--- a/solution.py
+++ b/solution.py
@@ -9,6 +9,7 @@
 BF16 = jnp.bfloat16
 LANES = 128
 PIECE = 16
+EARLY = 192
 SHAPE = (4, 2, 8, 2, 8)
 AXES = ("zh", "zl", "y", "c", "x")
 LAST = (((1,), (1,)), ((), ()))
@@ -58,18 +59,19 @@
 
 
 def layer_kernel(
-    rows, cols, tiles_hbm, own_hbm, halo_hbm, weight, labels,
-    weight_out, grads,
-    tiles, columns, sums, sems,
+    rows, cols, tiles_hbm, own_hbm, rest_hbm, weight, labels,
+    weight_out, out,
+    tiles, columns, sums, grads, sems,
 ):
     count, tile = tiles.shape[0], tiles.shape[1]
     classes, hidden = weight.shape
     padded = grads.shape[1]
     nodes = labels.shape[1]
+    early = own_hbm.shape[1]
     group = 4
     copies = [
-        pltpu.make_async_copy(own_hbm, columns.at[:, 0:2], sems.at[0]),
-        pltpu.make_async_copy(halo_hbm, columns.at[:, 2:3], sems.at[1]),
+        pltpu.make_async_copy(own_hbm, columns.at[:, :early], sems.at[0]),
+        pltpu.make_async_copy(rest_hbm, columns.at[:, early:], sems.at[1]),
         pltpu.make_async_copy(tiles_hbm, tiles, sems.at[2]),
     ]
     for copy in copies:
@@ -83,7 +85,8 @@
 
     def column(t):
         member = cols[t] // 3
-        return columns[member, cols[t] - 3 * member]
+        start = pl.multiple_of((cols[t] - 3 * member) * tile, tile)
+        return columns[member, pl.ds(start, tile), :]
 
     sums[...] = jnp.zeros_like(sums)
     grads[...] = jnp.zeros_like(grads)
@@ -127,10 +130,29 @@
         both = dot(grad, right)
         grads[cols[start]] += both[:, :tile]
         grads[cols[start + 1]] += both[:, tile:]
+    for r in range(out.shape[0]):
+        for j in range(3):
+            out[r, j * padded : (j + 1) * padded, :] = grads[3 * r + j].astype(BF16)
+
+
+def layer_scratch(reps, nodes, hidden, count, tile, padded):
+    return [
+        pltpu.VMEM((count, tile, tile), BF16),
+        pltpu.VMEM((reps, 3 * tile, hidden), BF16),
+        pltpu.VMEM((nodes, hidden), F32),
+        pltpu.VMEM((3 * reps, padded, tile), F32),
+        pltpu.SemaphoreType.DMA((3,)),
+    ]
+
+
+def fold_kernel(parts, own, halo):
+    padded = halo.shape[0]
+    summed = jnp.sum(parts[...].astype(F32), axis=0)
+    own[...] = summed[: 2 * padded]
+    halo[...] = summed[2 * padded :].astype(BF16)
 
 def sum_kernel(parts, out):
-    summed = jnp.sum(parts[...].astype(F32), axis=0, keepdims=True)
-    out[...] = jnp.broadcast_to(summed.astype(out.dtype), out.shape)
+    out[...] = jnp.sum(parts[...].astype(F32), axis=0)
 
 
 def rows_kernel(counts, send_lists, own, before, after, weight, out):
@@ -138,7 +160,7 @@
     classes = weight.shape[0]
     first, second = slots_onehot(counts, send_lists, out.shape[0])
     send = send_lists.shape[1]
-    total = jnp.concatenate([own[0], own[1]], axis=1)
+    total = jnp.concatenate([own[:padded], own[padded:]], axis=1)
     total += dot(before[:, send:], first, LAST)
     total += dot(after[:, :send], second, LAST)
     grad = total[:classes].astype(BF16)
@@ -167,8 +189,7 @@
     reps = lax.axis_size("x")
     dom = AXES[:-1]
     domains = lax.axis_size(dom)
-    near = ("zl", "y", "c")
-    far = ("zh", "x")
+    near = ("zl", "c", "x")
     padded = round_up(classes + 1, PIECE)
     up = [(i, i + 1) for i in range(domains - 1)]
     down = [(i + 1, i) for i in range(domains - 1)]
@@ -183,53 +204,45 @@
     )(counts, send_lists, features)
     from_before = lax.ppermute(second, dom, up)
     from_after = lax.ppermute(first, dom, down)
-    own_rows = lax.all_gather(features, "x", axis=0, tiled=True)
-    halo_rows = lax.all_gather(
-        jnp.concatenate([from_before, from_after], axis=0), "x", axis=0, tiled=True
-    )
+    own_rows = lax.all_to_all(
+        jnp.broadcast_to(features[:EARLY][None], (reps, EARLY, hidden)), "x", 0, 0, tiled=True
+    )
+    rest = jnp.concatenate([features[EARLY:], from_before, from_after], axis=0)
+    rest_rows = lax.all_gather(rest, "x", axis=0)
 
     weight_parts, parts = pl.pallas_call(
         layer_kernel,
         out_shape=(
             shape((lax.axis_size(near), PIECE, LANES), BF16),
-            shape((3 * reps, padded, tile), F32),
+            shape((reps, 3 * padded, LANES), BF16),
         ),
         in_specs=[smem(), smem(), hbm(), hbm(), hbm(), vmem(), vmem()],
         out_specs=(vmem(),) * 2,
-        scratch_shapes=[
-            pltpu.VMEM((count, tile, tile), BF16),
-            pltpu.VMEM((reps, 3, tile, hidden), BF16),
-            pltpu.VMEM((nodes, hidden), F32),
-            pltpu.SemaphoreType.DMA((3,)),
-        ],
+        scratch_shapes=layer_scratch(reps, nodes, hidden, count, tile, padded),
         compiler_params=params(56),
-    )(
-        tile_rows,
-        tile_cols,
-        tiles,
-        own_rows.reshape(reps, 2, tile, hidden),
-        halo_rows.reshape(reps, 1, tile, hidden),
-        weight,
-        labels.reshape(1, nodes),
-    )
-
-    def fold(parts, copies):
-        return pl.pallas_call(
-            sum_kernel,
-            out_shape=shape((copies, *parts.shape[1:]), BF16),
-            in_specs=[vmem()],
-            out_specs=vmem(),
-            compiler_params=params(4),
-        )(parts)
-
-    own = lax.psum_scatter(parts, "x", scatter_dimension=0, tiled=True)
+    )(tile_rows, tile_cols, tiles, own_rows, rest_rows, weight, labels.reshape(1, nodes))
+
     weight_parts = lax.all_to_all(weight_parts, near, 0, 0, tiled=True)
-    weight_parts = fold(weight_parts, lax.axis_size(far))
-    weight_parts = lax.all_to_all(weight_parts, far, 0, 0, tiled=True)
-    weight_parts = fold(weight_parts, lax.axis_size(near))
-    weight_parts = lax.all_to_all(weight_parts, near, 0, 0, tiled=True)
-
-    halo = own[2].astype(BF16)
+    weight_part = pl.pallas_call(
+        sum_kernel,
+        out_shape=shape(weight_parts.shape[1:], F32),
+        in_specs=[vmem()],
+        out_specs=vmem(),
+        compiler_params=params(4),
+    )(weight_parts)
+    weight_part, parts = lax.optimization_barrier((weight_part, parts))
+    parts = lax.all_to_all(parts, "x", 0, 0, tiled=True)
+    weight_part = lax.psum(lax.psum(weight_part, "y"), "zh").astype(BF16)
+    copies = jnp.broadcast_to(weight_part[None], weight_parts.shape)
+    weight_parts = lax.all_to_all(copies, near, 0, 0, tiled=True)
+
+    own, halo = pl.pallas_call(
+        fold_kernel,
+        out_shape=(shape((2 * padded, LANES), F32), shape((padded, LANES), BF16)),
+        in_specs=[vmem()],
+        out_specs=(vmem(),) * 2,
+        compiler_params=params(8),
+    )(parts)
     before = lax.ppermute(halo, dom, up)
     after = lax.ppermute(halo, dom, down)
     grad_features = pl.pallas_call(

time: 144 us -> 149 us (1.035)
  blocking collectives: 65.1 us -> 82.9 us
  starting transfers between devices: 30 us -> 43.7 us
  between operations: 14.2 us -> 0.78 us
  waiting for transfers between devices: 17.8 us -> 5 us
    psum x0 -> x2, blocking collectives: none -> 37.6 us  [per_device(): weight_part = lax.psum(lax.psum(weight_part, 'y'), 'zh').astype(BF16)]
    all_to_all x1 -> x0, blocking collectives: 22.7 us -> none  [per_device(): weight_parts = lax.all_to_all(weight_parts, far, 0, 0, tiled=True)]
    all_to_all x1 -> x3, starting transfers between devices: 6.79 us -> 24.1 us  [the longest x1 13.1 us: per_device(): weight_parts = lax.all_to_all(copies, near, 0, 0, tiled=True)]
    all_gather x1 -> x0, waiting for transfers between devices: 13.6 us -> none  [per_device(): own_rows = lax.all_gather(features, 'x', axis=0, tiled=True)]
    all_gather x1, blocking collectives: 22.3 us -> 25.7 us  [per_device(): rest_rows = lax.all_gather(rest, 'x', axis=0)]
    ppermute x1, starting transfers between devices: 12.6 us -> 9.94 us  [per_device(): from_after = lax.ppermute(first, dom, down)]
    broadcast_in_dim x0 -> x2, local copies, waits for them, and re-layouts: none -> 1.64 us  [the longest x1 0.96 us: per_device(): jnp.broadcast_to(features[:EARLY][None], (reps, EARLY, hidden))]
    all_to_all x1 -> x3, waiting for transfers between devices: 2.43 us -> 3.96 us  [the longest x1 3.95 us: per_device(): weight_parts = lax.all_to_all(copies, near, 0, 0, tiled=True)]
  transfers between devices with their start and end apart: 7 -> 7, of which waited for: 3 -> 2; matrix products, arithmetic and copies ran while one was open for 1% -> 0% of each run, Pallas kernels for 2% -> 2%
where the time goes in v4:
time: 149 us
  blocking collectives  82.9 us (56%)
  starting transfers between devices  43.7 us (29%)
  Pallas kernels  12.6 us (8%)
  waiting for transfers between devices  5 us (3%)
  local copies, waits for them, and re-layouts  3.49 us (2%)
    psum x2, blocking collectives, per_device(): weight_part = lax.psum(lax.psum(weight_part, 'y'), 'zh').astype(BF16)  37.6 us
    all_gather x1, blocking collectives, per_device(): rest_rows = lax.all_gather(rest, 'x', axis=0)  25.7 us
    all_to_all x1, blocking collectives, per_device(): weight_parts = lax.all_to_all(weight_parts, near, 0, 0, tiled=True)  19.6 us
    all_to_all x1, starting transfers between devices, per_device(): weight_parts = lax.all_to_all(copies, near, 0, 0, tiled=True)  13.1 us
    ppermute x1, starting transfers between devices, per_device(): from_after = lax.ppermute(first, dom, down)  9.94 us
    pallas_call x1, Pallas kernels, per_device(): pl.pallas_call(layer_kernel, out_shape=(shape((lax.axis_size(near), PIECE...  8.28 us
    all_to_all x1, starting transfers between devices, per_device(): lax.all_to_all(jnp.broadcast_to(features[:EARLY][None], (reps, EARLY, hid...  7.44 us
    ppermute x1, starting transfers between devices, per_device(): from_before = lax.ppermute(second, dom, up)  4.14 us
  transfers between devices with their start and end apart: 7, of which 2 were waited for; matrix products, arithmetic and copies ran while one was open for 0% of the time, Pallas kernels for 2%

profile of v4, /device:TPU:1, one launch (start us, length us, event | category | flops | bytes accessed | tf_op | source)
XLA Modules:
  0.0 148.5 jit_solution(17126521347234371235)
XLA Ops:
  0.6 0.9 slice.6
  1.5 1.0 broadcast_in_dim.4
  2.5 0.0 slice-start
  2.5 7.4 %all-to-all-start = ((bf16[8,192,256]{2,1,0:T(8,128)(2,1)}), bf16[8,192,256]{2,1,0:T(8,128)(2,1)S(1)}, u32[]{:S(2)}, u32[]{:S(2)}) async-start(bf16[8,192,256]{2,1,0:T(8,128)(2,1)} %broadcast_in_dim.4), calls=%async_computation | async-start | bytes 1572864 | tf_op jit(solution)/shard_map/all_to_all | solution.py:207
  9.9 1.8 %shard_map.103 = (bf16[64,256]{1,0:T(8,128)(2,1)}, bf16[64,256]{1,0:T(8,128)(2,1)}) custom-call(s32[2]{0:T(128)} %counts.3, s32[2,64]{1,0:T(2,128)} %send_lists.3, bf16[256,256]{1,0:T(8,128)(2,1)} %features.1), custom_call_target="tpu_custom_call" | custom-call | tf_op jit(solution)/shard_map/pallas_call | solution.py:199
  11.7 4.1 %collective-permute-start = (bf16[64,256]{1,0:T(8,128)(2,1)}, bf16[64,256]{1,0:T(8,128)(2,1)S(1)}, u32[]{:S(2)}, u32[]{:S(2)}) collective-permute-start(bf16[64,256]{1,0:T(8,128)(2,1)} %get-tuple-element.13), channel_id=1, source_target_pairs={{0,8},{8,16},{16,24},{24,32},{32,40},{40,48},{48,56},{56,64},{64,7... | collective-permute-start | bytes 98312 | tf_op jit(solution)/shard_map/ppermute | solution.py:205
  15.9 9.9 %collective-permute-start.1 = (bf16[64,256]{1,0:T(8,128)(2,1)}, bf16[64,256]{1,0:T(8,128)(2,1)S(1)}, u32[]{:S(2)}, u32[]{:S(2)}) collective-permute-start(bf16[64,256]{1,0:T(8,128)(2,1)} %get-tuple-element.14), channel_id=1, source_target_pairs={{8,0},{16,8},{24,16},{32,24},{40,32},{48,40},{56,48},{64,56},{72,6... | collective-permute-start | bytes 98312 | tf_op jit(solution)/shard_map/ppermute | solution.py:206
  25.8 0.0 collective-permute-done
  25.8 1.0 collective-permute-done.1
  26.9 0.0 slice-done
  26.9 25.7 %all-gather = bf16[1536,256]{1,0:T(8,128)(2,1)} all-gather(bf16[192,256]{1,0:T(8,128)(2,1)S(1)} %pad_maximum_fusion), channel_id=2, replica_groups=mesh['zh'=4,'zl'=2,'y'=8,'c'=2,'x'=8] {'x'}, dimensions={0}, use_global_device_ids=true | all-gather | bytes 884736 | tf_op jit(solution)/shard_map/all_gather | solution.py:211
  52.6 0.0 all-to-all-done.own_hbm
  52.6 0.0 copy-start.3
  52.6 0.9 copy-done.3
  53.5 8.3 %shard_map.104 = (bf16[32,16,128]{2,1,0:T(8,128)(2,1)}, bf16[8,528,128]{2,1,0:T(8,128)(2,1)}) custom-call(s32[64]{0:T(128)} %rows.1, s32[64]{0:T(128)} %cols.1, bf16[64,128,128]{2,1,0:T(8,128)(2,1)} %tiles_hbm.1, bf16[8,192,256]{2,1,0:T(8,128)(2,1)} %copy-done.3, bf16[8,192,256]{2,1,0:T(8,128)(2,1)} %bitcast.7, bf16[172,256]{1,0:T(8,128)(2,1)} %bitcast.5, ...), custom_call_target="tpu_custom_call" | custom-call | tf_op jit(solution)/shard_map/pallas_call | solution.py:213
  61.8 19.6 %all_to_all.20.parts = bf16[32,16,128]{2,1,0:T(8,128)(2,1)S(1)} all-to-all(bf16[32,16,128]{2,1,0:T(8,128)(2,1)} %get-tuple-element.15), channel_id=1, replica_groups=mesh['zh'=4,'zl'=2,'y'=8,'c'=2,'x'=8] {'zl','c','x'}, dimensions={0} | all-to-all | bytes 262144 | tf_op jit(solution)/shard_map/all_to_all | solution.py:225
  81.4 3.6 %all-to-all-start.2 = ((bf16[8,528,128]{2,1,0:T(8,128)(2,1)}), bf16[8,528,128]{2,1,0:T(8,128)(2,1)S(1)}, u32[]{:S(2)}, u32[]{:S(2)}) async-start(bf16[8,528,128]{2,1,0:T(8,128)(2,1)} %get-tuple-element.17), calls=%async_computation.2 | async-start | bytes 2162688 | tf_op jit(solution)/shard_map/all_to_all | solution.py:234
  85.0 0.0 copy-start
  85.0 0.0 copy-start.1
  85.0 0.0 copy-start.2
  85.0 15.3 %psum.14 = f32[16,128]{1,0:T(8,128)S(1)} all-reduce(f32[16,128]{1,0:T(8,128)S(1)} %shard_map.105), channel_id=1, replica_groups=mesh['zh'=4,'zl'=2,'y'=8,'c'=2,'x'=8] {'y'}, use_global_device_ids=true, to_apply=%region_0.0 | all-reduce | flops 2048 | bytes 16384 | tf_op jit(solution)/shard_map/psum | solution.py:235
  100.3 22.3 %psum.15 = bf16[16,128]{1,0:T(8,128)(2,1)S(1)} all-reduce(f32[16,128]{1,0:T(8,128)S(1)} %psum.14), channel_id=1, replica_groups=mesh['zh'=4,'zl'=2,'y'=8,'c'=2,'x'=8] {'zh'}, use_global_device_ids=true, to_apply=%region_1.0 | all-reduce | flops 2048 | bytes 12288 | tf_op jit(solution)/shard_map/psum | solution.py:235
  122.6 0.0 all-to-all-done.2.parts
  122.6 0.7 broadcast_in_dim.5
  123.3 13.1 %all-to-all-start.3 = ((bf16[32,16,128]{2,1,0:T(8,128)(2,1)}), bf16[32,16,128]{2,1,0:T(8,128)(2,1)S(1)}, u32[]{:S(2)}, u32[]{:S(2)}) async-start(bf16[32,16,128]{2,1,0:T(8,128)(2,1)} %broadcast_in_dim.5), calls=%async_computation.3 | async-start | bytes 262144 | tf_op jit(solution)/shard_map/all_to_all | solution.py:237
  136.4 0.1 shard_map.106
  136.6 2.1 %collective-permute-start.3 = (bf16[176,128]{1,0:T(8,128)(2,1)S(1)}, bf16[176,128]{1,0:T(8,128)(2,1)S(1)}, u32[]{:S(2)}, u32[]{:S(2)}) collective-permute-start(bf16[176,128]{1,0:T(8,128)(2,1)S(1)} %get-tuple-element.19), channel_id=1, source_target_pairs={{8,0},{16,8},{24,16},{32,24},{40,32},{48,40},{56,48},{64,56},{72,6... | collective-permute-start | bytes 135176 | tf_op jit(solution)/shard_map/ppermute | solution.py:247
  138.7 3.4 %collective-permute-start.2 = (bf16[176,128]{1,0:T(8,128)(2,1)S(1)}, bf16[176,128]{1,0:T(8,128)(2,1)S(1)}, u32[]{:S(2)}, u32[]{:S(2)}) collective-permute-start(bf16[176,128]{1,0:T(8,128)(2,1)S(1)} %get-tuple-element.19), channel_id=1, source_target_pairs={{0,8},{8,16},{16,24},{24,32},{32,40},{40,48},{48,56},{56,64},{64,7... | collective-permute-start | bytes 135176 | tf_op jit(solution)/shard_map/ppermute | solution.py:246
  142.1 4.0 %all-to-all-done.3.refs_0_ = bf16[32,16,128]{2,1,0:T(8,128)(2,1)S(1)} async-done(((bf16[32,16,128]{2,1,0:T(8,128)(2,1)}), bf16[32,16,128]{2,1,0:T(8,128)(2,1)S(1)}, u32[]{:S(2)}, u32[]{:S(2)}) %all-to-all-start.3) | async-done | bytes 131104 | tf_op jit(solution)/shard_map/all_to_all | solution.py:237
  146.1 0.7 shard_map.108
  146.8 0.0 collective-permute-done.3.after
  146.8 0.0 collective-permute-done.2.before
  146.8 0.0 copy-done
  146.8 0.0 copy-done.1
  146.8 0.0 copy-done.2
  146.8 1.7 %shard_map.107 = bf16[256,256]{1,0:T(8,128)(2,1)} custom-call(s32[2]{0:T(128)S(1)} %copy-done.2, s32[2,64]{1,0:T(2,128)S(1)} %copy-done.1, f32[352,128]{1,0:T(8,128)S(1)} %get-tuple-element.18.own, bf16[176,128]{1,0:T(8,128)(2,1)S(1)} %collective-permute-done.2.before, bf16[176,128]{1,0:T(8,128)(2,1)S(1)} %collective-permute-done.3.after, ...), custom_call_target="tpu_custom_call" | custom-call | tf_op jit(solution)/shard_map/pallas_call | solution.py:248
  (2 shorter events, 0.0 us)
Async XLA Ops:
  2.5 24.4 %slice-start = ((bf16[256,256]{1,0:T(8,128)(2,1)}), bf16[64,256]{1,0:T(8,128)(2,1)S(1)}, s32[]{:S(2)}) async-start(bf16[256,256]{1,0:T(8,128)(2,1)} %features.1), calls=%async_computation.4 | async-start | bytes 65536 | tf_op jit(solution)/shard_map/slice | solution.py:210
  2.5 50.1 %all-to-all-start = ((bf16[8,192,256]{2,1,0:T(8,128)(2,1)}), bf16[8,192,256]{2,1,0:T(8,128)(2,1)S(1)}, u32[]{:S(2)}, u32[]{:S(2)}) async-start(bf16[8,192,256]{2,1,0:T(8,128)(2,1)} %broadcast_in_dim.4), calls=%async_computation | async-start | bytes 1572864 | tf_op jit(solution)/shard_map/all_to_all | solution.py:207
  11.7 14.1 %collective-permute-start = (bf16[64,256]{1,0:T(8,128)(2,1)}, bf16[64,256]{1,0:T(8,128)(2,1)S(1)}, u32[]{:S(2)}, u32[]{:S(2)}) collective-permute-start(bf16[64,256]{1,0:T(8,128)(2,1)} %get-tuple-element.13), channel_id=1, source_target_pairs={{0,8},{8,16},{16,24},{24,32},{32,40},{40,48},{48,56},{56,64},{64,7... | collective-permute-start | bytes 98312 | tf_op jit(solution)/shard_map/ppermute | solution.py:205
  15.9 11.0 %collective-permute-start.1 = (bf16[64,256]{1,0:T(8,128)(2,1)}, bf16[64,256]{1,0:T(8,128)(2,1)S(1)}, u32[]{:S(2)}, u32[]{:S(2)}) collective-permute-start(bf16[64,256]{1,0:T(8,128)(2,1)} %get-tuple-element.14), channel_id=1, source_target_pairs={{8,0},{16,8},{24,16},{32,24},{40,32},{48,40},{56,48},{64,56},{72,6... | collective-permute-start | bytes 98312 | tf_op jit(solution)/shard_map/ppermute | solution.py:206
  52.6 0.9 copy-start.3
  81.4 41.2 %all-to-all-start.2 = ((bf16[8,528,128]{2,1,0:T(8,128)(2,1)}), bf16[8,528,128]{2,1,0:T(8,128)(2,1)S(1)}, u32[]{:S(2)}, u32[]{:S(2)}) async-start(bf16[8,528,128]{2,1,0:T(8,128)(2,1)} %get-tuple-element.17), calls=%async_computation.2 | async-start | bytes 2162688 | tf_op jit(solution)/shard_map/all_to_all | solution.py:234
  85.0 61.8 %copy-start = (bf16[256,172]{0,1:T(8,128)(2,1)S(1)}, bf16[256,172]{0,1:T(8,128)(2,1)}, u32[]{:S(2)}) copy-start(bf16[256,172]{0,1:T(8,128)(2,1)} %param.9) | copy-start | bytes 264196
  85.0 61.8 %copy-start.1 = (s32[2,64]{1,0:T(2,128)S(1)}, s32[2,64]{1,0:T(2,128)}, u32[]{:S(2)}) copy-start(s32[2,64]{1,0:T(2,128)} %send_lists.3) | copy-start | bytes 1540
  85.0 61.8 %copy-start.2 = (s32[2]{0:T(128)S(1)}, s32[2]{0:T(128)}, u32[]{:S(2)}) copy-start(s32[2]{0:T(128)} %counts.3) | copy-start | bytes 28
  123.3 22.8 %all-to-all-start.3 = ((bf16[32,16,128]{2,1,0:T(8,128)(2,1)}), bf16[32,16,128]{2,1,0:T(8,128)(2,1)S(1)}, u32[]{:S(2)}, u32[]{:S(2)}) async-start(bf16[32,16,128]{2,1,0:T(8,128)(2,1)} %broadcast_in_dim.5), calls=%async_computation.3 | async-start | bytes 262144 | tf_op jit(solution)/shard_map/all_to_all | solution.py:237
  136.6 10.2 %collective-permute-start.3 = (bf16[176,128]{1,0:T(8,128)(2,1)S(1)}, bf16[176,128]{1,0:T(8,128)(2,1)S(1)}, u32[]{:S(2)}, u32[]{:S(2)}) collective-permute-start(bf16[176,128]{1,0:T(8,128)(2,1)S(1)} %get-tuple-element.19), channel_id=1, source_target_pairs={{8,0},{16,8},{24,16},{32,24},{40,32},{48,40},{56,48},{64,56},{72,6... | collective-permute-start | bytes 135176 | tf_op jit(solution)/shard_map/ppermute | solution.py:247
  138.7 8.1 %collective-permute-start.2 = (bf16[176,128]{1,0:T(8,128)(2,1)S(1)}, bf16[176,128]{1,0:T(8,128)(2,1)S(1)}, u32[]{:S(2)}, u32[]{:S(2)}) collective-permute-start(bf16[176,128]{1,0:T(8,128)(2,1)S(1)} %get-tuple-element.19), channel_id=1, source_target_pairs={{0,8},{8,16},{16,24},{24,32},{32,40},{40,48},{48,56},{56,64},{64,7... | collective-permute-start | bytes 135176 | tf_op jit(solution)/shard_map/ppermute | solution.py:246

commit v5 on v3

--- a/solution.py
+++ b/solution.py
@@ -11,6 +11,9 @@
 PIECE = 16
 SHAPE = (4, 2, 8, 2, 8)
 AXES = ("zh", "zl", "y", "c", "x")
+NEAR = ("zl", "y", "c")
+FAR = ("zh", "x")
+CHUNK = 16
 LAST = (((1,), (1,)), ((), ()))
 FIRST = (((0,), (0,)), ((), ()))
 PLAIN = (((1,), (0,)), ((), ()))
@@ -51,14 +54,15 @@
     return [side.astype(BF16) for side in sides]
 
 
-def pick_kernel(counts, send_lists, features, first, second):
-    sides = slots_onehot(counts, send_lists, features.shape[0])
-    for onehot, out in zip(sides, (first, second), strict=True):
-        out[...] = dot(onehot, features[...], FIRST).astype(BF16)
+def pick_kernel(core, counts, send_lists, features, partner, outside):
+    first, second = slots_onehot(counts, send_lists, features.shape[0])
+    even = core[0] == 0
+    partner[...] = dot(jnp.where(even, second, first), features[...], FIRST).astype(BF16)
+    outside[...] = dot(jnp.where(even, first, second), features[...], FIRST).astype(BF16)
 
 
 def layer_kernel(
-    rows, cols, tiles_hbm, own_hbm, halo_hbm, weight, labels,
+    core, rows, cols, tiles_hbm, own_hbm, halo_hbm, weight, labels,
     weight_out, grads,
     tiles, columns, sums, sems,
 ):
@@ -66,13 +70,27 @@
     classes, hidden = weight.shape
     padded = grads.shape[1]
     nodes = labels.shape[1]
-    group = 4
+    send = tile // 2
+    partner_at = pl.multiple_of(send * (1 - core[0]), send)
+    outside_at = pl.multiple_of(send * core[0], send)
     copies = [
         pltpu.make_async_copy(own_hbm, columns.at[:, 0:2], sems.at[0]),
-        pltpu.make_async_copy(halo_hbm, columns.at[:, 2:3], sems.at[1]),
-        pltpu.make_async_copy(tiles_hbm, tiles, sems.at[2]),
+        pltpu.make_async_copy(
+            halo_hbm.at[:, :send], columns.at[:, 2, pl.ds(partner_at, send)], sems.at[1]
+        ),
+        pltpu.make_async_copy(
+            halo_hbm.at[:, send:], columns.at[:, 2, pl.ds(outside_at, send)], sems.at[2]
+        ),
     ]
-    for copy in copies:
+    tile_copies = [
+        pltpu.make_async_copy(
+            tiles_hbm.at[pl.ds(start, CHUNK)],
+            tiles.at[pl.ds(start, CHUNK)],
+            sems.at[3 + start // CHUNK],
+        )
+        for start in range(0, count, CHUNK)
+    ]
+    for copy in copies + tile_copies:
         copy.start()
 
     def masked(t):
@@ -89,13 +107,11 @@
     grads[...] = jnp.zeros_like(grads)
     for copy in copies:
         copy.wait()
-    for start in range(0, count, group):
-        picks = [masked(t) for t in range(start, start + group)]
-        left = jnp.concatenate(
-            [jnp.concatenate([p[i] for p in picks], axis=1) for i in range(2)], axis=0
-        )
-        right = jnp.concatenate([column(t) for t in range(start, start + group)], axis=0)
-        sums[...] += dot(left, right)
+    for t in range(count):
+        if t % CHUNK == 0:
+            tile_copies[t // CHUNK].wait()
+        at = pl.ds(pl.multiple_of(rows[t] * tile, tile), tile)
+        sums[at, :] += dot(tiles[t], column(t))
 
     total = sums[...]
     high = total.astype(BF16)
@@ -128,13 +144,17 @@
         grads[cols[start]] += both[:, :tile]
         grads[cols[start + 1]] += both[:, tile:]
 
+
 def sum_kernel(parts, out):
     summed = jnp.sum(parts[...].astype(F32), axis=0, keepdims=True)
     out[...] = jnp.broadcast_to(summed.astype(out.dtype), out.shape)
 
 
-def rows_kernel(counts, send_lists, own, before, after, weight, out):
-    padded = before.shape[0]
+def rows_kernel(core, counts, send_lists, own, partner, outside, weight, out):
+    padded = partner.shape[0]
+    even = core[0] == 0
+    before = jnp.where(even, outside[...], partner[...])
+    after = jnp.where(even, partner[...], outside[...])
     classes = weight.shape[0]
     first, second = slots_onehot(counts, send_lists, out.shape[0])
     send = send_lists.shape[1]
@@ -167,48 +187,52 @@
     reps = lax.axis_size("x")
     dom = AXES[:-1]
     domains = lax.axis_size(dom)
-    near = ("zl", "y", "c")
-    far = ("zh", "x")
     padded = round_up(classes + 1, PIECE)
-    up = [(i, i + 1) for i in range(domains - 1)]
-    down = [(i + 1, i) for i in range(domains - 1)]
+    core = jnp.reshape(lax.axis_index("c"), (1,)).astype(jnp.int32)
+    outer = [(i, i + 1) for i in range(1, domains - 1, 2)]
+    outer += [(target, source) for source, target in outer]
+
+    def exchange(to_partner, to_outside):
+        return (
+            lax.ppermute(to_partner, "c", [(0, 1), (1, 0)]),
+            lax.ppermute(to_outside, dom, outer),
+        )
+
     shape = jax.ShapeDtypeStruct
     weight = weight.T
 
-    first, second = pl.pallas_call(
+    picked = pl.pallas_call(
         pick_kernel,
         out_shape=(shape((send, hidden), BF16),) * 2,
-        in_specs=[smem(), vmem(), vmem()],
+        in_specs=[smem(), smem(), vmem(), vmem()],
         out_specs=(vmem(),) * 2,
-    )(counts, send_lists, features)
-    from_before = lax.ppermute(second, dom, up)
-    from_after = lax.ppermute(first, dom, down)
+    )(core, counts, send_lists, features)
+    halo = jnp.concatenate(exchange(*picked), axis=0)
     own_rows = lax.all_gather(features, "x", axis=0, tiled=True)
-    halo_rows = lax.all_gather(
-        jnp.concatenate([from_before, from_after], axis=0), "x", axis=0, tiled=True
-    )
+    halo_rows = lax.all_gather(halo, "x", axis=0)
 
     weight_parts, parts = pl.pallas_call(
         layer_kernel,
         out_shape=(
-            shape((lax.axis_size(near), PIECE, LANES), BF16),
+            shape((lax.axis_size(NEAR), PIECE, LANES), BF16),
             shape((3 * reps, padded, tile), F32),
         ),
-        in_specs=[smem(), smem(), hbm(), hbm(), hbm(), vmem(), vmem()],
+        in_specs=[smem(), smem(), smem(), hbm(), hbm(), hbm(), vmem(), vmem()],
         out_specs=(vmem(),) * 2,
         scratch_shapes=[
             pltpu.VMEM((count, tile, tile), BF16),
             pltpu.VMEM((reps, 3, tile, hidden), BF16),
             pltpu.VMEM((nodes, hidden), F32),
-            pltpu.SemaphoreType.DMA((3,)),
+            pltpu.SemaphoreType.DMA((3 + count // CHUNK,)),
         ],
         compiler_params=params(56),
     )(
+        core,
         tile_rows,
         tile_cols,
         tiles,
         own_rows.reshape(reps, 2, tile, hidden),
-        halo_rows.reshape(reps, 1, tile, hidden),
+        halo_rows,
         weight,
         labels.reshape(1, nodes),
     )
@@ -223,22 +247,21 @@
         )(parts)
 
     own = lax.psum_scatter(parts, "x", scatter_dimension=0, tiled=True)
-    weight_parts = lax.all_to_all(weight_parts, near, 0, 0, tiled=True)
-    weight_parts = fold(weight_parts, lax.axis_size(far))
-    weight_parts = lax.all_to_all(weight_parts, far, 0, 0, tiled=True)
-    weight_parts = fold(weight_parts, lax.axis_size(near))
-    weight_parts = lax.all_to_all(weight_parts, near, 0, 0, tiled=True)
+    weight_parts = lax.all_to_all(weight_parts, NEAR, 0, 0, tiled=True)
+    weight_parts = fold(weight_parts, lax.axis_size(FAR))
+    weight_parts = lax.all_to_all(weight_parts, FAR, 0, 0, tiled=True)
+    weight_parts = fold(weight_parts, lax.axis_size(NEAR))
+    weight_parts = lax.all_to_all(weight_parts, NEAR, 0, 0, tiled=True)
 
     halo = own[2].astype(BF16)
-    before = lax.ppermute(halo, dom, up)
-    after = lax.ppermute(halo, dom, down)
     grad_features = pl.pallas_call(
         rows_kernel,
         out_shape=shape((nodes, hidden), BF16),
-        in_specs=[smem()] + [vmem()] * 5,
+        in_specs=[smem(), smem()] + [vmem()] * 5,
         out_specs=vmem(),
         compiler_params=params(4),
-    )(counts, send_lists, own, before, after, weight)
+    )(core, counts, send_lists, own, *exchange(halo, halo), weight)
+    weight_parts, grad_features = lax.optimization_barrier((weight_parts, grad_features))
 
     scale = 1.0 / (domains * reps * nodes)
     weight_grad, loss = pl.pallas_call(

time: 144 us -> 142 us (0.986)
  waiting for transfers between devices: 17.8 us -> 14.5 us
    all_gather x1, waiting for transfers between devices: 13.6 us -> 8.85 us  [per_device(): own_rows = lax.all_gather(features, 'x', axis=0, tiled=True)]
    ppermute x4, waiting for transfers between devices: 1.05 us -> 4.93 us  [the longest x2 3.82 us: exchange(): lax.ppermute(to_outside, dom, outer)]
    all_to_all x1, waiting for transfers between devices: 2.43 us -> 0.01 us  [per_device(): weight_parts = lax.all_to_all(weight_parts, NEAR, 0, 0, tiled=True)]
  transfers between devices with their start and end apart: 7 -> 7, of which waited for: 3 -> 4; matrix products, arithmetic and copies ran while one was open for 1% -> 1% of each run, Pallas kernels for 2% -> 3%
where the time goes in v5:
time: 142 us; the launch traced here: 141 us
  blocking collectives  66.1 us (47%)
  starting transfers between devices  31.4 us (22%)
  waiting for transfers between devices  14.5 us (10%)
  between operations  14.2 us (10%)
  Pallas kernels  12.3 us (9%)
  local copies, waits for them, and re-layouts  2.7 us (2%)
    all_gather x1, blocking collectives, per_device(): halo_rows = lax.all_gather(halo, 'x', axis=0)  22.6 us
    all_to_all x1, blocking collectives, per_device(): weight_parts = lax.all_to_all(weight_parts, FAR, 0, 0, tiled=True)  22.4 us
    all_to_all x1, blocking collectives, per_device(): weight_parts = lax.all_to_all(weight_parts, NEAR, 0, 0, tiled=True)  21.1 us
    ppermute x2, starting transfers between devices, exchange(): lax.ppermute(to_partner, 'c', [(0, 1), (1, 0)])  18 us
    all_gather x1, waiting for transfers between devices, per_device(): own_rows = lax.all_gather(features, 'x', axis=0, tiled=True)  8.85 us
    pallas_call x1, Pallas kernels, per_device(): pl.pallas_call(layer_kernel, out_shape=(shape((lax.axis_size(NEAR), PIECE...  7.45 us
    all_to_all x1, starting transfers between devices, per_device(): weight_parts = lax.all_to_all(weight_parts, NEAR, 0, 0, tiled=True)  7.08 us
    ppermute x2, starting transfers between devices, exchange(): lax.ppermute(to_outside, dom, outer)  6.23 us
  transfers between devices with their start and end apart: 7, of which 4 were waited for; matrix products, arithmetic and copies ran while one was open for 1% of the time, Pallas kernels for 3%

profile of v5, /device:TPU:1, one launch (start us, length us, event | category | flops | bytes accessed | tf_op | source)
XLA Modules:
  0.0 141.2 jit_solution(11905409212125405219)
XLA Ops:
  7.2 0.0 all-gather.3.cloned.1.call-start
  7.2 0.7 all-gather.3.cloned.1.call-update
  7.9 0.0 reduce-scatter.2.cloned.1.call-start
  7.9 1.8 %shard_map.103 = (bf16[64,256]{1,0:T(8,128)(2,1)}, bf16[64,256]{1,0:T(8,128)(2,1)}) custom-call(s32[1]{0:T(128)} %bitcast.core, s32[2]{0:T(128)} %counts.3, s32[2,64]{1,0:T(2,128)} %send_lists.3, bf16[256,256]{1,0:T(8,128)(2,1)} %features.1), custom_call_target="tpu_custom_call" | custom-call | tf_op jit(solution)/shard_map/pallas_call | solution.py:204
  9.7 16.0 %collective-permute-start = (bf16[64,256]{1,0:T(8,128)(2,1)}, bf16[64,256]{1,0:T(8,128)(2,1)S(1)}, u32[]{:S(2)}, u32[]{:S(2)}) collective-permute-start(bf16[64,256]{1,0:T(8,128)(2,1)} %get-tuple-element.11), channel_id=1, source_target_pairs={{0,8},{8,0},{1,9},{9,1},{2,10},{10,2},{3,11},{11,3},{4,12},{12,4},... | collective-permute-start | bytes 98312 | tf_op jit(solution)/shard_map/ppermute | solution.py:197
  25.8 1.9 %collective-permute-start.1 = (bf16[64,256]{1,0:T(8,128)(2,1)}, bf16[64,256]{1,0:T(8,128)(2,1)S(1)}, u32[]{:S(2)}, u32[]{:S(2)}) collective-permute-start(bf16[64,256]{1,0:T(8,128)(2,1)} %get-tuple-element.12), channel_id=1, source_target_pairs={{8,16},{24,32},{40,48},{56,64},{72,80},{88,96},{104,112},{120,128}... | collective-permute-start | bytes 98312 | tf_op jit(solution)/shard_map/ppermute | solution.py:198
  27.7 0.0 collective-permute-done
  27.7 3.7 %collective-permute-done.1 = bf16[64,256]{1,0:T(8,128)(2,1)S(1)} collective-permute-done((bf16[64,256]{1,0:T(8,128)(2,1)}, bf16[64,256]{1,0:T(8,128)(2,1)S(1)}, u32[]{:S(2)}, u32[]{:S(2)}) %collective-permute-start.1) | collective-permute-done | bytes 32800 | tf_op jit(solution)/shard_map/ppermute | solution.py:198
  31.5 22.6 %all-gather = bf16[1024,256]{1,0:T(8,128)(2,1)} all-gather(bf16[128,256]{1,0:T(8,128)(2,1)S(1)} %pad_maximum_fusion), channel_id=2, replica_groups=mesh['zh'=4,'zl'=2,'y'=8,'c'=2,'x'=8] {'x'}, dimensions={0}, use_global_device_ids=true | all-gather | bytes 589824 | tf_op jit(solution)/shard_map/all_gather | solution.py:212
  54.0 8.9 %all-gather.3.cloned.1.call-done = bf16[2048,256]{1,0:T(8,128)(2,1)} async-done(((bf16[256,256]{1,0:T(8,128)(2,1)}), bf16[2048,256]{1,0:T(8,128)(2,1)}) %all-gather.3.cloned.1.call-update) | async-done | bytes 1048592 | tf_op jit(solution)/shard_map/all_gather | solution.py:211
  62.9 7.4 %shard_map.104 = (bf16[32,16,128]{2,1,0:T(8,128)(2,1)}, f32[24,176,128]{2,1,0:T(8,128)}) custom-call(s32[1]{0:T(128)} %bitcast.core, s32[64]{0:T(128)} %rows.1, s32[64]{0:T(128)} %cols.1, bf16[64,128,128]{2,1,0:T(8,128)(2,1)} %tiles_hbm.1, bf16[8,2,128,256]{3,2,1,0:T(8,128)(2,1)} %bitcast.12, bf16[8,128,256]{2,1,0:T(8,128)(2,1)} %bitcast.11, ...), custom_call_target="tpu_custom_call" | custom-call | tf_op jit(solution)/shard_map/pallas_call | solution.py:214
  70.3 0.0 copy-start.4
  70.3 0.0 copy-start.1
  70.3 0.0 copy-start.2
  70.4 0.0 copy-start.3
  70.4 0.0 reduce-scatter.2.cloned.1.call-update
  70.4 0.8 copy-done.4
  71.2 21.1 %all_to_all.15.parts = bf16[32,16,128]{2,1,0:T(8,128)(2,1)S(1)} all-to-all(bf16[32,16,128]{2,1,0:T(8,128)(2,1)S(1)} %copy-done.4), channel_id=1, replica_groups=mesh['zh'=4,'zl'=2,'y'=8,'c'=2,'x'=8] {'zl','y','c'}, dimensions={0} | all-to-all | bytes 262144 | tf_op jit(solution)/shard_map/all_to_all | solution.py:250
  92.4 22.4 %all_to_all.16.parts = bf16[32,16,128]{2,1,0:T(8,128)(2,1)S(1)} all-to-all(bf16[32,16,128]{2,1,0:T(8,128)(2,1)S(1)} %shard_map.105), channel_id=1, replica_groups=mesh['zh'=4,'zl'=2,'y'=8,'c'=2,'x'=8] {'zh','x'}, dimensions={0} | all-to-all | bytes 262144 | tf_op jit(solution)/shard_map/all_to_all | solution.py:252
  114.8 0.7 shard_map.106
  115.5 7.1 %all-to-all-start.2 = ((bf16[32,16,128]{2,1,0:T(8,128)(2,1)}), bf16[32,16,128]{2,1,0:T(8,128)(2,1)S(1)}, u32[]{:S(2)}, u32[]{:S(2)}) async-start(bf16[32,16,128]{2,1,0:T(8,128)(2,1)} %shard_map.106), calls=%async_computation.2 | async-start | bytes 262144 | tf_op jit(solution)/shard_map/all_to_all | solution.py:254
  122.6 0.0 reduce-scatter.2.cloned.1.call-done.own
  122.6 0.9 fusion
  123.5 4.3 %collective-permute-start.3 = (bf16[176,128]{1,0:T(8,128)(2,1)S(1)}, bf16[176,128]{1,0:T(8,128)(2,1)S(1)}, u32[]{:S(2)}, u32[]{:S(2)}) collective-permute-start(bf16[176,128]{1,0:T(8,128)(2,1)S(1)} %fusion), channel_id=1, source_target_pairs={{8,16},{24,32},{40,48},{56,64},{72,80},{88,96},{104,112},{120,128}... | collective-permute-start | bytes 135176 | tf_op jit(solution)/shard_map/ppermute | solution.py:198
  127.8 1.9 %collective-permute-start.2 = (bf16[176,128]{1,0:T(8,128)(2,1)S(1)}, bf16[176,128]{1,0:T(8,128)(2,1)S(1)}, u32[]{:S(2)}, u32[]{:S(2)}) collective-permute-start(bf16[176,128]{1,0:T(8,128)(2,1)S(1)} %fusion), channel_id=1, source_target_pairs={{0,8},{8,0},{1,9},{9,1},{2,10},{10,2},{3,11},{11,3},{4,12},{12,4},... | collective-permute-start | bytes 135176 | tf_op jit(solution)/shard_map/ppermute | solution.py:197
  129.8 0.1 collective-permute-done.3.outside
  129.9 1.1 collective-permute-done.2.partner
  131.0 0.0 copy-done.1
  131.0 0.0 copy-done.2
  131.0 0.0 copy-done.3
  131.0 0.0 copy-start
  131.0 0.9 copy-done
  131.9 1.7 %shard_map.107 = bf16[256,256]{1,0:T(8,128)(2,1)} custom-call(s32[1]{0:T(128)} %bitcast.core, s32[2]{0:T(128)S(1)} %copy-done.3, s32[2,64]{1,0:T(2,128)S(1)} %copy-done.2, f32[3,176,128]{2,1,0:T(8,128)S(1)} %copy-done, bf16[176,128]{1,0:T(8,128)(2,1)S(1)} %collective-permute-done.2.partner, bf16[176,128]{1,0:T(8,128)(2,1)S(1)} %collective-permute-done.3.outside, ...), custom_call_target="tpu_custom_call" | custom-call | tf_op jit(solution)/shard_map/pallas_call | solution.py:257
  133.6 0.0 all-to-all-done.2.refs_0_
  133.6 0.7 shard_map.108
  (2 shorter events, 0.0 us)
Async XLA Ops:
  7.2 55.7 %all-gather.3.cloned.1.call-start = ((), (), s32[]{:S(2)}) async-start(), calls=%async_computation.4 | async-start | bytes 1179648 | tf_op jit(solution)/shard_map/all_gather | solution.py:211
  7.9 114.7 %reduce-scatter.2.cloned.1.call-start = ((), (), s32[]{:S(2)}) async-start(), calls=%async_computation.5 | async-start | bytes 2433024 | tf_op jit(solution)/shard_map/reduce_scatter | solution.py:249
  9.7 18.0 %collective-permute-start = (bf16[64,256]{1,0:T(8,128)(2,1)}, bf16[64,256]{1,0:T(8,128)(2,1)S(1)}, u32[]{:S(2)}, u32[]{:S(2)}) collective-permute-start(bf16[64,256]{1,0:T(8,128)(2,1)} %get-tuple-element.11), channel_id=1, source_target_pairs={{0,8},{8,0},{1,9},{9,1},{2,10},{10,2},{3,11},{11,3},{4,12},{12,4},... | collective-permute-start | bytes 98312 | tf_op jit(solution)/shard_map/ppermute | solution.py:197
  25.8 5.7 %collective-permute-start.1 = (bf16[64,256]{1,0:T(8,128)(2,1)}, bf16[64,256]{1,0:T(8,128)(2,1)S(1)}, u32[]{:S(2)}, u32[]{:S(2)}) collective-permute-start(bf16[64,256]{1,0:T(8,128)(2,1)} %get-tuple-element.12), channel_id=1, source_target_pairs={{8,16},{24,32},{40,48},{56,64},{72,80},{88,96},{104,112},{120,128}... | collective-permute-start | bytes 98312 | tf_op jit(solution)/shard_map/ppermute | solution.py:198
  70.3 0.9 copy-start.4
  70.3 60.6 %copy-start.1 = (bf16[256,172]{0,1:T(8,128)(2,1)S(1)}, bf16[256,172]{0,1:T(8,128)(2,1)}, u32[]{:S(2)}) copy-start(bf16[256,172]{0,1:T(8,128)(2,1)} %param.9) | copy-start | bytes 264196
  70.3 60.6 %copy-start.2 = (s32[2,64]{1,0:T(2,128)S(1)}, s32[2,64]{1,0:T(2,128)}, u32[]{:S(2)}) copy-start(s32[2,64]{1,0:T(2,128)} %send_lists.3) | copy-start | bytes 1540
  70.4 60.6 %copy-start.3 = (s32[2]{0:T(128)S(1)}, s32[2]{0:T(128)}, u32[]{:S(2)}) copy-start(s32[2]{0:T(128)} %counts.3) | copy-start | bytes 28
  115.5 18.1 %all-to-all-start.2 = ((bf16[32,16,128]{2,1,0:T(8,128)(2,1)}), bf16[32,16,128]{2,1,0:T(8,128)(2,1)S(1)}, u32[]{:S(2)}, u32[]{:S(2)}) async-start(bf16[32,16,128]{2,1,0:T(8,128)(2,1)} %shard_map.106), calls=%async_computation.2 | async-start | bytes 262144 | tf_op jit(solution)/shard_map/all_to_all | solution.py:254
  123.5 6.3 %collective-permute-start.3 = (bf16[176,128]{1,0:T(8,128)(2,1)S(1)}, bf16[176,128]{1,0:T(8,128)(2,1)S(1)}, u32[]{:S(2)}, u32[]{:S(2)}) collective-permute-start(bf16[176,128]{1,0:T(8,128)(2,1)S(1)} %fusion), channel_id=1, source_target_pairs={{8,16},{24,32},{40,48},{56,64},{72,80},{88,96},{104,112},{120,128}... | collective-permute-start | bytes 135176 | tf_op jit(solution)/shard_map/ppermute | solution.py:198
  127.8 3.1 %collective-permute-start.2 = (bf16[176,128]{1,0:T(8,128)(2,1)S(1)}, bf16[176,128]{1,0:T(8,128)(2,1)S(1)}, u32[]{:S(2)}, u32[]{:S(2)}) collective-permute-start(bf16[176,128]{1,0:T(8,128)(2,1)S(1)} %fusion), channel_id=1, source_target_pairs={{0,8},{8,0},{1,9},{9,1},{2,10},{10,2},{3,11},{11,3},{4,12},{12,4},... | collective-permute-start | bytes 135176 | tf_op jit(solution)/shard_map/ppermute | solution.py:197
  131.0 1.0 copy-start
Sparse Core Ops, SparseCore 0:
  10.7 52.1 all-gather.2
  70.5 49.0 reduce-scatter.1

commit v6 on v5

--- a/solution.py
+++ b/solution.py
@@ -9,11 +9,13 @@
 BF16 = jnp.bfloat16
 LANES = 128
 PIECE = 16
+EARLY = 192
 SHAPE = (4, 2, 8, 2, 8)
 AXES = ("zh", "zl", "y", "c", "x")
-NEAR = ("zl", "y", "c")
-FAR = ("zh", "x")
+NEAR = ("zl", "c", "x")
+FAR = ("y", "zh")
 CHUNK = 16
+LIMIT = 56
 LAST = (((1,), (1,)), ((), ()))
 FIRST = (((0,), (0,)), ((), ()))
 PLAIN = (((1,), (0,)), ((), ()))
@@ -54,7 +56,8 @@
     return [side.astype(BF16) for side in sides]
 
 
-def pick_kernel(core, counts, send_lists, features, partner, outside):
+def pick_kernel(core, counts, send_lists, features, partner, outside, copies):
+    copies[...] = jnp.broadcast_to(features[: copies.shape[1]][None], copies.shape)
     first, second = slots_onehot(counts, send_lists, features.shape[0])
     even = core[0] == 0
     partner[...] = dot(jnp.where(even, second, first), features[...], FIRST).astype(BF16)
@@ -62,31 +65,33 @@
 
 
 def layer_kernel(
-    core, rows, cols, tiles_hbm, own_hbm, halo_hbm, weight, labels,
-    weight_out, grads,
-    tiles, columns, sums, sems,
+    core, rows, cols, tiles_hbm, own_hbm, rest_hbm, weight, labels,
+    weight_out, out,
+    tiles, columns, sums, grads, sems,
 ):
     count, tile = tiles.shape[0], tiles.shape[1]
     classes, hidden = weight.shape
     padded = grads.shape[1]
     nodes = labels.shape[1]
-    send = tile // 2
-    partner_at = pl.multiple_of(send * (1 - core[0]), send)
-    outside_at = pl.multiple_of(send * core[0], send)
+    send, early = tile // 2, own_hbm.shape[1]
+    late = nodes - early
+    partner_at = pl.multiple_of(nodes + send * (1 - core[0]), send)
+    outside_at = pl.multiple_of(nodes + send * core[0], send)
     copies = [
-        pltpu.make_async_copy(own_hbm, columns.at[:, 0:2], sems.at[0]),
+        pltpu.make_async_copy(own_hbm, columns.at[:, :early], sems.at[0]),
+        pltpu.make_async_copy(rest_hbm.at[:, :late], columns.at[:, early:nodes], sems.at[1]),
         pltpu.make_async_copy(
-            halo_hbm.at[:, :send], columns.at[:, 2, pl.ds(partner_at, send)], sems.at[1]
+            rest_hbm.at[:, late : late + send], columns.at[:, pl.ds(partner_at, send)], sems.at[2]
         ),
         pltpu.make_async_copy(
-            halo_hbm.at[:, send:], columns.at[:, 2, pl.ds(outside_at, send)], sems.at[2]
+            rest_hbm.at[:, late + send :], columns.at[:, pl.ds(outside_at, send)], sems.at[3]
         ),
     ]
     tile_copies = [
         pltpu.make_async_copy(
             tiles_hbm.at[pl.ds(start, CHUNK)],
             tiles.at[pl.ds(start, CHUNK)],
-            sems.at[3 + start // CHUNK],
+            sems.at[4 + start // CHUNK],
         )
         for start in range(0, count, CHUNK)
     ]
@@ -101,7 +106,8 @@
 
     def column(t):
         member = cols[t] // 3
-        return columns[member, cols[t] - 3 * member]
+        start = pl.multiple_of((cols[t] - 3 * member) * tile, tile)
+        return columns[member, pl.ds(start, tile), :]
 
     sums[...] = jnp.zeros_like(sums)
     grads[...] = jnp.zeros_like(grads)
@@ -143,11 +149,19 @@
         both = dot(grad, right)
         grads[cols[start]] += both[:, :tile]
         grads[cols[start + 1]] += both[:, tile:]
-
+    for r in range(out.shape[0]):
+        for j in range(3):
+            out[r, j * padded : (j + 1) * padded, :] = grads[3 * r + j].astype(BF16)
+
+
+def fold_kernel(parts, own, halo):
+    padded = halo.shape[0]
+    summed = jnp.sum(parts[...].astype(F32), axis=0)
+    own[...] = summed[: 2 * padded]
+    halo[...] = summed[2 * padded :].astype(BF16)
 
 def sum_kernel(parts, out):
-    summed = jnp.sum(parts[...].astype(F32), axis=0, keepdims=True)
-    out[...] = jnp.broadcast_to(summed.astype(out.dtype), out.shape)
+    out[...] = jnp.sum(parts[...].astype(F32), axis=0)
 
 
 def rows_kernel(core, counts, send_lists, own, partner, outside, weight, out):
@@ -158,7 +172,7 @@
     classes = weight.shape[0]
     first, second = slots_onehot(counts, send_lists, out.shape[0])
     send = send_lists.shape[1]
-    total = jnp.concatenate([own[0], own[1]], axis=1)
+    total = jnp.concatenate([own[:padded], own[padded:]], axis=1)
     total += dot(before[:, send:], first, LAST)
     total += dot(after[:, :send], second, LAST)
     grad = total[:classes].astype(BF16)
@@ -201,59 +215,59 @@
     shape = jax.ShapeDtypeStruct
     weight = weight.T
 
-    picked = pl.pallas_call(
+    *picked, copies = pl.pallas_call(
         pick_kernel,
-        out_shape=(shape((send, hidden), BF16),) * 2,
+        out_shape=(
+            shape((send, hidden), BF16),
+            shape((send, hidden), BF16),
+            shape((reps, EARLY, hidden), BF16),
+        ),
         in_specs=[smem(), smem(), vmem(), vmem()],
-        out_specs=(vmem(),) * 2,
+        out_specs=(vmem(),) * 3,
     )(core, counts, send_lists, features)
-    halo = jnp.concatenate(exchange(*picked), axis=0)
-    own_rows = lax.all_gather(features, "x", axis=0, tiled=True)
-    halo_rows = lax.all_gather(halo, "x", axis=0)
+    own_rows = lax.all_to_all(copies, "x", 0, 0, tiled=True)
+    rest = jnp.concatenate([features[EARLY:], *exchange(*picked)], axis=0)
+    rest_rows = lax.all_gather(rest, "x", axis=0)
 
     weight_parts, parts = pl.pallas_call(
         layer_kernel,
         out_shape=(
             shape((lax.axis_size(NEAR), PIECE, LANES), BF16),
-            shape((3 * reps, padded, tile), F32),
+            shape((reps, 3 * padded, LANES), BF16),
         ),
         in_specs=[smem(), smem(), smem(), hbm(), hbm(), hbm(), vmem(), vmem()],
         out_specs=(vmem(),) * 2,
         scratch_shapes=[
             pltpu.VMEM((count, tile, tile), BF16),
-            pltpu.VMEM((reps, 3, tile, hidden), BF16),
+            pltpu.VMEM((reps, 3 * tile, hidden), BF16),
             pltpu.VMEM((nodes, hidden), F32),
-            pltpu.SemaphoreType.DMA((3 + count // CHUNK,)),
+            pltpu.VMEM((3 * reps, padded, tile), F32),
+            pltpu.SemaphoreType.DMA((4 + count // CHUNK,)),
         ],
-        compiler_params=params(56),
-    )(
-        core,
-        tile_rows,
-        tile_cols,
-        tiles,
-        own_rows.reshape(reps, 2, tile, hidden),
-        halo_rows,
-        weight,
-        labels.reshape(1, nodes),
-    )
-
-    def fold(parts, copies):
-        return pl.pallas_call(
-            sum_kernel,
-            out_shape=shape((copies, *parts.shape[1:]), BF16),
-            in_specs=[vmem()],
-            out_specs=vmem(),
-            compiler_params=params(4),
-        )(parts)
-
-    own = lax.psum_scatter(parts, "x", scatter_dimension=0, tiled=True)
+        compiler_params=params(LIMIT),
+    )(core, tile_rows, tile_cols, tiles, own_rows, rest_rows, weight, labels.reshape(1, nodes))
+
     weight_parts = lax.all_to_all(weight_parts, NEAR, 0, 0, tiled=True)
-    weight_parts = fold(weight_parts, lax.axis_size(FAR))
-    weight_parts = lax.all_to_all(weight_parts, FAR, 0, 0, tiled=True)
-    weight_parts = fold(weight_parts, lax.axis_size(NEAR))
-    weight_parts = lax.all_to_all(weight_parts, NEAR, 0, 0, tiled=True)
-
-    halo = own[2].astype(BF16)
+    weight_part = pl.pallas_call(
+        sum_kernel,
+        out_shape=shape(weight_parts.shape[1:], F32),
+        in_specs=[vmem()],
+        out_specs=vmem(),
+        compiler_params=params(4),
+    )(weight_parts)
+    weight_part, parts = lax.optimization_barrier((weight_part, parts))
+    parts = lax.all_to_all(parts, "x", 0, 0, tiled=True)
+    weight_part = lax.psum(lax.psum(weight_part, "y"), "zh").astype(BF16)
+    copies = jnp.broadcast_to(weight_part[None], weight_parts.shape)
+    weight_parts = lax.all_to_all(copies, NEAR, 0, 0, tiled=True)
+
+    own, halo = pl.pallas_call(
+        fold_kernel,
+        out_shape=(shape((2 * padded, LANES), F32), shape((padded, LANES), BF16)),
+        in_specs=[vmem()],
+        out_specs=(vmem(),) * 2,
+        compiler_params=params(8),
+    )(parts)
     grad_features = pl.pallas_call(
         rows_kernel,
         out_shape=shape((nodes, hidden), BF16),

time: 142 us -> 147 us (1.035)
  blocking collectives: 66.1 us -> 82.1 us
  between operations: 14.2 us -> 0.79 us
  starting transfers between devices: 31.4 us -> 42.2 us
  waiting for transfers between devices: 14.5 us -> 7.56 us
    psum x0 -> x2, blocking collectives: none -> 38.2 us  [per_device(): weight_part = lax.psum(lax.psum(weight_part, 'y'), 'zh').astype(BF16)]
    all_to_all x1 -> x0, blocking collectives: 22.4 us -> none  [per_device(): weight_parts = lax.all_to_all(weight_parts, FAR, 0, 0, tiled=True)]
    all_to_all x1 -> x3, starting transfers between devices: 7.08 us -> 24.1 us  [the longest x1 13.1 us: per_device(): weight_parts = lax.all_to_all(copies, NEAR, 0, 0, tiled=True)]
    all_gather x1 -> x0, waiting for transfers between devices: 8.85 us -> none  [per_device(): own_rows = lax.all_gather(features, 'x', axis=0, tiled=True)]
    ppermute x2, starting transfers between devices: 18 us -> 14.2 us  [exchange(): lax.ppermute(to_partner, 'c', [(0, 1), (1, 0)])]
    ppermute x2, starting transfers between devices: 6.23 us -> 3.84 us  [exchange(): lax.ppermute(to_outside, dom, outer)]
    all_to_all x1 -> x3, waiting for transfers between devices: 0.01 us -> 2.16 us  [the longest x1 2.15 us: per_device(): weight_parts = lax.all_to_all(copies, NEAR, 0, 0, tiled=True)]
    all_gather x1, blocking collectives: 22.6 us -> 24.5 us  [per_device(): rest_rows = lax.all_gather(rest, 'x', axis=0)]
  transfers between devices with their start and end apart: 7 -> 7, of which waited for: 4 -> 3; matrix products, arithmetic and copies ran while one was open for 1% -> 0% of each run, Pallas kernels for 3% -> 1%
where the time goes in v6:
time: 147 us; the launch traced here: 146 us
  blocking collectives  82.1 us (56%)
  starting transfers between devices  42.2 us (29%)
  Pallas kernels  11.8 us (8%)
  waiting for transfers between devices  7.56 us (5%)
  local copies, waits for them, and re-layouts  1.61 us (1%)
    psum x2, blocking collectives, per_device(): weight_part = lax.psum(lax.psum(weight_part, 'y'), 'zh').astype(BF16)  38.2 us
    all_gather x1, blocking collectives, per_device(): rest_rows = lax.all_gather(rest, 'x', axis=0)  24.5 us
    all_to_all x1, blocking collectives, per_device(): weight_parts = lax.all_to_all(weight_parts, NEAR, 0, 0, tiled=True)  19.4 us
    ppermute x2, starting transfers between devices, exchange(): lax.ppermute(to_partner, 'c', [(0, 1), (1, 0)])  14.2 us
    all_to_all x1, starting transfers between devices, per_device(): weight_parts = lax.all_to_all(copies, NEAR, 0, 0, tiled=True)  13.1 us
    all_to_all x1, starting transfers between devices, per_device(): own_rows = lax.all_to_all(copies, 'x', 0, 0, tiled=True)  7.44 us
    pallas_call x1, Pallas kernels, per_device(): pl.pallas_call(layer_kernel, out_shape=(shape((lax.axis_size(NEAR), PIECE...  7.19 us
    ppermute x2, waiting for transfers between devices, exchange(): lax.ppermute(to_outside, dom, outer)  5.39 us
  transfers between devices with their start and end apart: 7, of which 3 were waited for; matrix products, arithmetic and copies ran while one was open for 0% of the time, Pallas kernels for 1%

profile of v6, /device:TPU:1, one launch (start us, length us, event | category | flops | bytes accessed | tf_op | source)
XLA Modules:
  0.0 146.1 jit_solution(15533332881239199779)
XLA Ops:
  0.6 0.0 slice-start
  0.6 2.1 %shard_map.103 = (bf16[64,256]{1,0:T(8,128)(2,1)}, bf16[64,256]{1,0:T(8,128)(2,1)}, bf16[8,192,256]{2,1,0:T(8,128)(2,1)}) custom-call(s32[1]{0:T(128)} %bitcast.core, s32[2]{0:T(128)} %counts.3, s32[2,64]{1,0:T(2,128)} %send_lists.3, bf16[256,256]{1,0:T(8,128)(2,1)} %features.1), custom_call_target="tpu_custom_call" | custom-call | tf_op jit(solution)/shard_map/pallas_call | solution.py:218
  2.7 0.0 copy-start.5
  2.7 0.0 copy-start.4
  2.7 7.4 %all-to-all-start = ((bf16[8,192,256]{2,1,0:T(8,128)(2,1)}), bf16[8,192,256]{2,1,0:T(8,128)(2,1)S(1)}, u32[]{:S(2)}, u32[]{:S(2)}) async-start(bf16[8,192,256]{2,1,0:T(8,128)(2,1)} %get-tuple-element.16), calls=%async_computation | async-start | bytes 1572864 | tf_op jit(solution)/shard_map/all_to_all | solution.py:228
  10.2 0.0 copy-done.5
  10.2 12.3 %collective-permute-start = (bf16[64,256]{1,0:T(8,128)(2,1)S(1)}, bf16[64,256]{1,0:T(8,128)(2,1)S(1)}, u32[]{:S(2)}, u32[]{:S(2)}) collective-permute-start(bf16[64,256]{1,0:T(8,128)(2,1)S(1)} %copy-done.5), channel_id=1, source_target_pairs={{0,8},{8,0},{1,9},{9,1},{2,10},{10,2},{3,11},{11,3},{4,12},{12,4},... | collective-permute-start | bytes 98312 | tf_op jit(solution)/shard_map/ppermute | solution.py:211
  22.5 0.0 copy-done.4
  22.5 1.9 %collective-permute-start.1 = (bf16[64,256]{1,0:T(8,128)(2,1)S(1)}, bf16[64,256]{1,0:T(8,128)(2,1)S(1)}, u32[]{:S(2)}, u32[]{:S(2)}) collective-permute-start(bf16[64,256]{1,0:T(8,128)(2,1)S(1)} %copy-done.4), channel_id=1, source_target_pairs={{8,16},{24,32},{40,48},{56,64},{72,80},{88,96},{104,112},{120,128}... | collective-permute-start | bytes 98312 | tf_op jit(solution)/shard_map/ppermute | solution.py:212
  24.4 0.0 collective-permute-done
  24.5 3.6 %collective-permute-done.1 = bf16[64,256]{1,0:T(8,128)(2,1)S(1)} collective-permute-done((bf16[64,256]{1,0:T(8,128)(2,1)S(1)}, bf16[64,256]{1,0:T(8,128)(2,1)S(1)}, u32[]{:S(2)}, u32[]{:S(2)}) %collective-permute-start.1) | collective-permute-done | bytes 32800 | tf_op jit(solution)/shard_map/ppermute | solution.py:212
  28.0 0.0 slice-done
  28.1 24.5 %all-gather = bf16[1536,256]{1,0:T(8,128)(2,1)} all-gather(bf16[192,256]{1,0:T(8,128)(2,1)S(1)} %pad_maximum_fusion), channel_id=2, replica_groups=mesh['zh'=4,'zl'=2,'y'=8,'c'=2,'x'=8] {'x'}, dimensions={0}, use_global_device_ids=true | all-gather | bytes 884736 | tf_op jit(solution)/shard_map/all_gather | solution.py:230
  52.6 0.0 all-to-all-done.own_hbm
  52.6 0.0 copy-start.3
  52.6 0.9 copy-done.3
  53.5 7.2 %shard_map.104 = (bf16[32,16,128]{2,1,0:T(8,128)(2,1)}, bf16[8,528,128]{2,1,0:T(8,128)(2,1)}) custom-call(s32[1]{0:T(128)} %bitcast.core, s32[64]{0:T(128)} %rows.1, s32[64]{0:T(128)} %cols.1, bf16[64,128,128]{2,1,0:T(8,128)(2,1)} %tiles_hbm.1, bf16[8,192,256]{2,1,0:T(8,128)(2,1)} %copy-done.3, bf16[8,192,256]{2,1,0:T(8,128)(2,1)} %bitcast.8, ...), custom_call_target="tpu_custom_call" | custom-call | tf_op jit(solution)/shard_map/pallas_call | solution.py:232
  60.7 19.4 %all_to_all.20.parts = bf16[32,16,128]{2,1,0:T(8,128)(2,1)S(1)} all-to-all(bf16[32,16,128]{2,1,0:T(8,128)(2,1)} %get-tuple-element.19), channel_id=1, replica_groups=mesh['zh'=4,'zl'=2,'y'=8,'c'=2,'x'=8] {'zl','c','x'}, dimensions={0} | all-to-all | bytes 262144 | tf_op jit(solution)/shard_map/all_to_all | solution.py:250
  80.1 3.6 %all-to-all-start.3 = ((bf16[8,528,128]{2,1,0:T(8,128)(2,1)}), bf16[8,528,128]{2,1,0:T(8,128)(2,1)S(1)}, u32[]{:S(2)}, u32[]{:S(2)}) async-start(bf16[8,528,128]{2,1,0:T(8,128)(2,1)} %get-tuple-element.22), calls=%async_computation.3 | async-start | bytes 2162688 | tf_op jit(solution)/shard_map/all_to_all | solution.py:259
  83.7 0.0 copy-start
  83.7 0.0 copy-start.1
  83.7 0.0 copy-start.2
  83.7 15.8 %psum.14 = f32[16,128]{1,0:T(8,128)S(1)} all-reduce(f32[16,128]{1,0:T(8,128)S(1)} %shard_map.105), channel_id=1, replica_groups=mesh['zh'=4,'zl'=2,'y'=8,'c'=2,'x'=8] {'y'}, use_global_device_ids=true, to_apply=%region_0.0 | all-reduce | flops 2048 | bytes 16384 | tf_op jit(solution)/shard_map/psum | solution.py:260
  99.5 22.4 %psum.15 = bf16[16,128]{1,0:T(8,128)(2,1)S(1)} all-reduce(f32[16,128]{1,0:T(8,128)S(1)} %psum.14), channel_id=1, replica_groups=mesh['zh'=4,'zl'=2,'y'=8,'c'=2,'x'=8] {'zh'}, use_global_device_ids=true, to_apply=%region_1.0 | all-reduce | flops 2048 | bytes 12288 | tf_op jit(solution)/shard_map/psum | solution.py:260
  121.9 0.0 all-to-all-done.3.parts
  122.0 0.7 broadcast_in_dim.2
  122.6 13.1 %all-to-all-start.2 = ((bf16[32,16,128]{2,1,0:T(8,128)(2,1)}), bf16[32,16,128]{2,1,0:T(8,128)(2,1)S(1)}, u32[]{:S(2)}, u32[]{:S(2)}) async-start(bf16[32,16,128]{2,1,0:T(8,128)(2,1)} %broadcast_in_dim.2), calls=%async_computation.2 | async-start | bytes 262144 | tf_op jit(solution)/shard_map/all_to_all | solution.py:262
  135.7 0.1 shard_map.106
  135.9 1.9 %collective-permute-start.3 = (bf16[176,128]{1,0:T(8,128)(2,1)S(1)}, bf16[176,128]{1,0:T(8,128)(2,1)S(1)}, u32[]{:S(2)}, u32[]{:S(2)}) collective-permute-start(bf16[176,128]{1,0:T(8,128)(2,1)S(1)} %get-tuple-element.24), channel_id=1, source_target_pairs={{8,16},{24,32},{40,48},{56,64},{72,80},{88,96},{104,112},{120,128}... | collective-permute-start | bytes 135176 | tf_op jit(solution)/shard_map/ppermute | solution.py:212
  137.8 1.9 %collective-permute-start.2 = (bf16[176,128]{1,0:T(8,128)(2,1)S(1)}, bf16[176,128]{1,0:T(8,128)(2,1)S(1)}, u32[]{:S(2)}, u32[]{:S(2)}) collective-permute-start(bf16[176,128]{1,0:T(8,128)(2,1)S(1)} %get-tuple-element.24), channel_id=1, source_target_pairs={{0,8},{8,0},{1,9},{9,1},{2,10},{10,2},{3,11},{11,3},{4,12},{12,4},... | collective-permute-start | bytes 135176 | tf_op jit(solution)/shard_map/ppermute | solution.py:211
  139.7 1.8 %collective-permute-done.3.outside = bf16[176,128]{1,0:T(8,128)(2,1)S(1)} collective-permute-done((bf16[176,128]{1,0:T(8,128)(2,1)S(1)}, bf16[176,128]{1,0:T(8,128)(2,1)S(1)}, u32[]{:S(2)}, u32[]{:S(2)}) %collective-permute-start.3) | collective-permute-done | bytes 45088 | tf_op jit(solution)/shard_map/ppermute | solution.py:212
  141.5 0.0 collective-permute-done.2.partner
  141.6 0.0 copy-done
  141.6 0.0 copy-done.1
  141.6 0.0 copy-done.2
  141.6 1.7 %shard_map.107 = bf16[256,256]{1,0:T(8,128)(2,1)} custom-call(s32[1]{0:T(128)} %bitcast.core, s32[2]{0:T(128)S(1)} %copy-done.2, s32[2,64]{1,0:T(2,128)S(1)} %copy-done.1, f32[352,128]{1,0:T(8,128)S(1)} %get-tuple-element.23.own, bf16[176,128]{1,0:T(8,128)(2,1)S(1)} %collective-permute-done.2.partner, bf16[176,128]{1,0:T(8,128)(2,1)S(1)} %collective-permute-done.3.outside, ...), custom_call_target="tpu_custom_call" | custom-call | tf_op jit(solution)/shard_map/pallas_call | solution.py:271
  143.3 2.2 %all-to-all-done.2.refs_0_ = bf16[32,16,128]{2,1,0:T(8,128)(2,1)S(1)} async-done(((bf16[32,16,128]{2,1,0:T(8,128)(2,1)}), bf16[32,16,128]{2,1,0:T(8,128)(2,1)S(1)}, u32[]{:S(2)}, u32[]{:S(2)}) %all-to-all-start.2) | async-done | bytes 131104 | tf_op jit(solution)/shard_map/all_to_all | solution.py:262
  145.4 0.7 shard_map.108
  (2 shorter events, 0.0 us)
Async XLA Ops:
  0.6 27.4 %slice-start = ((bf16[256,256]{1,0:T(8,128)(2,1)}), bf16[64,256]{1,0:T(8,128)(2,1)S(1)}, s32[]{:S(2)}) async-start(bf16[256,256]{1,0:T(8,128)(2,1)} %features.1), calls=%async_computation.4 | async-start | bytes 65536 | tf_op jit(solution)/shard_map/slice | solution.py:229
  2.7 7.4 %copy-start.5 = (bf16[64,256]{1,0:T(8,128)(2,1)S(1)}, bf16[64,256]{1,0:T(8,128)(2,1)}, u32[]{:S(2)}) copy-start(bf16[64,256]{1,0:T(8,128)(2,1)} %get-tuple-element.17) | copy-start | bytes 98308
  2.7 19.8 %copy-start.4 = (bf16[64,256]{1,0:T(8,128)(2,1)S(1)}, bf16[64,256]{1,0:T(8,128)(2,1)}, u32[]{:S(2)}) copy-start(bf16[64,256]{1,0:T(8,128)(2,1)} %get-tuple-element.18) | copy-start | bytes 98308
  2.7 49.9 %all-to-all-start = ((bf16[8,192,256]{2,1,0:T(8,128)(2,1)}), bf16[8,192,256]{2,1,0:T(8,128)(2,1)S(1)}, u32[]{:S(2)}, u32[]{:S(2)}) async-start(bf16[8,192,256]{2,1,0:T(8,128)(2,1)} %get-tuple-element.16), calls=%async_computation | async-start | bytes 1572864 | tf_op jit(solution)/shard_map/all_to_all | solution.py:228
  10.2 14.3 %collective-permute-start = (bf16[64,256]{1,0:T(8,128)(2,1)S(1)}, bf16[64,256]{1,0:T(8,128)(2,1)S(1)}, u32[]{:S(2)}, u32[]{:S(2)}) collective-permute-start(bf16[64,256]{1,0:T(8,128)(2,1)S(1)} %copy-done.5), channel_id=1, source_target_pairs={{0,8},{8,0},{1,9},{9,1},{2,10},{10,2},{3,11},{11,3},{4,12},{12,4},... | collective-permute-start | bytes 98312 | tf_op jit(solution)/shard_map/ppermute | solution.py:211
  22.5 5.5 %collective-permute-start.1 = (bf16[64,256]{1,0:T(8,128)(2,1)S(1)}, bf16[64,256]{1,0:T(8,128)(2,1)S(1)}, u32[]{:S(2)}, u32[]{:S(2)}) collective-permute-start(bf16[64,256]{1,0:T(8,128)(2,1)S(1)} %copy-done.4), channel_id=1, source_target_pairs={{8,16},{24,32},{40,48},{56,64},{72,80},{88,96},{104,112},{120,128}... | collective-permute-start | bytes 98312 | tf_op jit(solution)/shard_map/ppermute | solution.py:212
  52.6 0.9 copy-start.3
  80.1 41.9 %all-to-all-start.3 = ((bf16[8,528,128]{2,1,0:T(8,128)(2,1)}), bf16[8,528,128]{2,1,0:T(8,128)(2,1)S(1)}, u32[]{:S(2)}, u32[]{:S(2)}) async-start(bf16[8,528,128]{2,1,0:T(8,128)(2,1)} %get-tuple-element.22), calls=%async_computation.3 | async-start | bytes 2162688 | tf_op jit(solution)/shard_map/all_to_all | solution.py:259
  83.7 57.9 %copy-start = (bf16[256,172]{0,1:T(8,128)(2,1)S(1)}, bf16[256,172]{0,1:T(8,128)(2,1)}, u32[]{:S(2)}) copy-start(bf16[256,172]{0,1:T(8,128)(2,1)} %param.9) | copy-start | bytes 264196
  83.7 57.9 %copy-start.1 = (s32[2,64]{1,0:T(2,128)S(1)}, s32[2,64]{1,0:T(2,128)}, u32[]{:S(2)}) copy-start(s32[2,64]{1,0:T(2,128)} %send_lists.3) | copy-start | bytes 1540
  83.7 57.9 %copy-start.2 = (s32[2]{0:T(128)S(1)}, s32[2]{0:T(128)}, u32[]{:S(2)}) copy-start(s32[2]{0:T(128)} %counts.3) | copy-start | bytes 28
  122.6 22.8 %all-to-all-start.2 = ((bf16[32,16,128]{2,1,0:T(8,128)(2,1)}), bf16[32,16,128]{2,1,0:T(8,128)(2,1)S(1)}, u32[]{:S(2)}, u32[]{:S(2)}) async-start(bf16[32,16,128]{2,1,0:T(8,128)(2,1)} %broadcast_in_dim.2), calls=%async_computation.2 | async-start | bytes 262144 | tf_op jit(solution)/shard_map/all_to_all | solution.py:262
  135.9 5.7 %collective-permute-start.3 = (bf16[176,128]{1,0:T(8,128)(2,1)S(1)}, bf16[176,128]{1,0:T(8,128)(2,1)S(1)}, u32[]{:S(2)}, u32[]{:S(2)}) collective-permute-start(bf16[176,128]{1,0:T(8,128)(2,1)S(1)} %get-tuple-element.24), channel_id=1, source_target_pairs={{8,16},{24,32},{40,48},{56,64},{72,80},{88,96},{104,112},{120,128}... | collective-permute-start | bytes 135176 | tf_op jit(solution)/shard_map/ppermute | solution.py:212
  137.8 3.7 %collective-permute-start.2 = (bf16[176,128]{1,0:T(8,128)(2,1)S(1)}, bf16[176,128]{1,0:T(8,128)(2,1)S(1)}, u32[]{:S(2)}, u32[]{:S(2)}) collective-permute-start(bf16[176,128]{1,0:T(8,128)(2,1)S(1)} %get-tuple-element.24), channel_id=1, source_target_pairs={{0,8},{8,0},{1,9},{9,1},{2,10},{10,2},{3,11},{11,3},{4,12},{12,4},... | collective-permute-start | bytes 135176 | tf_op jit(solution)/shard_map/ppermute | solution.py:211

commit v7 on v5

--- a/solution.py
+++ b/solution.py
@@ -150,7 +150,10 @@
     out[...] = jnp.broadcast_to(summed.astype(out.dtype), out.shape)
 
 
-def rows_kernel(core, counts, send_lists, own, partner, outside, weight, out):
+def last_kernel(
+    scale, core, counts, send_lists, own, partner, outside, weight, parts,
+    out, weight_grad, loss,
+):
     padded = partner.shape[0]
     even = core[0] == 0
     before = jnp.where(even, outside[...], partner[...])
@@ -158,16 +161,13 @@
     classes = weight.shape[0]
     first, second = slots_onehot(counts, send_lists, out.shape[0])
     send = send_lists.shape[1]
-    total = jnp.concatenate([own[0], own[1]], axis=1)
+    total = own[...]
     total += dot(before[:, send:], first, LAST)
     total += dot(after[:, :send], second, LAST)
     grad = total[:classes].astype(BF16)
     out[...] = dot(grad, weight[...], FIRST).astype(BF16)
 
-
-def last_kernel(scale, parts, weight_grad, loss):
-    classes = weight_grad.shape[0]
-    pieces = round_up(classes + 1, PIECE) // PIECE
+    pieces = padded // PIECE
     gathered = jnp.concatenate(
         [
             jnp.concatenate([parts[pieces * h + q].astype(F32) for q in range(pieces)], axis=0)
@@ -254,23 +254,26 @@
     weight_parts = lax.all_to_all(weight_parts, NEAR, 0, 0, tiled=True)
 
     halo = own[2].astype(BF16)
-    grad_features = pl.pallas_call(
-        rows_kernel,
-        out_shape=shape((nodes, hidden), BF16),
-        in_specs=[smem(), smem()] + [vmem()] * 5,
-        out_specs=vmem(),
+    scale = 1.0 / (domains * reps * nodes)
+    grad_features, weight_grad, loss = pl.pallas_call(
+        lambda *refs: last_kernel(scale, *refs),
+        out_shape=(
+            shape((nodes, hidden), BF16),
+            shape((classes, hidden), F32),
+            shape((1, 1), F32),
+        ),
+        in_specs=[smem(), smem()] + [vmem()] * 6,
+        out_specs=(vmem(),) * 3,
         compiler_params=params(4),
-    )(core, counts, send_lists, own, *exchange(halo, halo), weight)
-    weight_parts, grad_features = lax.optimization_barrier((weight_parts, grad_features))
-
-    scale = 1.0 / (domains * reps * nodes)
-    weight_grad, loss = pl.pallas_call(
-        lambda *refs: last_kernel(scale, *refs),
-        out_shape=(shape((classes, hidden), F32), shape((1, 1), F32)),
-        in_specs=[vmem()],
-        out_specs=(vmem(),) * 2,
-        compiler_params=params(4),
-    )(weight_parts)
+    )(
+        core,
+        counts,
+        send_lists,
+        jnp.concatenate([own[0], own[1]], axis=1),
+        *exchange(halo, halo),
+        weight,
+        weight_parts,
+    )
     return grad_features, weight_grad.T, loss.reshape(())
 
 

time: 142 us -> 141 us (level)
    pallas_call x1 -> x0, Pallas kernels: 1.69 us -> none  [per_device(): pl.pallas_call(rows_kernel, out_shape=shape((nodes, hidden), BF16), in_sp...]
  transfers between devices with their start and end apart: 7 -> 7, of which waited for: 4 -> 3; matrix products, arithmetic and copies ran while one was open for 1% -> 1% of each run, Pallas kernels for 3% -> 2%
where the time goes in v7:
time: 141 us; the launch traced here: 140 us
  blocking collectives  66.1 us (47%)
  starting transfers between devices  31.2 us (22%)
  waiting for transfers between devices  14.5 us (10%)
  between operations  14.2 us (10%)
  Pallas kernels  11.7 us (8%)
  local copies, waits for them, and re-layouts  2.7 us (2%)
    all_gather x1, blocking collectives, per_device(): halo_rows = lax.all_gather(halo, 'x', axis=0)  22.6 us
    all_to_all x1, blocking collectives, per_device(): weight_parts = lax.all_to_all(weight_parts, FAR, 0, 0, tiled=True)  22.4 us
    all_to_all x1, blocking collectives, per_device(): weight_parts = lax.all_to_all(weight_parts, NEAR, 0, 0, tiled=True)  21.1 us
    ppermute x2, starting transfers between devices, exchange(): lax.ppermute(to_partner, 'c', [(0, 1), (1, 0)])  18 us
    all_gather x1, waiting for transfers between devices, per_device(): own_rows = lax.all_gather(features, 'x', axis=0, tiled=True)  8.85 us
    pallas_call x1, Pallas kernels, per_device(): pl.pallas_call(layer_kernel, out_shape=(shape((lax.axis_size(NEAR), PIECE...  7.45 us
    all_to_all x1, starting transfers between devices, per_device(): weight_parts = lax.all_to_all(weight_parts, NEAR, 0, 0, tiled=True)  7.1 us
    ppermute x2, starting transfers between devices, exchange(): lax.ppermute(to_outside, dom, outer)  6.08 us
  transfers between devices with their start and end apart: 7, of which 3 were waited for; matrix products, arithmetic and copies ran while one was open for 1% of the time, Pallas kernels for 2%

profile of v7, /device:TPU:1, one launch (start us, length us, event | category | flops | bytes accessed | tf_op | source)
XLA Modules:
  0.0 140.4 jit_solution(11989516560360710663)
XLA Ops:
  7.2 0.0 all-gather.3.cloned.1.call-start
  7.2 0.7 all-gather.3.cloned.1.call-update
  7.9 0.0 reduce-scatter.2.cloned.1.call-start
  7.9 1.8 %shard_map.103 = (bf16[64,256]{1,0:T(8,128)(2,1)}, bf16[64,256]{1,0:T(8,128)(2,1)}) custom-call(s32[1]{0:T(128)} %bitcast.core.refs_0_, s32[2]{0:T(128)} %refs_1_.1, s32[2,64]{1,0:T(2,128)} %refs_2_.1, bf16[256,256]{1,0:T(8,128)(2,1)} %features.1), custom_call_target="tpu_custom_call" | custom-call | tf_op jit(solution)/shard_map/pallas_call | solution.py:204
  9.7 16.0 %collective-permute-start = (bf16[64,256]{1,0:T(8,128)(2,1)}, bf16[64,256]{1,0:T(8,128)(2,1)S(1)}, u32[]{:S(2)}, u32[]{:S(2)}) collective-permute-start(bf16[64,256]{1,0:T(8,128)(2,1)} %get-tuple-element.10), channel_id=1, source_target_pairs={{0,8},{8,0},{1,9},{9,1},{2,10},{10,2},{3,11},{11,3},{4,12},{12,4},... | collective-permute-start | bytes 98312 | tf_op jit(solution)/shard_map/ppermute | solution.py:197
  25.8 1.9 %collective-permute-start.1 = (bf16[64,256]{1,0:T(8,128)(2,1)}, bf16[64,256]{1,0:T(8,128)(2,1)S(1)}, u32[]{:S(2)}, u32[]{:S(2)}) collective-permute-start(bf16[64,256]{1,0:T(8,128)(2,1)} %get-tuple-element.11), channel_id=1, source_target_pairs={{8,16},{24,32},{40,48},{56,64},{72,80},{88,96},{104,112},{120,128}... | collective-permute-start | bytes 98312 | tf_op jit(solution)/shard_map/ppermute | solution.py:198
  27.7 0.0 collective-permute-done
  27.7 3.7 %collective-permute-done.1 = bf16[64,256]{1,0:T(8,128)(2,1)S(1)} collective-permute-done((bf16[64,256]{1,0:T(8,128)(2,1)}, bf16[64,256]{1,0:T(8,128)(2,1)S(1)}, u32[]{:S(2)}, u32[]{:S(2)}) %collective-permute-start.1) | collective-permute-done | bytes 32800 | tf_op jit(solution)/shard_map/ppermute | solution.py:198
  31.5 22.6 %all-gather = bf16[1024,256]{1,0:T(8,128)(2,1)} all-gather(bf16[128,256]{1,0:T(8,128)(2,1)S(1)} %pad_maximum_fusion.1), channel_id=2, replica_groups=mesh['zh'=4,'zl'=2,'y'=8,'c'=2,'x'=8] {'x'}, dimensions={0}, use_global_device_ids=true | all-gather | bytes 589824 | tf_op jit(solution)/shard_map/all_gather | solution.py:212
  54.0 8.9 %all-gather.3.cloned.1.call-done = bf16[2048,256]{1,0:T(8,128)(2,1)} async-done(((bf16[256,256]{1,0:T(8,128)(2,1)}), bf16[2048,256]{1,0:T(8,128)(2,1)}) %all-gather.3.cloned.1.call-update) | async-done | bytes 1048592 | tf_op jit(solution)/shard_map/all_gather | solution.py:211
  62.9 7.4 %shard_map.104 = (bf16[32,16,128]{2,1,0:T(8,128)(2,1)}, f32[24,176,128]{2,1,0:T(8,128)}) custom-call(s32[1]{0:T(128)} %bitcast.core.refs_0_, s32[64]{0:T(128)} %rows.1, s32[64]{0:T(128)} %cols.1, bf16[64,128,128]{2,1,0:T(8,128)(2,1)} %tiles_hbm.1, bf16[8,2,128,256]{3,2,1,0:T(8,128)(2,1)} %bitcast.16, bf16[8,128,256]{2,1,0:T(8,128)(2,1)} %bitcast.15, ...), custom_call_target="tpu_custom_call" | custom-call | tf_op jit(solution)/shard_map/pallas_call | solution.py:214
  70.3 0.0 copy-start.3
  70.3 0.0 copy-start
  70.3 0.0 copy-start.1
  70.4 0.0 copy-start.2
  70.4 0.0 reduce-scatter.2.cloned.1.call-update
  70.4 0.8 copy-done.3
  71.2 21.1 %all_to_all.15.parts = bf16[32,16,128]{2,1,0:T(8,128)(2,1)S(1)} all-to-all(bf16[32,16,128]{2,1,0:T(8,128)(2,1)S(1)} %copy-done.3), channel_id=1, replica_groups=mesh['zh'=4,'zl'=2,'y'=8,'c'=2,'x'=8] {'zl','y','c'}, dimensions={0} | all-to-all | bytes 262144 | tf_op jit(solution)/shard_map/all_to_all | solution.py:250
  92.4 22.4 %all_to_all.16.parts = bf16[32,16,128]{2,1,0:T(8,128)(2,1)S(1)} all-to-all(bf16[32,16,128]{2,1,0:T(8,128)(2,1)S(1)} %shard_map.105), channel_id=1, replica_groups=mesh['zh'=4,'zl'=2,'y'=8,'c'=2,'x'=8] {'zh','x'}, dimensions={0} | all-to-all | bytes 262144 | tf_op jit(solution)/shard_map/all_to_all | solution.py:252
  114.8 0.7 shard_map.106
  115.5 7.1 %all-to-all-start.2 = ((bf16[32,16,128]{2,1,0:T(8,128)(2,1)}), bf16[32,16,128]{2,1,0:T(8,128)(2,1)S(1)}, u32[]{:S(2)}, u32[]{:S(2)}) async-start(bf16[32,16,128]{2,1,0:T(8,128)(2,1)} %shard_map.106), calls=%async_computation.3 | async-start | bytes 262144 | tf_op jit(solution)/shard_map/all_to_all | solution.py:254
  122.6 0.0 reduce-scatter.2.cloned.1.call-done
  122.7 0.9 fusion
  123.6 4.2 %collective-permute-start.3 = (bf16[176,128]{1,0:T(8,128)(2,1)S(1)}, bf16[176,128]{1,0:T(8,128)(2,1)S(1)}, u32[]{:S(2)}, u32[]{:S(2)}) collective-permute-start(bf16[176,128]{1,0:T(8,128)(2,1)S(1)} %fusion), channel_id=1, source_target_pairs={{8,16},{24,32},{40,48},{56,64},{72,80},{88,96},{104,112},{120,128}... | collective-permute-start | bytes 135176 | tf_op jit(solution)/shard_map/ppermute | solution.py:198
  127.7 1.9 %collective-permute-start.2 = (bf16[176,128]{1,0:T(8,128)(2,1)S(1)}, bf16[176,128]{1,0:T(8,128)(2,1)S(1)}, u32[]{:S(2)}, u32[]{:S(2)}) collective-permute-start(bf16[176,128]{1,0:T(8,128)(2,1)S(1)} %fusion), channel_id=1, source_target_pairs={{0,8},{8,0},{1,9},{9,1},{2,10},{10,2},{3,11},{11,3},{4,12},{12,4},... | collective-permute-start | bytes 135176 | tf_op jit(solution)/shard_map/ppermute | solution.py:197
  129.7 0.9 slice_bitcast_fusion.1
  130.6 1.2 all-to-all-done.2.refs_7_
  131.8 0.0 collective-permute-done.3.refs_5_
  131.8 0.0 collective-permute-done.2.refs_4_
  131.8 0.0 copy-done
  131.8 0.0 copy-done.1
  131.8 0.0 copy-done.2
  131.8 1.7 %shard_map.107 = (bf16[256,256]{1,0:T(8,128)(2,1)}, f32[172,256]{1,0:T(8,128)}, f32[1,1]{1,0:T(1,128)}) custom-call(s32[1]{0:T(128)} %bitcast.core.refs_0_, s32[2]{0:T(128)S(1)} %copy-done.2, s32[2,64]{1,0:T(2,128)S(1)} %copy-done.1, f32[176,256]{1,0:T(8,128)S(1)} %pad_maximum_fusion.refs_3_, bf16[176,128]{1,0:T(8,128)(2,1)S(1)} %collective-permute-done.2.refs_4_, ...), custom_call_target="tpu_custom_call" | custom-call | tf_op jit(solution)/shard_map/pallas_call | solution.py:258
  (3 shorter events, 0.1 us)
Async XLA Ops:
  7.2 55.7 %all-gather.3.cloned.1.call-start = ((), (), s32[]{:S(2)}) async-start(), calls=%async_computation.4 | async-start | bytes 1179648 | tf_op jit(solution)/shard_map/all_gather | solution.py:211
  7.9 114.8 %reduce-scatter.2.cloned.1.call-start = ((), (), s32[]{:S(2)}) async-start(), calls=%async_computation.5 | async-start | bytes 2433024 | tf_op jit(solution)/shard_map/reduce_scatter | solution.py:249
  9.7 18.0 %collective-permute-start = (bf16[64,256]{1,0:T(8,128)(2,1)}, bf16[64,256]{1,0:T(8,128)(2,1)S(1)}, u32[]{:S(2)}, u32[]{:S(2)}) collective-permute-start(bf16[64,256]{1,0:T(8,128)(2,1)} %get-tuple-element.10), channel_id=1, source_target_pairs={{0,8},{8,0},{1,9},{9,1},{2,10},{10,2},{3,11},{11,3},{4,12},{12,4},... | collective-permute-start | bytes 98312 | tf_op jit(solution)/shard_map/ppermute | solution.py:197
  25.8 5.7 %collective-permute-start.1 = (bf16[64,256]{1,0:T(8,128)(2,1)}, bf16[64,256]{1,0:T(8,128)(2,1)S(1)}, u32[]{:S(2)}, u32[]{:S(2)}) collective-permute-start(bf16[64,256]{1,0:T(8,128)(2,1)} %get-tuple-element.11), channel_id=1, source_target_pairs={{8,16},{24,32},{40,48},{56,64},{72,80},{88,96},{104,112},{120,128}... | collective-permute-start | bytes 98312 | tf_op jit(solution)/shard_map/ppermute | solution.py:198
  70.3 0.9 copy-start.3
  70.3 61.5 %copy-start = (bf16[256,172]{0,1:T(8,128)(2,1)S(1)}, bf16[256,172]{0,1:T(8,128)(2,1)}, u32[]{:S(2)}) copy-start(bf16[256,172]{0,1:T(8,128)(2,1)} %param.9) | copy-start | bytes 264196
  70.3 61.5 %copy-start.1 = (s32[2,64]{1,0:T(2,128)S(1)}, s32[2,64]{1,0:T(2,128)}, u32[]{:S(2)}) copy-start(s32[2,64]{1,0:T(2,128)} %refs_2_.1) | copy-start | bytes 1540
  70.4 61.5 %copy-start.2 = (s32[2]{0:T(128)S(1)}, s32[2]{0:T(128)}, u32[]{:S(2)}) copy-start(s32[2]{0:T(128)} %refs_1_.1) | copy-start | bytes 28
  115.5 16.3 %all-to-all-start.2 = ((bf16[32,16,128]{2,1,0:T(8,128)(2,1)}), bf16[32,16,128]{2,1,0:T(8,128)(2,1)S(1)}, u32[]{:S(2)}, u32[]{:S(2)}) async-start(bf16[32,16,128]{2,1,0:T(8,128)(2,1)} %shard_map.106), calls=%async_computation.3 | async-start | bytes 262144 | tf_op jit(solution)/shard_map/all_to_all | solution.py:254
  123.6 8.2 %collective-permute-start.3 = (bf16[176,128]{1,0:T(8,128)(2,1)S(1)}, bf16[176,128]{1,0:T(8,128)(2,1)S(1)}, u32[]{:S(2)}, u32[]{:S(2)}) collective-permute-start(bf16[176,128]{1,0:T(8,128)(2,1)S(1)} %fusion), channel_id=1, source_target_pairs={{8,16},{24,32},{40,48},{56,64},{72,80},{88,96},{104,112},{120,128}... | collective-permute-start | bytes 135176 | tf_op jit(solution)/shard_map/ppermute | solution.py:198
  127.7 4.1 %collective-permute-start.2 = (bf16[176,128]{1,0:T(8,128)(2,1)S(1)}, bf16[176,128]{1,0:T(8,128)(2,1)S(1)}, u32[]{:S(2)}, u32[]{:S(2)}) collective-permute-start(bf16[176,128]{1,0:T(8,128)(2,1)S(1)} %fusion), channel_id=1, source_target_pairs={{0,8},{8,0},{1,9},{9,1},{2,10},{10,2},{3,11},{11,3},{4,12},{12,4},... | collective-permute-start | bytes 135176 | tf_op jit(solution)/shard_map/ppermute | solution.py:197
Sparse Core Ops, SparseCore 0:
  10.7 52.1 all-gather.2
  70.5 49.1 reduce-scatter.1

commit v8 on v7

--- a/solution.py
+++ b/solution.py
@@ -13,7 +13,7 @@
 AXES = ("zh", "zl", "y", "c", "x")
 NEAR = ("zl", "y", "c")
 FAR = ("zh", "x")
-CHUNK = 16
+CHUNK = 32
 LAST = (((1,), (1,)), ((), ()))
 FIRST = (((0,), (0,)), ((), ()))
 PLAIN = (((1,), (0,)), ((), ()))
@@ -62,9 +62,9 @@
 
 
 def layer_kernel(
-    core, rows, cols, tiles_hbm, own_hbm, halo_hbm, weight, labels,
+    core, rows_hbm, cols_hbm, tiles_hbm, own_hbm, halo_hbm, weight_hbm, labels_hbm,
     weight_out, grads,
-    tiles, columns, sums, sems,
+    rows, cols, tiles, columns, weight, labels, sums, small_sems, sems,
 ):
     count, tile = tiles.shape[0], tiles.shape[1]
     classes, hidden = weight.shape
@@ -74,6 +74,10 @@
     partner_at = pl.multiple_of(send * (1 - core[0]), send)
     outside_at = pl.multiple_of(send * core[0], send)
     copies = [
+        pltpu.make_async_copy(rows_hbm, rows, small_sems.at[0]),
+        pltpu.make_async_copy(cols_hbm, cols, small_sems.at[1]),
+        pltpu.make_async_copy(weight_hbm, weight, small_sems.at[2]),
+        pltpu.make_async_copy(labels_hbm, labels, small_sems.at[3]),
         pltpu.make_async_copy(own_hbm, columns.at[:, 0:2], sems.at[0]),
         pltpu.make_async_copy(
             halo_hbm.at[:, :send], columns.at[:, 2, pl.ds(partner_at, send)], sems.at[1]
@@ -217,12 +221,17 @@
             shape((lax.axis_size(NEAR), PIECE, LANES), BF16),
             shape((3 * reps, padded, tile), F32),
         ),
-        in_specs=[smem(), smem(), smem(), hbm(), hbm(), hbm(), vmem(), vmem()],
+        in_specs=[smem()] + [hbm()] * 7,
         out_specs=(vmem(),) * 2,
         scratch_shapes=[
+            pltpu.SMEM((count,), jnp.int32),
+            pltpu.SMEM((count,), jnp.int32),
             pltpu.VMEM((count, tile, tile), BF16),
             pltpu.VMEM((reps, 3, tile, hidden), BF16),
+            pltpu.VMEM((classes, hidden), BF16),
+            pltpu.VMEM((1, nodes), jnp.int32),
             pltpu.VMEM((nodes, hidden), F32),
+            pltpu.SemaphoreType.DMA((4,)),
             pltpu.SemaphoreType.DMA((3 + count // CHUNK,)),
         ],
         compiler_params=params(56),

time: 141 us -> 140 us (level)
  no operation moved by 1% of the time
where the time goes in v8:
time: 140 us
  blocking collectives  66.2 us (47%)
  starting transfers between devices  31.1 us (22%)
  waiting for transfers between devices  14.6 us (10%)
  between operations  14.2 us (10%)
  Pallas kernels  10.8 us (8%)
  local copies, waits for them, and re-layouts  2.7 us (2%)
    all_gather x1, blocking collectives, per_device(): halo_rows = lax.all_gather(halo, 'x', axis=0)  22.6 us
    all_to_all x1, blocking collectives, per_device(): weight_parts = lax.all_to_all(weight_parts, FAR, 0, 0, tiled=True)  22.4 us
    all_to_all x1, blocking collectives, per_device(): weight_parts = lax.all_to_all(weight_parts, NEAR, 0, 0, tiled=True)  21.2 us
    ppermute x2, starting transfers between devices, exchange(): lax.ppermute(to_partner, 'c', [(0, 1), (1, 0)])  18 us
    all_gather x1, waiting for transfers between devices, per_device(): own_rows = lax.all_gather(features, 'x', axis=0, tiled=True)  8.85 us
    all_to_all x1, starting transfers between devices, per_device(): weight_parts = lax.all_to_all(weight_parts, NEAR, 0, 0, tiled=True)  7.11 us
    pallas_call x1, Pallas kernels, per_device(): pl.pallas_call(layer_kernel, out_shape=(shape((lax.axis_size(NEAR), PIECE...  6.57 us
    ppermute x2, starting transfers between devices, exchange(): lax.ppermute(to_outside, dom, outer)  5.99 us
  transfers between devices with their start and end apart: 7, of which 3 were waited for; matrix products, arithmetic and copies ran while one was open for 1% of the time, Pallas kernels for 2%

profile of v8, /device:TPU:1, one launch (start us, length us, event | category | flops | bytes accessed | tf_op | source)
XLA Modules:
  0.0 139.6 jit_solution(12843397127303210459)
XLA Ops:
  7.2 0.0 all-gather.3.cloned.1.call-start
  7.2 0.7 all-gather.3.cloned.1.call-update
  7.9 0.0 reduce-scatter.2.cloned.1.call-start
  7.9 1.8 %shard_map.103 = (bf16[64,256]{1,0:T(8,128)(2,1)}, bf16[64,256]{1,0:T(8,128)(2,1)}) custom-call(s32[1]{0:T(128)} %bitcast.core.refs_0_, s32[2]{0:T(128)} %refs_1_.1, s32[2,64]{1,0:T(2,128)} %refs_2_.1, bf16[256,256]{1,0:T(8,128)(2,1)} %features.1), custom_call_target="tpu_custom_call" | custom-call | tf_op jit(solution)/shard_map/pallas_call | solution.py:208
  9.7 16.0 %collective-permute-start = (bf16[64,256]{1,0:T(8,128)(2,1)}, bf16[64,256]{1,0:T(8,128)(2,1)S(1)}, u32[]{:S(2)}, u32[]{:S(2)}) collective-permute-start(bf16[64,256]{1,0:T(8,128)(2,1)} %get-tuple-element.10), channel_id=1, source_target_pairs={{0,8},{8,0},{1,9},{9,1},{2,10},{10,2},{3,11},{11,3},{4,12},{12,4},... | collective-permute-start | bytes 98312 | tf_op jit(solution)/shard_map/ppermute | solution.py:201
  25.8 1.9 %collective-permute-start.1 = (bf16[64,256]{1,0:T(8,128)(2,1)}, bf16[64,256]{1,0:T(8,128)(2,1)S(1)}, u32[]{:S(2)}, u32[]{:S(2)}) collective-permute-start(bf16[64,256]{1,0:T(8,128)(2,1)} %get-tuple-element.11), channel_id=1, source_target_pairs={{8,16},{24,32},{40,48},{56,64},{72,80},{88,96},{104,112},{120,128}... | collective-permute-start | bytes 98312 | tf_op jit(solution)/shard_map/ppermute | solution.py:202
  27.7 0.0 collective-permute-done
  27.7 3.7 %collective-permute-done.1 = bf16[64,256]{1,0:T(8,128)(2,1)S(1)} collective-permute-done((bf16[64,256]{1,0:T(8,128)(2,1)}, bf16[64,256]{1,0:T(8,128)(2,1)S(1)}, u32[]{:S(2)}, u32[]{:S(2)}) %collective-permute-start.1) | collective-permute-done | bytes 32800 | tf_op jit(solution)/shard_map/ppermute | solution.py:202
  31.5 22.6 %all-gather = bf16[1024,256]{1,0:T(8,128)(2,1)} all-gather(bf16[128,256]{1,0:T(8,128)(2,1)S(1)} %pad_maximum_fusion.1), channel_id=2, replica_groups=mesh['zh'=4,'zl'=2,'y'=8,'c'=2,'x'=8] {'x'}, dimensions={0}, use_global_device_ids=true | all-gather | bytes 589824 | tf_op jit(solution)/shard_map/all_gather | solution.py:216
  54.0 8.9 %all-gather.3.cloned.1.call-done = bf16[2048,256]{1,0:T(8,128)(2,1)} async-done(((bf16[256,256]{1,0:T(8,128)(2,1)}), bf16[2048,256]{1,0:T(8,128)(2,1)}) %all-gather.3.cloned.1.call-update) | async-done | bytes 1048592 | tf_op jit(solution)/shard_map/all_gather | solution.py:215
  62.9 6.6 %shard_map.104 = (bf16[32,16,128]{2,1,0:T(8,128)(2,1)}, f32[24,176,128]{2,1,0:T(8,128)}) custom-call(s32[1]{0:T(128)} %bitcast.core.refs_0_, s32[64]{0:T(128)} %rows_hbm.1, s32[64]{0:T(128)} %cols_hbm.1, bf16[64,128,128]{2,1,0:T(8,128)(2,1)} %tiles_hbm.1, bf16[8,2,128,256]{3,2,1,0:T(8,128)(2,1)} %bitcast.16, bf16[8,128,256]{2,1,0:T(8,128)(2,1)} %bitcast.15, ...), custom_call_target="tpu_custom_call" | custom-call | tf_op jit(solution)/shard_map/pallas_call | solution.py:218
  69.4 0.0 copy-start.3
  69.5 0.0 copy-start
  69.5 0.0 copy-start.1
  69.5 0.0 copy-start.2
  69.5 0.0 reduce-scatter.2.cloned.1.call-update
  69.5 0.8 copy-done.3
  70.4 21.2 %all_to_all.15.parts = bf16[32,16,128]{2,1,0:T(8,128)(2,1)S(1)} all-to-all(bf16[32,16,128]{2,1,0:T(8,128)(2,1)S(1)} %copy-done.3), channel_id=1, replica_groups=mesh['zh'=4,'zl'=2,'y'=8,'c'=2,'x'=8] {'zl','y','c'}, dimensions={0} | all-to-all | bytes 262144 | tf_op jit(solution)/shard_map/all_to_all | solution.py:259
  91.6 22.4 %all_to_all.16.parts = bf16[32,16,128]{2,1,0:T(8,128)(2,1)S(1)} all-to-all(bf16[32,16,128]{2,1,0:T(8,128)(2,1)S(1)} %shard_map.105), channel_id=1, replica_groups=mesh['zh'=4,'zl'=2,'y'=8,'c'=2,'x'=8] {'zh','x'}, dimensions={0} | all-to-all | bytes 262144 | tf_op jit(solution)/shard_map/all_to_all | solution.py:261
  114.0 0.7 shard_map.106
  114.7 7.1 %all-to-all-start.2 = ((bf16[32,16,128]{2,1,0:T(8,128)(2,1)}), bf16[32,16,128]{2,1,0:T(8,128)(2,1)S(1)}, u32[]{:S(2)}, u32[]{:S(2)}) async-start(bf16[32,16,128]{2,1,0:T(8,128)(2,1)} %shard_map.106), calls=%async_computation.3 | async-start | bytes 262144 | tf_op jit(solution)/shard_map/all_to_all | solution.py:263
  121.8 0.0 reduce-scatter.2.cloned.1.call-done
  121.9 0.9 fusion
  122.8 4.1 %collective-permute-start.3 = (bf16[176,128]{1,0:T(8,128)(2,1)S(1)}, bf16[176,128]{1,0:T(8,128)(2,1)S(1)}, u32[]{:S(2)}, u32[]{:S(2)}) collective-permute-start(bf16[176,128]{1,0:T(8,128)(2,1)S(1)} %fusion), channel_id=1, source_target_pairs={{8,16},{24,32},{40,48},{56,64},{72,80},{88,96},{104,112},{120,128}... | collective-permute-start | bytes 135176 | tf_op jit(solution)/shard_map/ppermute | solution.py:202
  126.8 1.9 %collective-permute-start.2 = (bf16[176,128]{1,0:T(8,128)(2,1)S(1)}, bf16[176,128]{1,0:T(8,128)(2,1)S(1)}, u32[]{:S(2)}, u32[]{:S(2)}) collective-permute-start(bf16[176,128]{1,0:T(8,128)(2,1)S(1)} %fusion), channel_id=1, source_target_pairs={{0,8},{8,0},{1,9},{9,1},{2,10},{10,2},{3,11},{11,3},{4,12},{12,4},... | collective-permute-start | bytes 135176 | tf_op jit(solution)/shard_map/ppermute | solution.py:201
  128.8 0.9 slice_bitcast_fusion.1
  129.7 1.2 all-to-all-done.2.refs_7_
  131.0 0.0 collective-permute-done.3.refs_5_
  131.0 0.0 collective-permute-done.2.refs_4_
  131.0 0.0 copy-done
  131.0 0.0 copy-done.1
  131.0 0.0 copy-done.2
  131.0 1.7 %shard_map.107 = (bf16[256,256]{1,0:T(8,128)(2,1)}, f32[172,256]{1,0:T(8,128)}, f32[1,1]{1,0:T(1,128)}) custom-call(s32[1]{0:T(128)} %bitcast.core.refs_0_, s32[2]{0:T(128)S(1)} %copy-done.2, s32[2,64]{1,0:T(2,128)S(1)} %copy-done.1, f32[176,256]{1,0:T(8,128)S(1)} %pad_maximum_fusion.refs_3_, bf16[176,128]{1,0:T(8,128)(2,1)S(1)} %collective-permute-done.2.refs_4_, ...), custom_call_target="tpu_custom_call" | custom-call | tf_op jit(solution)/shard_map/pallas_call | solution.py:267
  (3 shorter events, 0.1 us)
Async XLA Ops:
  7.2 55.7 %all-gather.3.cloned.1.call-start = ((), (), s32[]{:S(2)}) async-start(), calls=%async_computation.4 | async-start | bytes 1179648 | tf_op jit(solution)/shard_map/all_gather | solution.py:215
  7.9 113.9 %reduce-scatter.2.cloned.1.call-start = ((), (), s32[]{:S(2)}) async-start(), calls=%async_computation.5 | async-start | bytes 2433024 | tf_op jit(solution)/shard_map/reduce_scatter | solution.py:258
  9.7 18.0 %collective-permute-start = (bf16[64,256]{1,0:T(8,128)(2,1)}, bf16[64,256]{1,0:T(8,128)(2,1)S(1)}, u32[]{:S(2)}, u32[]{:S(2)}) collective-permute-start(bf16[64,256]{1,0:T(8,128)(2,1)} %get-tuple-element.10), channel_id=1, source_target_pairs={{0,8},{8,0},{1,9},{9,1},{2,10},{10,2},{3,11},{11,3},{4,12},{12,4},... | collective-permute-start | bytes 98312 | tf_op jit(solution)/shard_map/ppermute | solution.py:201
  25.8 5.7 %collective-permute-start.1 = (bf16[64,256]{1,0:T(8,128)(2,1)}, bf16[64,256]{1,0:T(8,128)(2,1)S(1)}, u32[]{:S(2)}, u32[]{:S(2)}) collective-permute-start(bf16[64,256]{1,0:T(8,128)(2,1)} %get-tuple-element.11), channel_id=1, source_target_pairs={{8,16},{24,32},{40,48},{56,64},{72,80},{88,96},{104,112},{120,128}... | collective-permute-start | bytes 98312 | tf_op jit(solution)/shard_map/ppermute | solution.py:202
  69.4 0.9 copy-start.3
  69.5 61.5 %copy-start = (bf16[256,172]{0,1:T(8,128)(2,1)S(1)}, bf16[256,172]{0,1:T(8,128)(2,1)}, u32[]{:S(2)}) copy-start(bf16[256,172]{0,1:T(8,128)(2,1)} %param.9) | copy-start | bytes 264196
  69.5 61.5 %copy-start.1 = (s32[2,64]{1,0:T(2,128)S(1)}, s32[2,64]{1,0:T(2,128)}, u32[]{:S(2)}) copy-start(s32[2,64]{1,0:T(2,128)} %refs_2_.1) | copy-start | bytes 1540
  69.5 61.5 %copy-start.2 = (s32[2]{0:T(128)S(1)}, s32[2]{0:T(128)}, u32[]{:S(2)}) copy-start(s32[2]{0:T(128)} %refs_1_.1) | copy-start | bytes 28
  114.7 16.3 %all-to-all-start.2 = ((bf16[32,16,128]{2,1,0:T(8,128)(2,1)}), bf16[32,16,128]{2,1,0:T(8,128)(2,1)S(1)}, u32[]{:S(2)}, u32[]{:S(2)}) async-start(bf16[32,16,128]{2,1,0:T(8,128)(2,1)} %shard_map.106), calls=%async_computation.3 | async-start | bytes 262144 | tf_op jit(solution)/shard_map/all_to_all | solution.py:263
  122.8 8.2 %collective-permute-start.3 = (bf16[176,128]{1,0:T(8,128)(2,1)S(1)}, bf16[176,128]{1,0:T(8,128)(2,1)S(1)}, u32[]{:S(2)}, u32[]{:S(2)}) collective-permute-start(bf16[176,128]{1,0:T(8,128)(2,1)S(1)} %fusion), channel_id=1, source_target_pairs={{8,16},{24,32},{40,48},{56,64},{72,80},{88,96},{104,112},{120,128}... | collective-permute-start | bytes 135176 | tf_op jit(solution)/shard_map/ppermute | solution.py:202
  126.8 4.2 %collective-permute-start.2 = (bf16[176,128]{1,0:T(8,128)(2,1)S(1)}, bf16[176,128]{1,0:T(8,128)(2,1)S(1)}, u32[]{:S(2)}, u32[]{:S(2)}) collective-permute-start(bf16[176,128]{1,0:T(8,128)(2,1)S(1)} %fusion), channel_id=1, source_target_pairs={{0,8},{8,0},{1,9},{9,1},{2,10},{10,2},{3,11},{11,3},{4,12},{12,4},... | collective-permute-start | bytes 135176 | tf_op jit(solution)/shard_map/ppermute | solution.py:201
Sparse Core Ops, SparseCore 0:
  10.7 52.1 all-gather.2
  69.6 49.0 reduce-scatter.1

commit v9 on v8

--- a/solution.py
+++ b/solution.py
@@ -11,8 +11,8 @@
 PIECE = 16
 SHAPE = (4, 2, 8, 2, 8)
 AXES = ("zh", "zl", "y", "c", "x")
-NEAR = ("zl", "y", "c")
-FAR = ("zh", "x")
+NEAR = ("zl", "c", "x")
+FAR = ("zh", "y")
 CHUNK = 32
 LAST = (((1,), (1,)), ((), ()))
 FIRST = (((0,), (0,)), ((), ()))

time: 140 us -> 139 us (level)
  starting transfers between devices: 31.1 us -> 29.6 us
    all_to_all x1, blocking collectives: 21.2 us -> 19.4 us  [per_device(): weight_parts = lax.all_to_all(weight_parts, NEAR, 0, 0, tiled=True)]
    all_to_all x1, blocking collectives: 22.4 us -> 24 us  [per_device(): weight_parts = lax.all_to_all(weight_parts, FAR, 0, 0, tiled=True)]
    all_to_all x1, starting transfers between devices: 7.11 us -> 5.66 us  [per_device(): weight_parts = lax.all_to_all(weight_parts, NEAR, 0, 0, tiled=True)]
where the time goes in v9:
time: 139 us
  blocking collectives  66 us (47%)
  starting transfers between devices  29.6 us (21%)
  waiting for transfers between devices  15.2 us (11%)
  between operations  14.2 us (10%)
  Pallas kernels  10.8 us (8%)
  local copies, waits for them, and re-layouts  2.7 us (2%)
    all_to_all x1, blocking collectives, per_device(): weight_parts = lax.all_to_all(weight_parts, FAR, 0, 0, tiled=True)  24 us
    all_gather x1, blocking collectives, per_device(): halo_rows = lax.all_gather(halo, 'x', axis=0)  22.6 us
    all_to_all x1, blocking collectives, per_device(): weight_parts = lax.all_to_all(weight_parts, NEAR, 0, 0, tiled=True)  19.4 us
    ppermute x2, starting transfers between devices, exchange(): lax.ppermute(to_partner, 'c', [(0, 1), (1, 0)])  18 us
    all_gather x1, waiting for transfers between devices, per_device(): own_rows = lax.all_gather(features, 'x', axis=0, tiled=True)  8.85 us
    pallas_call x1, Pallas kernels, per_device(): pl.pallas_call(layer_kernel, out_shape=(shape((lax.axis_size(NEAR), PIECE...  6.6 us
    ppermute x2, starting transfers between devices, exchange(): lax.ppermute(to_outside, dom, outer)  5.94 us
    all_to_all x1, starting transfers between devices, per_device(): weight_parts = lax.all_to_all(weight_parts, NEAR, 0, 0, tiled=True)  5.66 us
  transfers between devices with their start and end apart: 7, of which 3 were waited for; matrix products, arithmetic and copies ran while one was open for 1% of the time, Pallas kernels for 2%

profile of v9, /device:TPU:1, one launch (start us, length us, event | category | flops | bytes accessed | tf_op | source)
XLA Modules:
  0.0 138.5 jit_solution(7023537116907666012)
XLA Ops:
  7.2 0.0 all-gather.3.cloned.1.call-start
  7.2 0.7 all-gather.3.cloned.1.call-update
  7.9 0.0 reduce-scatter.2.cloned.1.call-start
  7.9 1.8 %shard_map.103 = (bf16[64,256]{1,0:T(8,128)(2,1)}, bf16[64,256]{1,0:T(8,128)(2,1)}) custom-call(s32[1]{0:T(128)} %bitcast.core.refs_0_, s32[2]{0:T(128)} %refs_1_.1, s32[2,64]{1,0:T(2,128)} %refs_2_.1, bf16[256,256]{1,0:T(8,128)(2,1)} %features.1), custom_call_target="tpu_custom_call" | custom-call | tf_op jit(solution)/shard_map/pallas_call | solution.py:208
  9.7 16.0 %collective-permute-start = (bf16[64,256]{1,0:T(8,128)(2,1)}, bf16[64,256]{1,0:T(8,128)(2,1)S(1)}, u32[]{:S(2)}, u32[]{:S(2)}) collective-permute-start(bf16[64,256]{1,0:T(8,128)(2,1)} %get-tuple-element.10), channel_id=1, source_target_pairs={{0,8},{8,0},{1,9},{9,1},{2,10},{10,2},{3,11},{11,3},{4,12},{12,4},... | collective-permute-start | bytes 98312 | tf_op jit(solution)/shard_map/ppermute | solution.py:201
  25.8 1.9 %collective-permute-start.1 = (bf16[64,256]{1,0:T(8,128)(2,1)}, bf16[64,256]{1,0:T(8,128)(2,1)S(1)}, u32[]{:S(2)}, u32[]{:S(2)}) collective-permute-start(bf16[64,256]{1,0:T(8,128)(2,1)} %get-tuple-element.11), channel_id=1, source_target_pairs={{8,16},{24,32},{40,48},{56,64},{72,80},{88,96},{104,112},{120,128}... | collective-permute-start | bytes 98312 | tf_op jit(solution)/shard_map/ppermute | solution.py:202
  27.7 0.0 collective-permute-done
  27.7 3.7 %collective-permute-done.1 = bf16[64,256]{1,0:T(8,128)(2,1)S(1)} collective-permute-done((bf16[64,256]{1,0:T(8,128)(2,1)}, bf16[64,256]{1,0:T(8,128)(2,1)S(1)}, u32[]{:S(2)}, u32[]{:S(2)}) %collective-permute-start.1) | collective-permute-done | bytes 32800 | tf_op jit(solution)/shard_map/ppermute | solution.py:202
  31.5 22.6 %all-gather = bf16[1024,256]{1,0:T(8,128)(2,1)} all-gather(bf16[128,256]{1,0:T(8,128)(2,1)S(1)} %pad_maximum_fusion.1), channel_id=2, replica_groups=mesh['zh'=4,'zl'=2,'y'=8,'c'=2,'x'=8] {'x'}, dimensions={0}, use_global_device_ids=true | all-gather | bytes 589824 | tf_op jit(solution)/shard_map/all_gather | solution.py:216
  54.0 8.9 %all-gather.3.cloned.1.call-done = bf16[2048,256]{1,0:T(8,128)(2,1)} async-done(((bf16[256,256]{1,0:T(8,128)(2,1)}), bf16[2048,256]{1,0:T(8,128)(2,1)}) %all-gather.3.cloned.1.call-update) | async-done | bytes 1048592 | tf_op jit(solution)/shard_map/all_gather | solution.py:215
  62.9 6.6 %shard_map.104 = (bf16[32,16,128]{2,1,0:T(8,128)(2,1)}, f32[24,176,128]{2,1,0:T(8,128)}) custom-call(s32[1]{0:T(128)} %bitcast.core.refs_0_, s32[64]{0:T(128)} %rows_hbm.1, s32[64]{0:T(128)} %cols_hbm.1, bf16[64,128,128]{2,1,0:T(8,128)(2,1)} %tiles_hbm.1, bf16[8,2,128,256]{3,2,1,0:T(8,128)(2,1)} %bitcast.16, bf16[8,128,256]{2,1,0:T(8,128)(2,1)} %bitcast.15, ...), custom_call_target="tpu_custom_call" | custom-call | tf_op jit(solution)/shard_map/pallas_call | solution.py:218
  69.5 0.0 copy-start.3
  69.5 0.0 copy-start
  69.5 0.0 copy-start.1
  69.5 0.0 copy-start.2
  69.5 0.0 reduce-scatter.2.cloned.1.call-update
  69.5 0.8 copy-done.3
  70.4 19.4 %all_to_all.15.parts = bf16[32,16,128]{2,1,0:T(8,128)(2,1)S(1)} all-to-all(bf16[32,16,128]{2,1,0:T(8,128)(2,1)S(1)} %copy-done.3), channel_id=1, replica_groups=mesh['zh'=4,'zl'=2,'y'=8,'c'=2,'x'=8] {'zl','c','x'}, dimensions={0} | all-to-all | bytes 262144 | tf_op jit(solution)/shard_map/all_to_all | solution.py:259
  89.9 24.0 %all_to_all.16.parts = bf16[32,16,128]{2,1,0:T(8,128)(2,1)S(1)} all-to-all(bf16[32,16,128]{2,1,0:T(8,128)(2,1)S(1)} %shard_map.105), channel_id=1, replica_groups=mesh['zh'=4,'zl'=2,'y'=8,'c'=2,'x'=8] {'zh','y'}, dimensions={0} | all-to-all | bytes 262144 | tf_op jit(solution)/shard_map/all_to_all | solution.py:261
  113.9 0.7 shard_map.106
  114.6 5.7 %all-to-all-start.2 = ((bf16[32,16,128]{2,1,0:T(8,128)(2,1)}), bf16[32,16,128]{2,1,0:T(8,128)(2,1)S(1)}, u32[]{:S(2)}, u32[]{:S(2)}) async-start(bf16[32,16,128]{2,1,0:T(8,128)(2,1)} %shard_map.106), calls=%async_computation.3 | async-start | bytes 262144 | tf_op jit(solution)/shard_map/all_to_all | solution.py:263
  120.2 0.0 reduce-scatter.2.cloned.1.call-done
  120.3 0.9 fusion
  121.2 4.0 %collective-permute-start.3 = (bf16[176,128]{1,0:T(8,128)(2,1)S(1)}, bf16[176,128]{1,0:T(8,128)(2,1)S(1)}, u32[]{:S(2)}, u32[]{:S(2)}) collective-permute-start(bf16[176,128]{1,0:T(8,128)(2,1)S(1)} %fusion), channel_id=1, source_target_pairs={{8,16},{24,32},{40,48},{56,64},{72,80},{88,96},{104,112},{120,128}... | collective-permute-start | bytes 135176 | tf_op jit(solution)/shard_map/ppermute | solution.py:202
  125.2 1.9 %collective-permute-start.2 = (bf16[176,128]{1,0:T(8,128)(2,1)S(1)}, bf16[176,128]{1,0:T(8,128)(2,1)S(1)}, u32[]{:S(2)}, u32[]{:S(2)}) collective-permute-start(bf16[176,128]{1,0:T(8,128)(2,1)S(1)} %fusion), channel_id=1, source_target_pairs={{0,8},{8,0},{1,9},{9,1},{2,10},{10,2},{3,11},{11,3},{4,12},{12,4},... | collective-permute-start | bytes 135176 | tf_op jit(solution)/shard_map/ppermute | solution.py:201
  127.1 0.9 slice_bitcast_fusion.1
  128.1 1.9 %all-to-all-done.2.refs_7_ = bf16[32,16,128]{2,1,0:T(8,128)(2,1)S(1)} async-done(((bf16[32,16,128]{2,1,0:T(8,128)(2,1)}), bf16[32,16,128]{2,1,0:T(8,128)(2,1)S(1)}, u32[]{:S(2)}, u32[]{:S(2)}) %all-to-all-start.2) | async-done | bytes 131104 | tf_op jit(solution)/shard_map/all_to_all | solution.py:263
  130.0 0.0 collective-permute-done.3.refs_5_
  130.0 0.0 collective-permute-done.2.refs_4_
  130.0 0.0 copy-done
  130.0 0.0 copy-done.1
  130.0 0.0 copy-done.2
  130.0 1.7 %shard_map.107 = (bf16[256,256]{1,0:T(8,128)(2,1)}, f32[172,256]{1,0:T(8,128)}, f32[1,1]{1,0:T(1,128)}) custom-call(s32[1]{0:T(128)} %bitcast.core.refs_0_, s32[2]{0:T(128)S(1)} %copy-done.2, s32[2,64]{1,0:T(2,128)S(1)} %copy-done.1, f32[176,256]{1,0:T(8,128)S(1)} %pad_maximum_fusion.refs_3_, bf16[176,128]{1,0:T(8,128)(2,1)S(1)} %collective-permute-done.2.refs_4_, ...), custom_call_target="tpu_custom_call" | custom-call | tf_op jit(solution)/shard_map/pallas_call | solution.py:267
  (3 shorter events, 0.1 us)
Async XLA Ops:
  7.2 55.7 %all-gather.3.cloned.1.call-start = ((), (), s32[]{:S(2)}) async-start(), calls=%async_computation.4 | async-start | bytes 1179648 | tf_op jit(solution)/shard_map/all_gather | solution.py:215
  7.9 112.4 %reduce-scatter.2.cloned.1.call-start = ((), (), s32[]{:S(2)}) async-start(), calls=%async_computation.5 | async-start | bytes 2433024 | tf_op jit(solution)/shard_map/reduce_scatter | solution.py:258
  9.7 18.0 %collective-permute-start = (bf16[64,256]{1,0:T(8,128)(2,1)}, bf16[64,256]{1,0:T(8,128)(2,1)S(1)}, u32[]{:S(2)}, u32[]{:S(2)}) collective-permute-start(bf16[64,256]{1,0:T(8,128)(2,1)} %get-tuple-element.10), channel_id=1, source_target_pairs={{0,8},{8,0},{1,9},{9,1},{2,10},{10,2},{3,11},{11,3},{4,12},{12,4},... | collective-permute-start | bytes 98312 | tf_op jit(solution)/shard_map/ppermute | solution.py:201
  25.8 5.7 %collective-permute-start.1 = (bf16[64,256]{1,0:T(8,128)(2,1)}, bf16[64,256]{1,0:T(8,128)(2,1)S(1)}, u32[]{:S(2)}, u32[]{:S(2)}) collective-permute-start(bf16[64,256]{1,0:T(8,128)(2,1)} %get-tuple-element.11), channel_id=1, source_target_pairs={{8,16},{24,32},{40,48},{56,64},{72,80},{88,96},{104,112},{120,128}... | collective-permute-start | bytes 98312 | tf_op jit(solution)/shard_map/ppermute | solution.py:202
  69.5 0.9 copy-start.3
  69.5 60.5 %copy-start = (bf16[256,172]{0,1:T(8,128)(2,1)S(1)}, bf16[256,172]{0,1:T(8,128)(2,1)}, u32[]{:S(2)}) copy-start(bf16[256,172]{0,1:T(8,128)(2,1)} %param.9) | copy-start | bytes 264196
  69.5 60.5 %copy-start.1 = (s32[2,64]{1,0:T(2,128)S(1)}, s32[2,64]{1,0:T(2,128)}, u32[]{:S(2)}) copy-start(s32[2,64]{1,0:T(2,128)} %refs_2_.1) | copy-start | bytes 1540
  69.5 60.5 %copy-start.2 = (s32[2]{0:T(128)S(1)}, s32[2]{0:T(128)}, u32[]{:S(2)}) copy-start(s32[2]{0:T(128)} %refs_1_.1) | copy-start | bytes 28
  114.6 15.4 %all-to-all-start.2 = ((bf16[32,16,128]{2,1,0:T(8,128)(2,1)}), bf16[32,16,128]{2,1,0:T(8,128)(2,1)S(1)}, u32[]{:S(2)}, u32[]{:S(2)}) async-start(bf16[32,16,128]{2,1,0:T(8,128)(2,1)} %shard_map.106), calls=%async_computation.3 | async-start | bytes 262144 | tf_op jit(solution)/shard_map/all_to_all | solution.py:263
  121.2 8.8 %collective-permute-start.3 = (bf16[176,128]{1,0:T(8,128)(2,1)S(1)}, bf16[176,128]{1,0:T(8,128)(2,1)S(1)}, u32[]{:S(2)}, u32[]{:S(2)}) collective-permute-start(bf16[176,128]{1,0:T(8,128)(2,1)S(1)} %fusion), channel_id=1, source_target_pairs={{8,16},{24,32},{40,48},{56,64},{72,80},{88,96},{104,112},{120,128}... | collective-permute-start | bytes 135176 | tf_op jit(solution)/shard_map/ppermute | solution.py:202
  125.2 4.8 %collective-permute-start.2 = (bf16[176,128]{1,0:T(8,128)(2,1)S(1)}, bf16[176,128]{1,0:T(8,128)(2,1)S(1)}, u32[]{:S(2)}, u32[]{:S(2)}) collective-permute-start(bf16[176,128]{1,0:T(8,128)(2,1)S(1)} %fusion), channel_id=1, source_target_pairs={{0,8},{8,0},{1,9},{9,1},{2,10},{10,2},{3,11},{11,3},{4,12},{12,4},... | collective-permute-start | bytes 135176 | tf_op jit(solution)/shard_map/ppermute | solution.py:201
Sparse Core Ops, SparseCore 0:
  10.7 52.1 all-gather.2
  69.7 47.2 reduce-scatter.1

commit v10 on v9

--- a/solution.py
+++ b/solution.py
@@ -13,7 +13,7 @@
 AXES = ("zh", "zl", "y", "c", "x")
 NEAR = ("zl", "c", "x")
 FAR = ("zh", "y")
-CHUNK = 32
+CHUNK = 64
 LAST = (((1,), (1,)), ((), ()))
 FIRST = (((0,), (0,)), ((), ()))
 PLAIN = (((1,), (0,)), ((), ()))

time: 139 us -> 139 us (level)
  no operation moved by 1% of the time
where the time goes in v10:
time: 139 us
  blocking collectives  66 us (47%)
  starting transfers between devices  29.6 us (21%)
  waiting for transfers between devices  15.2 us (11%)
  between operations  14.2 us (10%)
  Pallas kernels  11.1 us (8%)
  local copies, waits for them, and re-layouts  2.7 us (2%)
    all_to_all x1, blocking collectives, per_device(): weight_parts = lax.all_to_all(weight_parts, FAR, 0, 0, tiled=True)  24 us
    all_gather x1, blocking collectives, per_device(): halo_rows = lax.all_gather(halo, 'x', axis=0)  22.6 us
    all_to_all x1, blocking collectives, per_device(): weight_parts = lax.all_to_all(weight_parts, NEAR, 0, 0, tiled=True)  19.4 us
    ppermute x2, starting transfers between devices, exchange(): lax.ppermute(to_partner, 'c', [(0, 1), (1, 0)])  18 us
    all_gather x1, waiting for transfers between devices, per_device(): own_rows = lax.all_gather(features, 'x', axis=0, tiled=True)  8.85 us
    pallas_call x1, Pallas kernels, per_device(): pl.pallas_call(layer_kernel, out_shape=(shape((lax.axis_size(NEAR), PIECE...  6.92 us
    ppermute x2, starting transfers between devices, exchange(): lax.ppermute(to_outside, dom, outer)  5.93 us
    all_to_all x1, starting transfers between devices, per_device(): weight_parts = lax.all_to_all(weight_parts, NEAR, 0, 0, tiled=True)  5.66 us
  transfers between devices with their start and end apart: 7, of which 3 were waited for; matrix products, arithmetic and copies ran while one was open for 1% of the time, Pallas kernels for 2%

profile of v10, /device:TPU:1, one launch (start us, length us, event | category | flops | bytes accessed | tf_op | source)
XLA Modules:
  0.0 138.9 jit_solution(6840862012524171188)
XLA Ops:
  7.2 0.0 all-gather.3.cloned.1.call-start
  7.2 0.7 all-gather.3.cloned.1.call-update
  7.9 0.0 reduce-scatter.2.cloned.1.call-start
  7.9 1.8 %shard_map.103 = (bf16[64,256]{1,0:T(8,128)(2,1)}, bf16[64,256]{1,0:T(8,128)(2,1)}) custom-call(s32[1]{0:T(128)} %bitcast.core.refs_0_, s32[2]{0:T(128)} %refs_1_.1, s32[2,64]{1,0:T(2,128)} %refs_2_.1, bf16[256,256]{1,0:T(8,128)(2,1)} %features.1), custom_call_target="tpu_custom_call" | custom-call | tf_op jit(solution)/shard_map/pallas_call | solution.py:208
  9.7 16.0 %collective-permute-start = (bf16[64,256]{1,0:T(8,128)(2,1)}, bf16[64,256]{1,0:T(8,128)(2,1)S(1)}, u32[]{:S(2)}, u32[]{:S(2)}) collective-permute-start(bf16[64,256]{1,0:T(8,128)(2,1)} %get-tuple-element.10), channel_id=1, source_target_pairs={{0,8},{8,0},{1,9},{9,1},{2,10},{10,2},{3,11},{11,3},{4,12},{12,4},... | collective-permute-start | bytes 98312 | tf_op jit(solution)/shard_map/ppermute | solution.py:201
  25.8 1.9 %collective-permute-start.1 = (bf16[64,256]{1,0:T(8,128)(2,1)}, bf16[64,256]{1,0:T(8,128)(2,1)S(1)}, u32[]{:S(2)}, u32[]{:S(2)}) collective-permute-start(bf16[64,256]{1,0:T(8,128)(2,1)} %get-tuple-element.11), channel_id=1, source_target_pairs={{8,16},{24,32},{40,48},{56,64},{72,80},{88,96},{104,112},{120,128}... | collective-permute-start | bytes 98312 | tf_op jit(solution)/shard_map/ppermute | solution.py:202
  27.7 0.0 collective-permute-done
  27.7 3.7 %collective-permute-done.1 = bf16[64,256]{1,0:T(8,128)(2,1)S(1)} collective-permute-done((bf16[64,256]{1,0:T(8,128)(2,1)}, bf16[64,256]{1,0:T(8,128)(2,1)S(1)}, u32[]{:S(2)}, u32[]{:S(2)}) %collective-permute-start.1) | collective-permute-done | bytes 32800 | tf_op jit(solution)/shard_map/ppermute | solution.py:202
  31.5 22.6 %all-gather = bf16[1024,256]{1,0:T(8,128)(2,1)} all-gather(bf16[128,256]{1,0:T(8,128)(2,1)S(1)} %pad_maximum_fusion.1), channel_id=2, replica_groups=mesh['zh'=4,'zl'=2,'y'=8,'c'=2,'x'=8] {'x'}, dimensions={0}, use_global_device_ids=true | all-gather | bytes 589824 | tf_op jit(solution)/shard_map/all_gather | solution.py:216
  54.0 8.9 %all-gather.3.cloned.1.call-done = bf16[2048,256]{1,0:T(8,128)(2,1)} async-done(((bf16[256,256]{1,0:T(8,128)(2,1)}), bf16[2048,256]{1,0:T(8,128)(2,1)}) %all-gather.3.cloned.1.call-update) | async-done | bytes 1048592 | tf_op jit(solution)/shard_map/all_gather | solution.py:215
  62.9 6.9 %shard_map.104 = (bf16[32,16,128]{2,1,0:T(8,128)(2,1)}, f32[24,176,128]{2,1,0:T(8,128)}) custom-call(s32[1]{0:T(128)} %bitcast.core.refs_0_, s32[64]{0:T(128)} %rows_hbm.1, s32[64]{0:T(128)} %cols_hbm.1, bf16[64,128,128]{2,1,0:T(8,128)(2,1)} %tiles_hbm.1, bf16[8,2,128,256]{3,2,1,0:T(8,128)(2,1)} %bitcast.16, bf16[8,128,256]{2,1,0:T(8,128)(2,1)} %bitcast.15, ...), custom_call_target="tpu_custom_call" | custom-call | tf_op jit(solution)/shard_map/pallas_call | solution.py:218
  69.8 0.0 copy-start.3
  69.8 0.0 copy-start
  69.8 0.0 copy-start.1
  69.8 0.0 copy-start.2
  69.8 0.0 reduce-scatter.2.cloned.1.call-update
  69.9 0.8 copy-done.3
  70.7 19.4 %all_to_all.15.parts = bf16[32,16,128]{2,1,0:T(8,128)(2,1)S(1)} all-to-all(bf16[32,16,128]{2,1,0:T(8,128)(2,1)S(1)} %copy-done.3), channel_id=1, replica_groups=mesh['zh'=4,'zl'=2,'y'=8,'c'=2,'x'=8] {'zl','c','x'}, dimensions={0} | all-to-all | bytes 262144 | tf_op jit(solution)/shard_map/all_to_all | solution.py:259
  90.2 24.0 %all_to_all.16.parts = bf16[32,16,128]{2,1,0:T(8,128)(2,1)S(1)} all-to-all(bf16[32,16,128]{2,1,0:T(8,128)(2,1)S(1)} %shard_map.105), channel_id=1, replica_groups=mesh['zh'=4,'zl'=2,'y'=8,'c'=2,'x'=8] {'zh','y'}, dimensions={0} | all-to-all | bytes 262144 | tf_op jit(solution)/shard_map/all_to_all | solution.py:261
  114.2 0.7 shard_map.106
  114.9 5.7 %all-to-all-start.2 = ((bf16[32,16,128]{2,1,0:T(8,128)(2,1)}), bf16[32,16,128]{2,1,0:T(8,128)(2,1)S(1)}, u32[]{:S(2)}, u32[]{:S(2)}) async-start(bf16[32,16,128]{2,1,0:T(8,128)(2,1)} %shard_map.106), calls=%async_computation.3 | async-start | bytes 262144 | tf_op jit(solution)/shard_map/all_to_all | solution.py:263
  120.5 0.0 reduce-scatter.2.cloned.1.call-done
  120.6 0.9 fusion
  121.5 4.0 %collective-permute-start.3 = (bf16[176,128]{1,0:T(8,128)(2,1)S(1)}, bf16[176,128]{1,0:T(8,128)(2,1)S(1)}, u32[]{:S(2)}, u32[]{:S(2)}) collective-permute-start(bf16[176,128]{1,0:T(8,128)(2,1)S(1)} %fusion), channel_id=1, source_target_pairs={{8,16},{24,32},{40,48},{56,64},{72,80},{88,96},{104,112},{120,128}... | collective-permute-start | bytes 135176 | tf_op jit(solution)/shard_map/ppermute | solution.py:202
  125.5 1.9 %collective-permute-start.2 = (bf16[176,128]{1,0:T(8,128)(2,1)S(1)}, bf16[176,128]{1,0:T(8,128)(2,1)S(1)}, u32[]{:S(2)}, u32[]{:S(2)}) collective-permute-start(bf16[176,128]{1,0:T(8,128)(2,1)S(1)} %fusion), channel_id=1, source_target_pairs={{0,8},{8,0},{1,9},{9,1},{2,10},{10,2},{3,11},{11,3},{4,12},{12,4},... | collective-permute-start | bytes 135176 | tf_op jit(solution)/shard_map/ppermute | solution.py:201
  127.4 0.9 slice_bitcast_fusion.1
  128.4 1.9 %all-to-all-done.2.refs_7_ = bf16[32,16,128]{2,1,0:T(8,128)(2,1)S(1)} async-done(((bf16[32,16,128]{2,1,0:T(8,128)(2,1)}), bf16[32,16,128]{2,1,0:T(8,128)(2,1)S(1)}, u32[]{:S(2)}, u32[]{:S(2)}) %all-to-all-start.2) | async-done | bytes 131104 | tf_op jit(solution)/shard_map/all_to_all | solution.py:263
  130.3 0.0 collective-permute-done.3.refs_5_
  130.3 0.0 collective-permute-done.2.refs_4_
  130.3 0.0 copy-done
  130.3 0.0 copy-done.1
  130.3 0.0 copy-done.2
  130.3 1.7 %shard_map.107 = (bf16[256,256]{1,0:T(8,128)(2,1)}, f32[172,256]{1,0:T(8,128)}, f32[1,1]{1,0:T(1,128)}) custom-call(s32[1]{0:T(128)} %bitcast.core.refs_0_, s32[2]{0:T(128)S(1)} %copy-done.2, s32[2,64]{1,0:T(2,128)S(1)} %copy-done.1, f32[176,256]{1,0:T(8,128)S(1)} %pad_maximum_fusion.refs_3_, bf16[176,128]{1,0:T(8,128)(2,1)S(1)} %collective-permute-done.2.refs_4_, ...), custom_call_target="tpu_custom_call" | custom-call | tf_op jit(solution)/shard_map/pallas_call | solution.py:267
  (3 shorter events, 0.1 us)
Async XLA Ops:
  7.2 55.7 %all-gather.3.cloned.1.call-start = ((), (), s32[]{:S(2)}) async-start(), calls=%async_computation.4 | async-start | bytes 1179648 | tf_op jit(solution)/shard_map/all_gather | solution.py:215
  7.9 112.7 %reduce-scatter.2.cloned.1.call-start = ((), (), s32[]{:S(2)}) async-start(), calls=%async_computation.5 | async-start | bytes 2433024 | tf_op jit(solution)/shard_map/reduce_scatter | solution.py:258
  9.7 18.0 %collective-permute-start = (bf16[64,256]{1,0:T(8,128)(2,1)}, bf16[64,256]{1,0:T(8,128)(2,1)S(1)}, u32[]{:S(2)}, u32[]{:S(2)}) collective-permute-start(bf16[64,256]{1,0:T(8,128)(2,1)} %get-tuple-element.10), channel_id=1, source_target_pairs={{0,8},{8,0},{1,9},{9,1},{2,10},{10,2},{3,11},{11,3},{4,12},{12,4},... | collective-permute-start | bytes 98312 | tf_op jit(solution)/shard_map/ppermute | solution.py:201
  25.8 5.7 %collective-permute-start.1 = (bf16[64,256]{1,0:T(8,128)(2,1)}, bf16[64,256]{1,0:T(8,128)(2,1)S(1)}, u32[]{:S(2)}, u32[]{:S(2)}) collective-permute-start(bf16[64,256]{1,0:T(8,128)(2,1)} %get-tuple-element.11), channel_id=1, source_target_pairs={{8,16},{24,32},{40,48},{56,64},{72,80},{88,96},{104,112},{120,128}... | collective-permute-start | bytes 98312 | tf_op jit(solution)/shard_map/ppermute | solution.py:202
  69.8 0.9 copy-start.3
  69.8 60.5 %copy-start = (bf16[256,172]{0,1:T(8,128)(2,1)S(1)}, bf16[256,172]{0,1:T(8,128)(2,1)}, u32[]{:S(2)}) copy-start(bf16[256,172]{0,1:T(8,128)(2,1)} %param.9) | copy-start | bytes 264196
  69.8 60.5 %copy-start.1 = (s32[2,64]{1,0:T(2,128)S(1)}, s32[2,64]{1,0:T(2,128)}, u32[]{:S(2)}) copy-start(s32[2,64]{1,0:T(2,128)} %refs_2_.1) | copy-start | bytes 1540
  69.8 60.5 %copy-start.2 = (s32[2]{0:T(128)S(1)}, s32[2]{0:T(128)}, u32[]{:S(2)}) copy-start(s32[2]{0:T(128)} %refs_1_.1) | copy-start | bytes 28
  114.9 15.4 %all-to-all-start.2 = ((bf16[32,16,128]{2,1,0:T(8,128)(2,1)}), bf16[32,16,128]{2,1,0:T(8,128)(2,1)S(1)}, u32[]{:S(2)}, u32[]{:S(2)}) async-start(bf16[32,16,128]{2,1,0:T(8,128)(2,1)} %shard_map.106), calls=%async_computation.3 | async-start | bytes 262144 | tf_op jit(solution)/shard_map/all_to_all | solution.py:263
  121.5 8.8 %collective-permute-start.3 = (bf16[176,128]{1,0:T(8,128)(2,1)S(1)}, bf16[176,128]{1,0:T(8,128)(2,1)S(1)}, u32[]{:S(2)}, u32[]{:S(2)}) collective-permute-start(bf16[176,128]{1,0:T(8,128)(2,1)S(1)} %fusion), channel_id=1, source_target_pairs={{8,16},{24,32},{40,48},{56,64},{72,80},{88,96},{104,112},{120,128}... | collective-permute-start | bytes 135176 | tf_op jit(solution)/shard_map/ppermute | solution.py:202
  125.5 4.8 %collective-permute-start.2 = (bf16[176,128]{1,0:T(8,128)(2,1)S(1)}, bf16[176,128]{1,0:T(8,128)(2,1)S(1)}, u32[]{:S(2)}, u32[]{:S(2)}) collective-permute-start(bf16[176,128]{1,0:T(8,128)(2,1)S(1)} %fusion), channel_id=1, source_target_pairs={{0,8},{8,0},{1,9},{9,1},{2,10},{10,2},{3,11},{11,3},{4,12},{12,4},... | collective-permute-start | bytes 135176 | tf_op jit(solution)/shard_map/ppermute | solution.py:201
Sparse Core Ops, SparseCore 0:
  10.7 52.1 all-gather.2
  70.0 47.3 reduce-scatter.1
